TPU v7x, 512 devices: a whole 4x4x16 slice. The times are simulated.
512 devices in a mesh: ctx: 16 (over y_lo, x, core), mp: 32 (over z, y_hi).
Axes of the slice: x: 4, y: 4 (y_hi: 2, y_lo: 2; y = y_hi * 2 + y_lo), z: 16, core: 2. Of those that a mesh axis runs over, the one named last changes fastest.
Arguments:
- queries: bfloat16 [16384, 4096], P('ctx', 'mp'), may hold values from -320 to 320
- keys_values: bfloat16 [16384, 2048], P('ctx', 'mp'), may hold values from -40 to 40
- query_taps: float32 [4, 4096], P(None, 'mp'), may hold values from -2.5 to 2.5
- pair_taps: float32 [4, 2048], P(None, 'mp'), may hold values from -2.5 to 2.5
- out_gain: float32 [4096], P('mp'), may hold values from 0.1 to 1.9
Outputs:
- head_outputs: bfloat16 [16384, 4096], P('ctx', 'mp')
All inputs are finite; a program needn't handle non-finite values.
Results may differ from a plain program's by a relative error of at most 0.012.
The roundings to bfloat16 on the way count: a program that leaves them out, or rounds other values in their place, can miss the bound.
Values may be sent and summed in bfloat16 or wider, within the bound.
No kernel may reach another device: no remote copies, remote signals or barrier semaphores. Data moves between devices by JAX's collectives and lax.ppermute only.
A program may use at most 64 MiB of HBM per device.

v0:
```python
import math

import jax
import jax.numpy as jnp
from jax import lax
from jax.sharding import PartitionSpec as P

HEAD_CHANNELS = 128
TAPS = 4
TRANSFORM_BLOCK = 128
KEEP = 16


NEGATIVE = -1e30
EPSILON = 1e-06


def shifted(value, axis, steps):
    count = lax.axis_size(axis)
    leading, last = (max(0, -steps), min(count, count - steps))
    return lax.ppermute(value, axis, [(source, source + steps) for source in range(leading, last)])


def from_partner(block, axis, apart):
    count = lax.axis_size(axis)
    route = []
    for low in range(count):
        high = low | 1 << apart
        if high != low and high < count:
            route += [(low, high), (high, low)]
    return lax.ppermute(block, axis, route)


def dct_table():
    frequency = jnp.arange(KEEP, dtype=jnp.float32)[:, None]
    offset = jnp.arange(TRANSFORM_BLOCK, dtype=jnp.float32)[None, :]
    table = jnp.cos(math.pi * (offset + 0.5) * frequency / TRANSFORM_BLOCK) * math.sqrt(
        2.0 / TRANSFORM_BLOCK
    )
    table = jnp.where(frequency == 0.0, table * math.sqrt(0.5), table)
    return table.astype(jnp.bfloat16)


def compress(values):
    blocks = values.reshape(values.shape[0] // TRANSFORM_BLOCK, TRANSFORM_BLOCK, values.shape[1])
    packed = jnp.einsum("jt,btc->bjc", dct_table(), blocks, preferred_element_type=jnp.float32)
    return packed.astype(jnp.bfloat16).reshape(-1, values.shape[1])


def causal_conv(history, values, weights):
    lead = weights.shape[0] - 1
    padded = jnp.concatenate([history, values], 0)
    length = values.shape[0]
    total = weights[0] * values.astype(jnp.float32)
    for shift in range(1, weights.shape[0]):
        total = total + weights[shift] * padded[lead - shift : lead - shift + length].astype(
            jnp.float32
        )
    return total.astype(jnp.bfloat16)


def local_state(query_heads, pairs, score_scale):
    entry_count = query_heads.shape[0] // TRANSFORM_BLOCK
    heads = query_heads.shape[1]
    scores = (
        jnp.einsum(
            "uxwi,umi->uxwm",
            query_heads.reshape(entry_count, TRANSFORM_BLOCK, heads, HEAD_CHANNELS),
            pairs[:, :HEAD_CHANNELS].reshape(entry_count, TRANSFORM_BLOCK, HEAD_CHANNELS),
            preferred_element_type=jnp.float32,
        )
        * score_scale
    )
    causal = (
        jnp.arange(TRANSFORM_BLOCK)[:, None, None] >= jnp.arange(TRANSFORM_BLOCK)[None, None, :]
    )
    scores = jnp.where(causal, scores, NEGATIVE)
    top = jnp.max(scores, -1)
    weights = jnp.where(causal, jnp.exp(scores - top[..., None]), 0.0)
    total = jnp.sum(weights, -1)
    summed = jnp.einsum(
        "cevo,coa->ceva",
        weights.astype(jnp.bfloat16),
        pairs[:, HEAD_CHANNELS:].reshape(entry_count, TRANSFORM_BLOCK, HEAD_CHANNELS),
        preferred_element_type=jnp.float32,
    )
    rows = entry_count * TRANSFORM_BLOCK
    return (
        top.reshape(rows, heads),
        total.reshape(rows, heads),
        summed.reshape(rows, heads, HEAD_CHANNELS),
    )


def attend(state, query_heads, query_blocks, keys, key_blocks, score_scale):
    top, total, summed = state
    entry_count = query_heads.shape[0]
    size = 512
    tops, totals, sums = ([], [], [])
    for begin in range(0, entry_count, size):
        part = query_heads[begin : begin + size]
        scores = (
            jnp.einsum(
                "qhd,kd->qhk", part, keys[:, :HEAD_CHANNELS], preferred_element_type=jnp.float32
            )
            * score_scale
        )
        seen = key_blocks[None, None, :] < query_blocks[begin : begin + size, None, None]
        scores = jnp.where(seen, scores, NEGATIVE)
        old_top = top[begin : begin + size]
        new_top = jnp.maximum(old_top, jnp.max(scores, -1))
        weights = jnp.where(seen, jnp.exp(scores - new_top[..., None]), 0.0)
        rescale = jnp.exp(old_top - new_top)
        totals.append(rescale * total[begin : begin + size] + jnp.sum(weights, -1))
        sums.append(
            rescale[..., None] * summed[begin : begin + size]
            + jnp.einsum(
                "qhk,kd->qhd",
                weights.astype(jnp.bfloat16),
                keys[:, HEAD_CHANNELS:],
                preferred_element_type=jnp.float32,
            )
        )
        tops.append(new_top)
    return (jnp.concatenate(tops, 0), jnp.concatenate(totals, 0), jnp.concatenate(sums, 0))


def per_device(queries, keys_values, query_taps, pair_taps, out_gain):
    rows = queries.shape[0]
    span_rows = rows // 2
    per_span = span_rows // TRANSFORM_BLOCK
    shards = lax.axis_size("ctx")
    place = lax.axis_index("ctx")
    member = lax.axis_index("mp")
    score_scale = 1.0 / math.sqrt(HEAD_CHANNELS)
    tail = TAPS - 1
    columns = queries.shape[1]
    first_tail = jnp.concatenate(
        [queries[span_rows - tail : span_rows], keys_values[span_rows - tail : span_rows]], 1
    )
    second_tail = jnp.concatenate([queries[rows - tail :], keys_values[rows - tail :]], 1)
    from_lower = shifted(first_tail, "ctx", 1)
    from_upper = shifted(second_tail, "ctx", -1)
    before_second = jnp.where(place == shards - 1, first_tail, from_upper)
    query_conv = jnp.concatenate(
        [
            causal_conv(from_lower[:, :columns], queries[:span_rows], query_taps),
            causal_conv(before_second[:, :columns], queries[span_rows:], query_taps),
        ],
        0,
    )
    pair_conv = jnp.concatenate(
        [
            causal_conv(from_lower[:, columns:], keys_values[:span_rows], pair_taps),
            causal_conv(before_second[:, columns:], keys_values[span_rows:], pair_taps),
        ],
        0,
    )
    width = keys_values.shape[1]
    rounds = (2 * HEAD_CHANNELS // width).bit_length() - 1

    def join(mine, other, bit):
        lower = member // 2**bit % 2 == 0
        return jnp.where(
            lower, jnp.concatenate([mine, other], 1), jnp.concatenate([other, mine], 1)
        )

    pairs = pair_conv
    packed = compress(pair_conv)
    for bit in range(rounds):
        other = from_partner(jnp.concatenate([pairs, packed], 0), "mp", bit)
        pairs = join(pairs, other[:rows], bit)
        packed = join(packed, other[rows:], bit)
    heads_here = columns // HEAD_CHANNELS
    query_heads = query_conv.reshape(rows, heads_here, HEAD_CHANNELS)
    own_rows = jnp.arange(rows)
    own_span = jnp.where(own_rows < span_rows, place, 2 * shards - 1 - place)
    query_blocks = own_span * per_span + own_rows % span_rows // TRANSFORM_BLOCK
    state = local_state(query_heads, pairs, score_scale)
    shard_rows = rows * KEEP // TRANSFORM_BLOCK
    half_rows = shard_rows // 2
    piece = lax.all_gather(packed, "ctx", axis=0, tiled=True)
    positions = jnp.arange(piece.shape[0])
    owner = positions // shard_rows
    within = positions % shard_rows
    span_index = jnp.where(within < half_rows, owner, 2 * shards - 1 - owner)
    key_blocks = span_index * per_span + within % half_rows // KEEP
    state = attend(state, query_heads, query_blocks, piece, key_blocks, score_scale)
    top, total, summed = state
    attended = summed / total[..., None]
    normed = attended * lax.rsqrt(jnp.mean(attended * attended, -1, keepdims=True) + EPSILON)
    return (normed.reshape(rows, columns) * out_gain).astype(jnp.bfloat16)


def solution(mesh):
    in_specs = (P("ctx", "mp"), P("ctx", "mp"), P(None, "mp"), P(None, "mp"), P("mp"))
    out_specs = P("ctx", "mp")
    return jax.shard_map(
        per_device, mesh=mesh, in_specs=in_specs, out_specs=out_specs, check_vma=False
    )
```

profile of v0, /device:TPU:1, one launch (start us, length us, event | category | flops | bytes accessed | tf_op | source)
XLA Modules:
  0.0 103.2 jit_solution(5550732140074275808)
XLA Ops:
  6.5 0.0 all-gather.2.cloned.1.call-start
  6.5 0.7 fusion.93
  7.2 0.8 fusion.95
  8.1 0.1 copy.40
  8.2 8.8 %collective-permute-start.1 = (bf16[3,192]{1,0:T(4,128)(2,1)S(1)}, bf16[3,192]{1,0:T(4,128)(2,1)S(1)}, u32[]{:S(2)}, u32[]{:S(2)}) collective-permute-start(bf16[3,192]{1,0:T(4,128)(2,1)S(1)} %pad_maximum_fusion.9), channel_id=1, source_target_pairs={{32,0},{64,32},{96,64},{128,96},{160,128},{192,160},{224,192},{256... | collective-permute-start | bytes 3464 | tf_op jit(solution)/shard_map/ppermute | solution.py:21
  17.0 0.9 fusion.94
  17.8 0.8 slice_bitcast_fusion.3
  18.7 0.1 copy.39
  18.8 0.0 collective-permute-done.1
  18.8 1.9 %collective-permute-start = (bf16[3,192]{1,0:T(4,128)(2,1)S(1)}, bf16[3,192]{1,0:T(4,128)(2,1)S(1)}, u32[]{:S(2)}, u32[]{:S(2)}) collective-permute-start(bf16[3,192]{1,0:T(4,128)(2,1)S(1)} %get-tuple-element.37), channel_id=1, source_target_pairs={{0,32},{32,64},{64,96},{96,128},{128,160},{160,192},{192,224},{224... | collective-permute-start | bytes 3464 | tf_op jit(solution)/shard_map/ppermute | solution.py:21
  20.8 0.1 copy.30
  20.9 1.0 collective-permute-done
  21.9 0.1 copy.29
  22.0 0.2 add_convert_fusion.3
  22.3 0.2 convolution_convert_fusion
  22.5 0.1 copy.32
  22.6 1.9 %collective-permute-start.2 = (bf16[1152,64]{0,1:T(8,128)(2,1)S(1)}, bf16[1152,64]{0,1:T(8,128)(2,1)S(1)}, u32[]{:S(2)}, u32[]{:S(2)}) collective-permute-start(bf16[1152,64]{0,1:T(8,128)(2,1)S(1)} %pad_maximum_fusion.2), channel_id=1, source_target_pairs={{0,1},{1,0},{2,3},{3,2},{4,5},{5,4},{6,7},{7,6},{8,9},{9,8},{10,11... | collective-permute-start | bytes 442376 | tf_op jit(solution)/shard_map/ppermute | solution.py:31
  24.5 0.8 slice_bitcast_fusion.7
  25.4 5.9 %collective-permute-done.2 = bf16[1152,64]{0,1:T(8,128)(2,1)S(1)} collective-permute-done((bf16[1152,64]{0,1:T(8,128)(2,1)S(1)}, bf16[1152,64]{0,1:T(8,128)(2,1)S(1)}, u32[]{:S(2)}, u32[]{:S(2)}) %collective-permute-start.2) | collective-permute-done | bytes 147488 | tf_op jit(solution)/shard_map/ppermute | solution.py:31
  31.3 0.1 maximum_select_fusion.1
  31.4 1.9 %collective-permute-start.3 = (bf16[1152,128]{0,1:T(8,128)(2,1)S(1)}, bf16[1152,128]{0,1:T(8,128)(2,1)S(1)}, u32[]{:S(2)}, u32[]{:S(2)}) collective-permute-start(bf16[1152,128]{0,1:T(8,128)(2,1)S(1)} %pad_maximum_fusion), channel_id=1, source_target_pairs={{0,2},{2,0},{1,3},{3,1},{4,6},{6,4},{5,7},{7,5},{8,10},{10,8},{9,1... | collective-permute-start | bytes 884744 | tf_op jit(solution)/shard_map/ppermute | solution.py:31
  33.4 1.0 fusion.92
  34.4 6.5 %collective-permute-done.3 = bf16[1152,128]{0,1:T(8,128)(2,1)S(1)} collective-permute-done((bf16[1152,128]{0,1:T(8,128)(2,1)S(1)}, bf16[1152,128]{0,1:T(8,128)(2,1)S(1)}, u32[]{:S(2)}, u32[]{:S(2)}) %collective-permute-start.3) | collective-permute-done | bytes 294944 | tf_op jit(solution)/shard_map/ppermute | solution.py:31
  40.9 0.6 maximum_select_fusion.2
  41.5 0.0 all-gather.2.cloned.1.call-update
  41.5 0.3 add_convert_fusion.1
  41.9 0.1 maximum_select_fusion
  42.0 0.2 copy.35
  42.2 0.2 copy.36
  42.4 0.3 fusion.99
  42.7 0.1 fusion.28
  42.9 0.3 fusion.30
  43.2 43.6 %all-gather.2.cloned.1.call-done = bf16[2048,256]{0,1:T(8,128)(2,1)} async-done(((bf16[128,256]{0,1:T(8,128)(2,1)}), bf16[2048,256]{0,1:T(8,128)(2,1)}) %all-gather.2.cloned.1.call-update) | async-done | bytes 1048592 | tf_op jit(solution)/shard_map/all_gather | solution.py:182
  86.8 0.0 copy-start.1
  86.8 2.0 %fusion = (f32[512]{0:T(512)S(1)}, f32[512,2048]{1,0:T(8,128)S(1)}) fusion(s32[2048]{0:T(1024)S(1)} %fusion.52, s32[512]{0:T(512)S(1)} %get-tuple-element.28, bf16[512,128]{1,0:T(8,128)(2,1)S(1)} %get-tuple-element.29, bf16[2048,256]{0,1:T(8,128)(2,1)} %all-gather.2.cloned.1.call-done), kind=kOutput, calls=%fused_computation.4 | convolution fusion | flops 272629248 | bytes 4861952 | tf_op jit(solution)/shard_map/qhd,kd->qhk/dot_general | solution.py:103
  88.8 0.0 copy-done.1
  88.9 2.1 %fusion.2 = (f32[512]{0:T(512)S(1)}, f32[512]{0:T(512)S(1)}, f32[512,2048]{1,0:T(8,128)S(1)}) fusion(f32[512,2048]{1,0:T(8,128)S(1)} %get-tuple-element.46, f32[512]{0:T(512)S(1)} %get-tuple-element.20, s32[2048]{0:T(1024)S(1)} %fusion.52, s32[512]{0:T(512)S(1)} %get-tuple-element.28, s32[512]{0:T(512)S(1)} %get-tuple-element.27, ...), kind=kOutput, calls=%fused_computation.6 | convolution fusion | flops 278920192 | bytes 9062400 | tf_op jit(solution)/shard_map/qhd,kd->qhk/dot_general | solution.py:103
  91.0 1.3 %fusion.4 = f32[512]{0:T(512)S(1)} fusion(f32[512,2048]{1,0:T(8,128)S(1)} %get-tuple-element.47, f32[512]{0:T(512)S(1)} %get-tuple-element.21, s32[2048]{0:T(1024)S(1)} %fusion.52, s32[512]{0:T(512)S(1)} %get-tuple-element.27), kind=kLoop, calls=%fused_computation.8 | loop fusion | flops 6290944 | bytes 4208640 | tf_op jit(solution)/shard_map/reduce_sum | solution.py:114
  92.3 0.2 bitcast_multiply_fusion
  92.5 1.2 %fusion.11 = f32[512,128]{1,0:T(8,128)S(1)} fusion(f32[512,128]{1,0:T(8,128)S(1)} %get-tuple-element.49, f32[512,2048]{1,0:T(8,128)S(1)} %get-tuple-element.46, f32[512]{0:T(512)S(1)} %get-tuple-element.20, s32[2048]{0:T(1024)S(1)} %fusion.52, s32[512]{0:T(512)S(1)} %get-tuple-element.28, bf16[2048,256]{0,1:T(8,128)(2,1)S(1)} %copy-done.1), kind=kOutput, calls=%fused_computation.14 | convolution fusion | flops 274792448 | bytes 5255168 | tf_op jit(solution)/shard_map/qhk,kd->qhd/dot_general | solution.py:117
  93.7 0.0 copy-start
  93.7 1.2 %fusion.14 = f32[512,128]{1,0:T(8,128)S(1)} fusion(f32[512,128]{1,0:T(8,128)S(1)} %get-tuple-element.48, f32[512,2048]{1,0:T(8,128)S(1)} %get-tuple-element.47, f32[512]{0:T(512)S(1)} %get-tuple-element.21, s32[2048]{0:T(1024)S(1)} %fusion.52, s32[512]{0:T(512)S(1)} %get-tuple-element.27, bf16[2048,256]{0,1:T(8,128)(2,1)S(1)} %copy-done.1), kind=kOutput, calls=%fused_computation.15 | convolution fusion | flops 274792448 | bytes 5255168 | tf_op jit(solution)/shard_map/qhk,kd->qhd/dot_general | solution.py:117
  94.9 0.4 fusion.21
  95.3 0.0 copy-done
  95.3 1.0 %fusion.20 = bf16[1024,128]{1,0:T(8,128)(2,1)} fusion(f32[512,128]{1,0:T(8,128)S(1)} %fusion.14, f32[512,128]{1,0:T(8,128)S(1)} %fusion.11, f32[128]{0:T(128)S(1)} %copy-done, f32[1024]{0:T(1024)S(1)} %add_rsqrt_fusion, f32[1024]{0:T(1024)S(1)} %bitcast.72), kind=kLoop, calls=%fused_computation.24 | loop fusion | flops 655360 | bytes 795136 | tf_op jit(solution)/shard_map/convert_element_type | solution.py:192
  (29 shorter events, 0.3 us)
Async XLA Ops:
  6.5 80.2 %all-gather.2.cloned.1.call-start = ((), (), s32[]{:S(2)}) async-start(), calls=%async_computation | async-start | bytes 1114112 | tf_op jit(solution)/shard_map/all_gather | solution.py:182
  8.2 10.7 %collective-permute-start.1 = (bf16[3,192]{1,0:T(4,128)(2,1)S(1)}, bf16[3,192]{1,0:T(4,128)(2,1)S(1)}, u32[]{:S(2)}, u32[]{:S(2)}) collective-permute-start(bf16[3,192]{1,0:T(4,128)(2,1)S(1)} %pad_maximum_fusion.9), channel_id=1, source_target_pairs={{32,0},{64,32},{96,64},{128,96},{160,128},{192,160},{224,192},{256... | collective-permute-start | bytes 3464 | tf_op jit(solution)/shard_map/ppermute | solution.py:21
  18.8 3.1 %collective-permute-start = (bf16[3,192]{1,0:T(4,128)(2,1)S(1)}, bf16[3,192]{1,0:T(4,128)(2,1)S(1)}, u32[]{:S(2)}, u32[]{:S(2)}) collective-permute-start(bf16[3,192]{1,0:T(4,128)(2,1)S(1)} %get-tuple-element.37), channel_id=1, source_target_pairs={{0,32},{32,64},{64,96},{96,128},{128,160},{160,192},{192,224},{224... | collective-permute-start | bytes 3464 | tf_op jit(solution)/shard_map/ppermute | solution.py:21
  22.6 8.7 %collective-permute-start.2 = (bf16[1152,64]{0,1:T(8,128)(2,1)S(1)}, bf16[1152,64]{0,1:T(8,128)(2,1)S(1)}, u32[]{:S(2)}, u32[]{:S(2)}) collective-permute-start(bf16[1152,64]{0,1:T(8,128)(2,1)S(1)} %pad_maximum_fusion.2), channel_id=1, source_target_pairs={{0,1},{1,0},{2,3},{3,2},{4,5},{5,4},{6,7},{7,6},{8,9},{9,8},{10,11... | collective-permute-start | bytes 442376 | tf_op jit(solution)/shard_map/ppermute | solution.py:31
  31.4 9.4 %collective-permute-start.3 = (bf16[1152,128]{0,1:T(8,128)(2,1)S(1)}, bf16[1152,128]{0,1:T(8,128)(2,1)S(1)}, u32[]{:S(2)}, u32[]{:S(2)}) collective-permute-start(bf16[1152,128]{0,1:T(8,128)(2,1)S(1)} %pad_maximum_fusion), channel_id=1, source_target_pairs={{0,2},{2,0},{1,3},{3,1},{4,6},{6,4},{5,7},{7,5},{8,10},{10,8},{9,1... | collective-permute-start | bytes 884744 | tf_op jit(solution)/shard_map/ppermute | solution.py:31
  86.8 2.1 %copy-start.1 = (bf16[2048,256]{0,1:T(8,128)(2,1)S(1)}, bf16[2048,256]{0,1:T(8,128)(2,1)}, u32[]{:S(2)}) copy-start(bf16[2048,256]{0,1:T(8,128)(2,1)} %all-gather.2.cloned.1.call-done) | copy-start | bytes 3145732
  93.7 1.6 %copy-start = (f32[128]{0:T(128)S(1)}, f32[128]{0:T(128)}, u32[]{:S(2)}) copy-start(f32[128]{0:T(128)} %param.9) | copy-start | bytes 1540
Sparse Core Ops, SparseCore 0:
  41.7 45.0 all-gather.1
where the time goes:
time: 104 us; the launch traced here: 103 us
  waiting for transfers between devices  57 us (55%)
  starting transfers between devices  14.6 us (14%)
  between operations  13.7 us (13%)
  matrix products  7.34 us (7%)
  local copies, waits for them, and re-layouts  6.06 us (6%)
  other arithmetic  4.51 us (4%)
    all_gather x1, waiting for transfers between devices, per_device(): piece = lax.all_gather(packed, 'ctx', axis=0, tiled=True)  43.6 us
    ppermute x2, waiting for transfers between devices, from_partner(): return lax.ppermute(block, axis, route)  12.4 us
    ppermute x2, starting transfers between devices, shifted(): lax.ppermute(value, axis, [(source, source + steps) for source in range(l...  10.7 us
    dot_general x2, matrix products, attend(): jnp.einsum('qhd,kd->qhk', part, keys[:, :HEAD_CHANNELS], preferred_elemen...  4.17 us
    ppermute x2, starting transfers between devices, from_partner(): return lax.ppermute(block, axis, route)  3.84 us
    dot_general x2, matrix products, attend(): jnp.einsum('qhk,kd->qhd', weights.astype(jnp.bfloat16), keys[:, HEAD_CHAN...  2.36 us
  transfers between devices with their start and end apart: 5, of which 4 were waited for; matrix products, arithmetic and copies ran while one was open for 5% of the time, Pallas kernels for 0%

commit v1 on v0

v1 whole, which is shorter than its diff:
```python
import functools
import math

import jax
import jax.numpy as jnp
import numpy as np
from jax import lax
from jax.experimental import pallas as pl
from jax.experimental.pallas import tpu as pltpu
from jax.sharding import Mesh, PartitionSpec as P

HEAD_CHANNELS = 128
TAPS = 4
BLOCK = 128
KEEP = 16
SPAN = 512
ROWS = 2 * SPAN
NEGATIVE = -1e30
EPSILON = 1e-06
EDGE = 16

CTX = ("y_lo", "x", "core")
MP = ("z_hi", "z_lo", "y_hi")
GROUP = ("z_lo", "y_hi")
CHIPS = ("y_lo", "x")

VMEM = pltpu.VMEM
SMEM = pltpu.SMEM
F32 = jnp.float32
BF16 = jnp.bfloat16


def spec(space=VMEM):
    return pl.BlockSpec(memory_space=space)


def dct_tile():
    j = np.arange(KEEP, dtype=np.float32)[:, None]
    u = np.arange(BLOCK, dtype=np.float32)[None, :]
    table = np.cos(np.float32(math.pi) * (u + np.float32(0.5)) * j / np.float32(BLOCK))
    table = table * np.float32(math.sqrt(2.0 / BLOCK))
    table = np.where(j == 0, table * np.float32(math.sqrt(0.5)), table)
    return np.tile(table.T, (1, BLOCK // KEEP)).astype(jnp.bfloat16)


def choose_halos(scalars, own, swap, hop):
    place = scalars[0]
    odd = place % 2 == 1
    lower = jnp.where(odd, swap[0], hop[0])
    lower = jnp.where(place == 0, jnp.zeros_like(lower), lower)
    upper = jnp.where(odd, hop[1], swap[1])
    upper = jnp.where(place == 15, own[0], upper)
    return lower, upper


def pack_kernel(scalars, kv, own, swap, hop, taps, table, conv_out, block_out):
    lower, upper = choose_halos(
        scalars, own[:, EDGE:].astype(F32), swap[:, EDGE:].astype(F32), hop[:, EDGE:].astype(F32)
    )
    lanes = lax.broadcasted_iota(jnp.int32, (64, BLOCK), 1)
    packed = jnp.zeros((64, BLOCK), F32)
    for half, halo in enumerate((lower, upper)):
        values = kv[:, half * SPAN : (half + 1) * SPAN].astype(F32)
        padded = jnp.concatenate([halo, values], 1)
        total = taps[:, 0:1] * values
        for w in range(1, TAPS):
            total = total + taps[:, w : w + 1] * pltpu.roll(padded, w, 1)[:, BLOCK:]
        conv = total.astype(BF16)
        conv_out[:, half * SPAN : (half + 1) * SPAN] = conv
        for b in range(SPAN // BLOCK):
            part = jnp.dot(
                conv[:, b * BLOCK : (b + 1) * BLOCK], table[...], preferred_element_type=F32
            )
            packed = jnp.where(lanes // KEEP == half * 4 + b, part, packed)
    packed = packed.astype(BF16)
    for k in range(block_out.shape[0]):
        block_out[k] = packed


def query_kernel(scalars, q, own, swap, hop, taps, out):
    lower, upper = choose_halos(
        scalars, own[:, :EDGE].astype(F32), swap[:, :EDGE].astype(F32), hop[:, :EDGE].astype(F32)
    )
    for half, halo in enumerate((lower, upper)):
        for b in range(SPAN // BLOCK):
            start = half * SPAN + b * BLOCK
            values = q[start : start + BLOCK].astype(F32)
            if b:
                halo = q[start - EDGE : start].astype(F32)
            padded = jnp.concatenate([halo, values], 0)
            total = taps[0:1] * values
            for w in range(1, TAPS):
                total = total + taps[w : w + 1] * pltpu.roll(padded, w, 0)[EDGE:]
            out[start : start + BLOCK] = total.astype(BF16)


def attend_kernel(
    scalars, q, far_own, far_other, mine, from1, from2, from3, gain, out, pairs, keys, values, scores
):
    place, member = scalars[0], scalars[1]
    core = place % 2
    factor = math.log2(math.e) / math.sqrt(HEAD_CHANNELS)
    for k, ref in enumerate((mine, from1, from2, from3)):
        pairs[member ^ k] = ref[...]
    for i in range(8):
        keys[i, core] = far_own[i, :HEAD_CHANNELS]
        keys[i, 1 - core] = far_other[i, :HEAD_CHANNELS]
        values[i, core] = far_own[i, HEAD_CHANNELS:]
        values[i, 1 - core] = far_other[i, HEAD_CHANNELS:]
    R = 256
    lane = lax.broadcasted_iota(jnp.int32, (BLOCK, BLOCK), 1)
    row = lax.broadcasted_iota(jnp.int32, (BLOCK, BLOCK), 0)
    causal = row >= lane
    lower_half = lane < BLOCK // 2
    key_block = (lane % (BLOCK // 2)) // KEEP
    nt = (((1,), (1,)), ((), ()))
    for half in range(2):
        for r in range(SPAN // R):
            start = half * SPAN + r * R
            query = q[start : start + R]
            tops = []
            for c in range(R // BLOCK):
                s = start + c * BLOCK
                near = jnp.dot(
                    query[c * BLOCK : (c + 1) * BLOCK],
                    jnp.concatenate([pairs[0, :, s : s + BLOCK], pairs[1, :, s : s + BLOCK]], 0),
                    preferred_element_type=F32,
                )
                near = jnp.where(causal, near, NEGATIVE)
                scores[c * BLOCK : (c + 1) * BLOCK, 2048:] = near
                tops.append(near)
            for i in range(8):
                far = jnp.dot(
                    query,
                    jnp.concatenate([keys[i, 0], keys[i, 1]], 1),
                    preferred_element_type=F32,
                )
                for e in range(2):
                    owner = 2 * i + e
                    for c in range(R // BLOCK):
                        block = r * (R // BLOCK) + c
                        if half == 0:
                            limit = jnp.where(owner < place, 4, jnp.where(owner == place, block, 0))
                            seen = lower_half & (key_block < limit)
                        else:
                            limit = jnp.where(owner > place, 4, jnp.where(owner == place, block, 0))
                            seen = lower_half | (key_block < limit)
                        tile = jnp.where(
                            seen,
                            far[c * BLOCK : (c + 1) * BLOCK, e * BLOCK : (e + 1) * BLOCK],
                            NEGATIVE,
                        )
                        scores[c * BLOCK : (c + 1) * BLOCK, owner * BLOCK : (owner + 1) * BLOCK] = tile
                        tops[c] = jnp.maximum(tops[c], tile)
            top = jnp.concatenate([jnp.max(t, 1, keepdims=True) for t in tops], 0) * factor
            total = jnp.zeros((R, BLOCK), F32)
            summed = jnp.zeros((R, HEAD_CHANNELS), F32)
            weights = jnp.exp2(scores[:, 2048:] * factor - top)
            total = total + weights
            weights = weights.astype(BF16)
            nears = []
            for c in range(R // BLOCK):
                s = start + c * BLOCK
                nears.append(
                    lax.dot_general(
                        weights[c * BLOCK : (c + 1) * BLOCK],
                        jnp.concatenate([pairs[2, :, s : s + BLOCK], pairs[3, :, s : s + BLOCK]], 0),
                        nt,
                        preferred_element_type=F32,
                    )
                )
            summed = summed + jnp.concatenate(nears, 0)
            for i in range(8):
                weights = jnp.exp2(scores[:, i * 256 : (i + 1) * 256] * factor - top)
                total = total + weights[:, :BLOCK] + weights[:, BLOCK:]
                summed = summed + lax.dot_general(
                    weights.astype(BF16),
                    jnp.concatenate([values[i, 0], values[i, 1]], 1),
                    nt,
                    preferred_element_type=F32,
                )
            attended = summed / jnp.sum(total, 1, keepdims=True)
            mean = jnp.mean(attended * attended, 1, keepdims=True)
            normed = attended * lax.rsqrt(mean + EPSILON)
            out[start : start + R] = (normed * gain[...]).astype(BF16)


def cost(flops, moved):
    return pl.CostEstimate(flops=flops, bytes_accessed=moved, transcendentals=0)


def per_device(queries, keys_values, query_taps, pair_taps, out_gain):
    place = lax.axis_index(CTX)
    member = lax.axis_index(GROUP)
    scalars = jnp.stack([place, member]).astype(jnp.int32)
    kv = keys_values.T
    tails = jnp.stack(
        [
            jnp.concatenate([queries[e - EDGE : e], kv[:, e - BLOCK : e]], 0)
            for e in (SPAN, ROWS)
        ]
    )
    swap = lax.ppermute(tails, "core", [(0, 1), (1, 0)])
    hop = lax.ppermute(
        tails, CTX, [(i, i + 1) for i in range(1, 15, 2)] + [(i + 1, i) for i in range(1, 15, 2)]
    )
    params = functools.partial(pltpu.CompilerParams, vmem_limit_bytes=24 << 20)
    conv, blocks = pl.pallas_call(
        pack_kernel,
        out_shape=(
            jax.ShapeDtypeStruct((64, ROWS), BF16),
            jax.ShapeDtypeStruct((32, 64, BLOCK), BF16),
        ),
        in_specs=[spec(SMEM)] + [spec()] * 6,
        out_specs=(spec(), spec()),
        compiler_params=params(),
        cost_estimate=cost(1 << 24, 1 << 20),
        name="pack",
    )(scalars, kv, tails, swap, hop, pair_taps.T, jnp.asarray(dct_tile()))
    gathered = lax.all_to_all(blocks, CHIPS + GROUP, 0, 0, tiled=True)
    others = [
        lax.ppermute(conv, GROUP, [(i, i ^ k) for i in range(4)]) for k in (1, 2, 3)
    ]
    query_conv = pl.pallas_call(
        query_kernel,
        out_shape=jax.ShapeDtypeStruct((ROWS, HEAD_CHANNELS), BF16),
        in_specs=[spec(SMEM)] + [spec()] * 5,
        out_specs=spec(),
        compiler_params=params(),
        cost_estimate=cost(1 << 24, 1 << 20),
        name="conv",
    )(scalars, queries, tails, swap, hop, query_taps)
    far_own = gathered.reshape(8, 2 * HEAD_CHANNELS, BLOCK)
    far_other = lax.ppermute(far_own, "core", [(0, 1), (1, 0)])
    return pl.pallas_call(
        attend_kernel,
        out_shape=jax.ShapeDtypeStruct((ROWS, HEAD_CHANNELS), BF16),
        in_specs=[spec(SMEM)] + [spec()] * 8,
        out_specs=spec(),
        scratch_shapes=[
            VMEM((4, 64, ROWS), BF16),
            VMEM((8, 2, HEAD_CHANNELS, BLOCK), BF16),
            VMEM((8, 2, HEAD_CHANNELS, BLOCK), BF16),
            VMEM((256, 2048 + BLOCK), F32),
        ],
        compiler_params=params(),
        cost_estimate=cost(1 << 30, 1 << 21),
        name="attend",
    )(scalars, query_conv, far_own, far_other, conv, *others, out_gain.reshape(1, -1))


def solution(mesh):
    fine = Mesh(mesh.devices.reshape(2, 4, 2, 8, 2, 2), CTX + MP)
    in_specs = (P(CTX, MP), P(CTX, MP), P(None, MP), P(None, MP), P(MP))
    return jax.shard_map(
        per_device, mesh=fine, in_specs=in_specs, out_specs=P(CTX, MP), check_vma=False
    )
```

time: 104 us -> 53.6 us (0.52)
  waiting for transfers between devices: 57 us -> 2.27 us
  blocking collectives: 0 us -> 18.5 us
  between operations: 13.7 us -> 0.16 us
  starting transfers between devices: 14.6 us -> 22.4 us
  Pallas kernels: 0 us -> 7.56 us
  matrix products: 7.34 us -> 0 us
  other arithmetic: 4.51 us -> 0.09 us
  local copies, waits for them, and re-layouts: 6.06 us -> 2.15 us
    all_gather x1 -> x0, waiting for transfers between devices: 43.6 us -> none  [per_device(): piece = lax.all_gather(packed, 'ctx', axis=0, tiled=True)]
    all_to_all x0 -> x1, blocking collectives: none -> 18.5 us  [per_device(): gathered = lax.all_to_all(blocks, CHIPS + GROUP, 0, 0, tiled=True)]
    ppermute x4 -> x6, waiting for transfers between devices: 13.4 us -> 2.27 us  [the longest x3 2.21 us: per_device(): lax.ppermute(conv, GROUP, [(i, i ^ k) for i in range(4)])]
    ppermute x4 -> x6, starting transfers between devices: 14.5 us -> 22.4 us  [the longest x3 9.88 us: per_device(): lax.ppermute(conv, GROUP, [(i, i ^ k) for i in range(4)])]
    pallas_call x0 -> x3, Pallas kernels: none -> 7.56 us  [the longest x1 5.76 us: per_device(): pl.pallas_call(attend_kernel, out_shape=jax.ShapeDtypeStruct((ROWS, HEAD_...]
    dot_general x7 -> x0, matrix products: 7.34 us -> none  [the longest x2 4.17 us: attend(): jnp.einsum('qhd,kd->qhk', part, keys[:, :HEAD_CHANNELS], preferred_elemen...]
    slice x21 -> x2, local copies, waits for them, and re-layouts: 4.09 us -> 1.44 us  [the longest x1 0.74 us: per_device(): kv[:, e - BLOCK:e]]
    reduce_sum x3 -> x0, other arithmetic: 1.73 us -> none  [the longest x1 1.25 us: attend(): totals.append(rescale * total[begin:begin + size] + jnp.sum(weights, -1))]
  transfers between devices with their start and end apart: 5 -> 6, of which waited for: 4 -> 2; matrix products, arithmetic and copies ran while one was open for 5% -> 0% of each run, Pallas kernels for 0% -> 2%
where the time goes in v1:
time: 53.6 us; the launch traced here: 53.1 us
  starting transfers between devices  22.4 us (42%)
  blocking collectives  18.5 us (35%)
  Pallas kernels  7.56 us (14%)
  waiting for transfers between devices  2.27 us (4%)
  local copies, waits for them, and re-layouts  2.15 us (4%)
    all_to_all x1, blocking collectives, per_device(): gathered = lax.all_to_all(blocks, CHIPS + GROUP, 0, 0, tiled=True)  18.5 us
    ppermute x3, starting transfers between devices, per_device(): lax.ppermute(conv, GROUP, [(i, i ^ k) for i in range(4)])  9.88 us
    pallas_call x1, Pallas kernels, per_device(): pl.pallas_call(attend_kernel, out_shape=jax.ShapeDtypeStruct((ROWS, HEAD_...  5.76 us
    ppermute x1, starting transfers between devices, per_device(): swap = lax.ppermute(tails, 'core', [(0, 1), (1, 0)])  4.94 us
    ppermute x1, starting transfers between devices, per_device(): lax.ppermute(tails, CTX, [(i, i + 1) for i in range(1, 15, 2)] + [(i + 1,...  4.64 us
    ppermute x1, starting transfers between devices, per_device(): far_other = lax.ppermute(far_own, 'core', [(0, 1), (1, 0)])  2.95 us
    ppermute x3, waiting for transfers between devices, per_device(): lax.ppermute(conv, GROUP, [(i, i ^ k) for i in range(4)])  2.21 us
  transfers between devices with their start and end apart: 6, of which 2 were waited for; matrix products, arithmetic and copies ran while one was open for 0% of the time, Pallas kernels for 2%

profile of v1, /device:TPU:1, one launch (start us, length us, event | category | flops | bytes accessed | tf_op | source)
XLA Modules:
  0.0 53.1 jit_solution(17946700330061326801)
XLA Ops:
  0.0 0.7 %fusion = (bf16[16,128]{1,0:T(8,128)(2,1)S(1)}, bf16[16,128]{1,0:T(8,128)(2,1)S(1)}) fusion(bf16[1024,128]{1,0:T(8,128)(2,1)} %q.1), kind=kLoop, calls=%fused_computation.4 | loop fusion | bytes 16384 | tf_op jit(solution)/shard_map/slice | solution.py:199
  0.7 0.7 %fusion.1 = (bf16[64,128]{1,0:T(8,128)(2,1)S(1)}, bf16[64,128]{1,0:T(8,128)(2,1)S(1)}) fusion(bf16[64,1024]{1,0:T(8,128)(2,1)} %bitcast.12), kind=kLoop, calls=%fused_computation.5 | loop fusion | bytes 65536 | tf_op jit(solution)/shard_map/slice | solution.py:199
  1.4 0.0 copy-start.1
  1.5 4.6 %collective-permute-start.1 = (bf16[2,80,128]{2,1,0:T(8,128)(2,1)S(1)}, bf16[2,80,128]{2,1,0:T(8,128)(2,1)S(1)}, u32[]{:S(2)}, u32[]{:S(2)}) collective-permute-start(bf16[2,80,128]{2,1,0:T(8,128)(2,1)S(1)} %pad_maximum_fusion.own), channel_id=1, source_target_pairs={{32,64},{96,128},{160,192},{224,256},{288,320},{352,384},{416,448}... | collective-permute-start | bytes 122888 | tf_op jit(solution)/shard_map/ppermute | solution.py:204
  6.1 4.9 %collective-permute-start = (bf16[2,80,128]{2,1,0:T(8,128)(2,1)S(1)}, bf16[2,80,128]{2,1,0:T(8,128)(2,1)S(1)}, u32[]{:S(2)}, u32[]{:S(2)}) collective-permute-start(bf16[2,80,128]{2,1,0:T(8,128)(2,1)S(1)} %pad_maximum_fusion.own), channel_id=1, source_target_pairs={{0,32},{32,0},{1,33},{33,1},{2,34},{34,2},{3,35},{35,3},{4,36},{36... | collective-permute-start | bytes 122888 | tf_op jit(solution)/shard_map/ppermute | solution.py:203
  11.1 0.0 copy-start.5
  11.1 0.0 copy-start.2
  11.1 0.1 pad_add_fusion.scalars
  11.2 0.6 %copy-done.5 = f32[4,64]{1,0:T(4,128)S(1)} copy-done((f32[4,64]{1,0:T(4,128)S(1)}, f32[4,64]{1,0:T(4,128)}, u32[]{:S(2)}) %copy-start.5) | copy-done | bytes 1048
  11.8 0.1 copy.7
  11.9 0.0 collective-permute-done.1.hop
  11.9 0.1 collective-permute-done.swap
  11.9 0.0 copy-done.1
  11.9 0.0 copy-done.2
  11.9 1.0 %pack.1 = (bf16[64,1024]{1,0:T(8,128)(2,1)S(1)}, bf16[32,64,128]{2,1,0:T(8,128)(2,1)S(1)}) custom-call(s32[2]{0:T(128)S(1)} %pad_add_fusion.scalars, bf16[64,1024]{1,0:T(8,128)(2,1)S(1)} %bitcast.13, bf16[2,80,128]{2,1,0:T(8,128)(2,1)S(1)} %pad_maximum_fusion.own, bf16[2,80,128]{2,1,0:T(8,128)(2,1)S(1)} %collective-permute-done.swap, ...), custom_call_target="tpu_custom_call" | custom-call | flops 16777216 | bytes 1048576 | tf_op jit(solution)/shard_map/pack/pallas_call | solution.py:208
  12.9 0.0 copy-start
  12.9 18.5 %all_to_all.5 = bf16[32,64,128]{2,1,0:T(8,128)(2,1)S(1)} all-to-all(bf16[32,64,128]{2,1,0:T(8,128)(2,1)S(1)} %get-tuple-element.7), channel_id=1, replica_groups=mesh['y_lo'=2,'x'=4,'core'=2,'z_hi'=8,'z_lo'=2,'y_hi'=2] {'y_lo','x','z_..., dimensions={0} | all-to-all | bytes 1048576 | tf_op jit(solution)/shard_map/all_to_all | solution.py:220
  31.4 0.0 copy-start.3
  31.4 3.0 %collective-permute-start.2 = (bf16[8,256,128]{2,1,0:T(8,128)(2,1)S(1)}, bf16[8,256,128]{2,1,0:T(8,128)(2,1)S(1)}, u32[]{:S(2)}, u32[]{:S(2)}) collective-permute-start(bf16[8,256,128]{2,1,0:T(8,128)(2,1)S(1)} %bitcast.10), channel_id=1, source_target_pairs={{0,32},{32,0},{1,33},{33,1},{2,34},{34,2},{3,35},{35,3},{4,36},{36... | collective-permute-start | bytes 1572872 | tf_op jit(solution)/shard_map/ppermute | solution.py:234
  34.4 2.1 %collective-permute-start.5 = (bf16[64,1024]{1,0:T(8,128)(2,1)S(1)}, bf16[64,1024]{1,0:T(8,128)(2,1)S(1)}, u32[]{:S(2)}, u32[]{:S(2)}) collective-permute-start(bf16[64,1024]{1,0:T(8,128)(2,1)S(1)} %get-tuple-element.8.mine), channel_id=1, source_target_pairs={{0,3},{1,2},{2,1},{3,0},{4,7},{5,6},{6,5},{7,4},{8,11},{9,10},{10,... | collective-permute-start | bytes 393224 | tf_op jit(solution)/shard_map/ppermute | solution.py:222
  36.5 3.0 %collective-permute-start.4 = (bf16[64,1024]{1,0:T(8,128)(2,1)S(1)}, bf16[64,1024]{1,0:T(8,128)(2,1)S(1)}, u32[]{:S(2)}, u32[]{:S(2)}) collective-permute-start(bf16[64,1024]{1,0:T(8,128)(2,1)S(1)} %get-tuple-element.8.mine), channel_id=1, source_target_pairs={{0,2},{1,3},{2,0},{3,1},{4,6},{5,7},{6,4},{7,5},{8,10},{9,11},{10,... | collective-permute-start | bytes 393224 | tf_op jit(solution)/shard_map/ppermute | solution.py:222
  39.5 4.8 %collective-permute-start.3 = (bf16[64,1024]{1,0:T(8,128)(2,1)S(1)}, bf16[64,1024]{1,0:T(8,128)(2,1)S(1)}, u32[]{:S(2)}, u32[]{:S(2)}) collective-permute-start(bf16[64,1024]{1,0:T(8,128)(2,1)S(1)} %get-tuple-element.8.mine), channel_id=1, source_target_pairs={{0,1},{1,0},{2,3},{3,2},{4,5},{5,4},{6,7},{7,6},{8,9},{9,8},{10,11... | collective-permute-start | bytes 393224 | tf_op jit(solution)/shard_map/ppermute | solution.py:222
  44.3 0.0 copy-done
  44.3 0.0 copy-done.3
  44.3 0.8 %conv.1.q = bf16[1024,128]{1,0:T(8,128)(2,1)S(1)} custom-call(s32[2]{0:T(128)S(1)} %pad_add_fusion.scalars, bf16[1024,128]{1,0:T(8,128)(2,1)S(1)} %copy-done, bf16[2,80,128]{2,1,0:T(8,128)(2,1)S(1)} %pad_maximum_fusion.own, bf16[2,80,128]{2,1,0:T(8,128)(2,1)S(1)} %collective-permute-done.swap, bf16[2,80,128]{2,1,0:T(8,128)(2,1)S(1)} %collective-permute-done.1.hop, ...), custom_call_target="tpu_custom_call" | custom-call | flops 16777216 | bytes 1048576 | tf_op jit(solution)/shard_map/conv/pallas_call | solution.py:224
  45.1 0.0 copy-start.4
  45.1 0.0 collective-permute-done.5.from3
  45.1 0.0 collective-permute-done.4.from2
  45.1 2.2 %collective-permute-done.3.from1 = bf16[64,1024]{1,0:T(8,128)(2,1)S(1)} collective-permute-done((bf16[64,1024]{1,0:T(8,128)(2,1)S(1)}, bf16[64,1024]{1,0:T(8,128)(2,1)S(1)}, u32[]{:S(2)}, u32[]{:S(2)}) %collective-permute-start.3) | collective-permute-done | bytes 131104 | tf_op jit(solution)/shard_map/ppermute | solution.py:222
  47.4 0.0 collective-permute-done.2.far_other
  47.4 0.0 copy-done.4
  47.4 5.8 %attend.1 = bf16[1024,128]{1,0:T(8,128)(2,1)} custom-call(s32[2]{0:T(128)S(1)} %pad_add_fusion.scalars, bf16[1024,128]{1,0:T(8,128)(2,1)S(1)} %conv.1.q, bf16[8,256,128]{2,1,0:T(8,128)(2,1)S(1)} %bitcast.11, bf16[8,256,128]{2,1,0:T(8,128)(2,1)S(1)} %collective-permute-done.2.far_other, bf16[64,1024]{1,0:T(8,128)(2,1)S(1)} %get-tuple-element.8.mine, ...), custom_call_target="tpu_custom_call" | custom-call | flops 1073741824 | bytes 2097152 | tf_op jit(solution)/shard_map/attend/pallas_call | solution.py:235
  (2 shorter events, 0.0 us)
Async XLA Ops:
  1.4 10.5 %copy-start.1 = (bf16[1024,64]{0,1:T(8,128)(2,1)S(1)}, bf16[1024,64]{0,1:T(8,128)(2,1)}, u32[]{:S(2)}) copy-start(bf16[1024,64]{0,1:T(8,128)(2,1)} %param.7) | copy-start | bytes 393220
  1.5 10.4 %collective-permute-start.1 = (bf16[2,80,128]{2,1,0:T(8,128)(2,1)S(1)}, bf16[2,80,128]{2,1,0:T(8,128)(2,1)S(1)}, u32[]{:S(2)}, u32[]{:S(2)}) collective-permute-start(bf16[2,80,128]{2,1,0:T(8,128)(2,1)S(1)} %pad_maximum_fusion.own), channel_id=1, source_target_pairs={{32,64},{96,128},{160,192},{224,256},{288,320},{352,384},{416,448}... | collective-permute-start | bytes 122888 | tf_op jit(solution)/shard_map/ppermute | solution.py:204
  6.1 5.8 %collective-permute-start = (bf16[2,80,128]{2,1,0:T(8,128)(2,1)S(1)}, bf16[2,80,128]{2,1,0:T(8,128)(2,1)S(1)}, u32[]{:S(2)}, u32[]{:S(2)}) collective-permute-start(bf16[2,80,128]{2,1,0:T(8,128)(2,1)S(1)} %pad_maximum_fusion.own), channel_id=1, source_target_pairs={{0,32},{32,0},{1,33},{33,1},{2,34},{34,2},{3,35},{35,3},{4,36},{36... | collective-permute-start | bytes 122888 | tf_op jit(solution)/shard_map/ppermute | solution.py:203
  11.1 0.7 %copy-start.5 = (f32[4,64]{1,0:T(4,128)S(1)}, f32[4,64]{1,0:T(4,128)}, u32[]{:S(2)}) copy-start(f32[4,64]{1,0:T(4,128)} %param.9) | copy-start | bytes 3076
  11.1 0.8 %copy-start.2 = (bf16[128,128]{1,0:T(8,128)(2,1)S(1)}, bf16[128,128]{1,0:T(8,128)(2,1)}, u32[]{:S(2)}) copy-start(bf16[128,128]{1,0:T(8,128)(2,1)} %constant.26.clone.table) | copy-start | bytes 98308
  12.9 31.4 %copy-start = (bf16[1024,128]{1,0:T(8,128)(2,1)S(1)}, bf16[1024,128]{1,0:T(8,128)(2,1)}, u32[]{:S(2)}) copy-start(bf16[1024,128]{1,0:T(8,128)(2,1)} %q.1) | copy-start | bytes 786436
  31.4 12.9 %copy-start.3 = (f32[4,128]{1,0:T(4,128)S(1)}, f32[4,128]{1,0:T(4,128)}, u32[]{:S(2)}) copy-start(f32[4,128]{1,0:T(4,128)} %taps.1) | copy-start | bytes 6148
  31.4 15.9 %collective-permute-start.2 = (bf16[8,256,128]{2,1,0:T(8,128)(2,1)S(1)}, bf16[8,256,128]{2,1,0:T(8,128)(2,1)S(1)}, u32[]{:S(2)}, u32[]{:S(2)}) collective-permute-start(bf16[8,256,128]{2,1,0:T(8,128)(2,1)S(1)} %bitcast.10), channel_id=1, source_target_pairs={{0,32},{32,0},{1,33},{33,1},{2,34},{34,2},{3,35},{35,3},{4,36},{36... | collective-permute-start | bytes 1572872 | tf_op jit(solution)/shard_map/ppermute | solution.py:234
  34.4 10.7 %collective-permute-start.5 = (bf16[64,1024]{1,0:T(8,128)(2,1)S(1)}, bf16[64,1024]{1,0:T(8,128)(2,1)S(1)}, u32[]{:S(2)}, u32[]{:S(2)}) collective-permute-start(bf16[64,1024]{1,0:T(8,128)(2,1)S(1)} %get-tuple-element.8.mine), channel_id=1, source_target_pairs={{0,3},{1,2},{2,1},{3,0},{4,7},{5,6},{6,5},{7,4},{8,11},{9,10},{10,... | collective-permute-start | bytes 393224 | tf_op jit(solution)/shard_map/ppermute | solution.py:222
  36.5 8.7 %collective-permute-start.4 = (bf16[64,1024]{1,0:T(8,128)(2,1)S(1)}, bf16[64,1024]{1,0:T(8,128)(2,1)S(1)}, u32[]{:S(2)}, u32[]{:S(2)}) collective-permute-start(bf16[64,1024]{1,0:T(8,128)(2,1)S(1)} %get-tuple-element.8.mine), channel_id=1, source_target_pairs={{0,2},{1,3},{2,0},{3,1},{4,6},{5,7},{6,4},{7,5},{8,10},{9,11},{10,... | collective-permute-start | bytes 393224 | tf_op jit(solution)/shard_map/ppermute | solution.py:222
  39.5 7.9 %collective-permute-start.3 = (bf16[64,1024]{1,0:T(8,128)(2,1)S(1)}, bf16[64,1024]{1,0:T(8,128)(2,1)S(1)}, u32[]{:S(2)}, u32[]{:S(2)}) collective-permute-start(bf16[64,1024]{1,0:T(8,128)(2,1)S(1)} %get-tuple-element.8.mine), channel_id=1, source_target_pairs={{0,1},{1,0},{2,3},{3,2},{4,5},{5,4},{6,7},{7,6},{8,9},{9,8},{10,11... | collective-permute-start | bytes 393224 | tf_op jit(solution)/shard_map/ppermute | solution.py:222
  45.1 2.2 %copy-start.4 = (f32[128]{0:T(128)S(1)}, f32[128]{0:T(128)}, u32[]{:S(2)}) copy-start(f32[128]{0:T(128)} %param.10) | copy-start | bytes 1540

commit v2 on v1

v2 whole, which is shorter than its diff:
```python
import functools
import math

import jax
import jax.numpy as jnp
import numpy as np
from jax import lax
from jax.experimental import pallas as pl
from jax.experimental.pallas import tpu as pltpu
from jax.sharding import Mesh, PartitionSpec as P

HEAD_CHANNELS = 128
TAPS = 4
BLOCK = 128
KEEP = 16
SPAN = 512
ROWS = 2 * SPAN
NEGATIVE = -1e30
EPSILON = 1e-06
EDGE = 16
CHUNK = 256
FACTOR = math.log2(math.e) / math.sqrt(HEAD_CHANNELS)

CTX = ("y_lo", "x", "core")
MP = ("z_hi", "z_lo", "y_hi")
GROUP = ("z_lo", "y_hi")
CHIPS = ("y_lo", "x")

VMEM = pltpu.VMEM
SMEM = pltpu.SMEM
F32 = jnp.float32
BF16 = jnp.bfloat16
NT = (((1,), (1,)), ((), ()))


def spec(space=VMEM):
    return pl.BlockSpec(memory_space=space)


def dct_table():
    j = np.arange(KEEP, dtype=np.float32)[:, None]
    u = np.arange(BLOCK, dtype=np.float32)[None, :]
    table = np.cos(np.float32(math.pi) * (u + np.float32(0.5)) * j / np.float32(BLOCK))
    table = table * np.float32(math.sqrt(2.0 / BLOCK))
    table = np.where(j == 0, table * np.float32(math.sqrt(0.5)), table)
    return table.astype(jnp.bfloat16)


def dct_tile():
    return np.tile(dct_table().T, (1, BLOCK // KEEP))


def tails_kernel(q, kv, out, sems):
    copies = []
    for half in range(2):
        end = (half + 1) * SPAN
        copies.append((q.at[end - EDGE : end], out.at[half, :EDGE]))
        copies.append((kv.at[:, end - BLOCK : end], out.at[half, EDGE:]))
    copies = [pltpu.make_async_copy(*c, sems.at[k]) for k, c in enumerate(copies)]
    for copy in copies:
        copy.start()
    for copy in copies:
        copy.wait()


def choose_halos(own, swap, hop):
    place = lax.axis_index(CTX)
    odd = place % 2 == 1
    lower = jnp.where(odd, swap[0], hop[0])
    lower = jnp.where(place == 0, jnp.zeros_like(lower), lower)
    upper = jnp.where(odd, hop[1], swap[1])
    upper = jnp.where(place == 15, own[0], upper)
    return lower, upper


def conv_kernel(kv, own, swap, hop, taps, conv_out):
    turned = jnp.transpose(
        jnp.concatenate(
            [
                jnp.concatenate([taps[...], jnp.zeros((4, 64), F32)], 0),
                jnp.zeros((8, 64), F32),
            ],
            1,
        )
    )[:64]
    halos = choose_halos(*(ref[:, EDGE:].astype(F32) for ref in (own, swap, hop)))
    for half, halo in enumerate(halos):
        values = kv[:, half * SPAN : (half + 1) * SPAN].astype(F32)
        padded = jnp.concatenate([halo, values], 1)
        total = turned[:, 0:1] * values
        for w in range(1, TAPS):
            total = total + turned[:, w : w + 1] * pltpu.roll(padded, w, 1)[:, BLOCK:]
        conv_out[:, half * SPAN : (half + 1) * SPAN] = total.astype(BF16)


def pack_kernel(conv, table, block_out):
    lanes = lax.broadcasted_iota(jnp.int32, (64, BLOCK), 1)
    packed = jnp.zeros((64, BLOCK), F32)
    for b in range(ROWS // BLOCK):
        part = jnp.dot(
            conv[:, b * BLOCK : (b + 1) * BLOCK], table[...], preferred_element_type=F32
        )
        packed = jnp.where(lanes // KEEP == b, part, packed)
    uneven = lax.axis_index(CHIPS) % 2 == 1
    packed = jnp.where(uneven, pltpu.roll(packed, BLOCK // 2, 1), packed).astype(BF16)
    for k in range(block_out.shape[0]):
        block_out[k] = packed


def join_kernel(mine, near, out):
    out[:64] = mine[...]
    out[64:] = near[...]


def query_kernel(q, own, swap, hop, taps, out):
    halos = choose_halos(*(ref[:, :EDGE].astype(F32) for ref in (own, swap, hop)))
    for half, halo in enumerate(halos):
        for b in range(SPAN // BLOCK):
            start = half * SPAN + b * BLOCK
            values = q[start : start + BLOCK].astype(F32)
            if b:
                halo = q[start - EDGE : start].astype(F32)
            padded = jnp.concatenate([halo, values], 0)
            total = taps[0:1] * values
            for w in range(1, TAPS):
                total = total + taps[w : w + 1] * pltpu.roll(padded, w, 0)[EDGE:]
            out[start : start + BLOCK] = total.astype(BF16)


def arrange(far, tiles):
    left = lax.broadcasted_iota(jnp.int32, (64, BLOCK), 1) < BLOCK // 2
    for kind in range(2):
        for j in range(4):
            for m in range(2):
                even, uneven = far[2 * j, 2 * kind + m], far[2 * j + 1, 2 * kind + m]
                rows = slice(64 * m, 64 * (m + 1))
                tiles[kind, 0, j, rows] = jnp.where(left, even, uneven)
                tiles[kind, 1, j, rows] = jnp.where(left, uneven, even)


class FarPass:
    def __init__(self, own, q, tiles, scores, tops, totals, sums):
        place = lax.axis_index(CTX)
        self.own, self.q, self.tiles, self.scores = own, q, tiles, scores
        self.tops, self.totals, self.sums = tops, totals, sums
        self.middle = place // 2
        self.before = self.middle if own else self.middle + place % 2
        self.turn = jnp.minimum(self.before // 2, 3)
        lane = lax.broadcasted_iota(jnp.int32, (1, BLOCK), 1)
        self.key_block = (lane % (BLOCK // 2)) // KEEP
        self.left = lane < BLOCK // 2

    def bias(self, high, j, block):
        def limit(i):
            low = jnp.where(i < self.before, 4, 0)
            top = jnp.where(i >= self.before + (1 if self.own else 0), 4, 0)
            value = jnp.where(high, top, low)
            return jnp.where(i == self.middle, block, value) if self.own else value

        first, second = limit(2 * j), limit(2 * j + 1)
        left, right = jnp.where(high, second, first), jnp.where(high, first, second)
        seen = self.key_block < jnp.where(self.left, left, right)
        return jnp.where(seen, 0.0, NEGATIVE)

    def variable(self):
        for v in range(5):
            high = v > self.turn
            side = high.astype(jnp.int32)
            yield v, high, side, v - side

    def score(self, r):
        rows = slice(r * CHUNK, (r + 1) * CHUNK)
        upper = self.q[SPAN + r * CHUNK : SPAN + (r + 1) * CHUNK]
        for j in range(2):
            far = jnp.dot(
                upper,
                jnp.concatenate([self.tiles[0, 0, 2 * j], self.tiles[0, 0, 2 * j + 1]], 1),
                preferred_element_type=F32,
            )
            one, two = far[:, :BLOCK], far[:, BLOCK:]
            self.scores[r, 5 + 2 * j] = one
            self.scores[r, 6 + 2 * j] = two
            self.tops[1, rows] = jnp.maximum(self.tops[1, rows], jnp.maximum(one, two))
        for v, high, side, j in self.variable():
            start = pl.multiple_of(side * SPAN + r * CHUNK, CHUNK)
            far = jnp.dot(
                self.q[pl.ds(start, CHUNK)], self.tiles[0, side, j], preferred_element_type=F32
            )
            biases = [
                jnp.broadcast_to(self.bias(high, j, r * (CHUNK // BLOCK) + c), (BLOCK, BLOCK))
                for c in range(CHUNK // BLOCK)
            ]
            far = far + jnp.concatenate(biases, 0)
            self.scores[r, v] = far
            self.tops[side, rows] = jnp.maximum(self.tops[side, rows], far)

    def add(self, r):
        rows = slice(r * CHUNK, (r + 1) * CHUNK)
        top = self.tops[1, rows] * FACTOR
        for j in range(2):
            one = jnp.exp2(self.scores[r, 5 + 2 * j] * FACTOR - top)
            two = jnp.exp2(self.scores[r, 6 + 2 * j] * FACTOR - top)
            self.totals[1, rows] = self.totals[1, rows] + one + two
            self.sums[1, rows] = self.sums[1, rows] + lax.dot_general(
                jnp.concatenate([one, two], 1).astype(BF16),
                jnp.concatenate([self.tiles[1, 0, 2 * j], self.tiles[1, 0, 2 * j + 1]], 1),
                NT,
                preferred_element_type=F32,
            )
        for v, high, side, j in self.variable():
            weights = jnp.exp2(self.scores[r, v] * FACTOR - self.tops[side, rows] * FACTOR)
            self.totals[side, rows] = self.totals[side, rows] + weights
            self.sums[side, rows] = self.sums[side, rows] + lax.dot_general(
                weights.astype(BF16), self.tiles[1, side, j], NT, preferred_element_type=F32
            )


def near_kernel(q, far, mine, near, both, tops, totals, sums, pairs, tiles, scores):
    member = lax.axis_index(GROUP)
    pairs[member] = mine[...]
    pairs[member ^ 1] = near[...]
    pairs[member ^ 2] = both[:64]
    pairs[member ^ 3] = both[64:]
    arrange(far, tiles)
    lane = lax.broadcasted_iota(jnp.int32, (BLOCK, BLOCK), 1)
    row = lax.broadcasted_iota(jnp.int32, (BLOCK, BLOCK), 0)

    def near_tile(kind, start):
        return jnp.concatenate(
            [pairs[2 * kind, :, start : start + BLOCK], pairs[2 * kind + 1, :, start : start + BLOCK]], 0
        )

    work = FarPass(True, q, tiles, scores, tops, totals, sums)
    for r in range(SPAN // CHUNK):
        blocks = [
            (half, r * CHUNK + c * BLOCK) for half in range(2) for c in range(CHUNK // BLOCK)
        ]
        for k, (half, start) in enumerate(blocks):
            place = half * SPAN + start
            score = jnp.dot(
                q[place : place + BLOCK], near_tile(0, place), preferred_element_type=F32
            )
            score = jnp.where(row >= lane, score, NEGATIVE)
            scores[r, 9 + half, start % CHUNK : start % CHUNK + BLOCK] = score
            tops[half, start : start + BLOCK] = score
        work.score(r)
        rows = slice(r * CHUNK, (r + 1) * CHUNK)
        for half in range(2):
            tops[half, rows] = jnp.broadcast_to(
                jnp.max(tops[half, rows], 1, keepdims=True), (CHUNK, BLOCK)
            )
        for k, (half, start) in enumerate(blocks):
            place = half * SPAN + start
            weights = jnp.exp2(
                scores[r, 9 + half, start % CHUNK : start % CHUNK + BLOCK] * FACTOR
                - tops[half, start : start + BLOCK] * FACTOR
            )
            totals[half, start : start + BLOCK] = weights
            sums[half, start : start + BLOCK] = lax.dot_general(
                weights.astype(BF16), near_tile(1, place), NT, preferred_element_type=F32
            )
        work.add(r)


def far_kernel(q, far, old_tops, old_totals, old_sums, gain, out, tiles, scores, tops, totals, sums):
    arrange(far, tiles)
    work = FarPass(False, q, tiles, scores, tops, totals, sums)
    for r in range(SPAN // CHUNK):
        rows = slice(r * CHUNK, (r + 1) * CHUNK)
        tops[:, rows] = old_tops[:, rows]
        work.score(r)
        for half in range(2):
            top = jnp.broadcast_to(jnp.max(tops[half, rows], 1, keepdims=True), (CHUNK, BLOCK))
            tops[half, rows] = top
            scale = jnp.exp2((old_tops[half, rows] - top) * FACTOR)
            totals[half, rows] = old_totals[half, rows] * scale
            sums[half, rows] = old_sums[half, rows] * scale
        work.add(r)
        for half in range(2):
            attended = sums[half, rows] / jnp.sum(totals[half, rows], 1, keepdims=True)
            mean = jnp.mean(attended * attended, 1, keepdims=True)
            normed = attended * lax.rsqrt(mean + EPSILON)
            start = half * SPAN + r * CHUNK
            out[start : start + CHUNK] = (normed * gain[...]).astype(BF16)


def cost(flops, moved):
    return pl.CostEstimate(flops=flops, bytes_accessed=moved, transcendentals=0)


def swapped(value, axis):
    return lax.ppermute(value, axis, [(0, 1), (1, 0)])


def per_device(queries, keys_values, query_taps, pair_taps, out_gain):
    def call(kernel, name, out_shape, operands, spaces=None, scratch=(), flops=1 << 24):
        many = isinstance(out_shape, tuple)
        return pl.pallas_call(
            kernel,
            out_shape=out_shape,
            in_specs=[spec(s) for s in spaces] if spaces else [spec()] * len(operands),
            out_specs=(spec(),) * len(out_shape) if many else spec(),
            scratch_shapes=scratch,
            compiler_params=pltpu.CompilerParams(vmem_limit_bytes=24 << 20),
            cost_estimate=cost(flops, 1 << 20),
            name=name,
        )(*operands)

    def shape(*dims, kind=BF16):
        return jax.ShapeDtypeStruct(dims, kind)

    kv = keys_values.T
    tails = call(
        tails_kernel,
        "tails",
        shape(2, EDGE + 64, BLOCK),
        (queries, kv),
        (pltpu.HBM, pltpu.HBM),
        [pltpu.SemaphoreType.DMA((4,))],
    )
    swap = swapped(tails, "core")
    hop = lax.ppermute(
        tails, CTX, [(i, i + 1) for i in range(1, 15, 2)] + [(i + 1, i) for i in range(1, 15, 2)]
    )
    conv = call(conv_kernel, "conv", shape(64, ROWS), (kv, tails, swap, hop, pair_taps))
    blocks = call(
        pack_kernel, "pack", shape(32, 64, BLOCK), (conv, jnp.asarray(dct_tile()))
    )
    gathered = lax.all_to_all(blocks, CHIPS + GROUP, 0, 0, tiled=True)
    near = swapped(conv, "y_hi")
    both = call(join_kernel, "join", shape(128, ROWS), (conv, near), flops=1 << 37)
    both = swapped(both, "z_lo")
    query_conv = call(
        query_kernel,
        "queries",
        shape(ROWS, HEAD_CHANNELS),
        (queries, tails, swap, hop, query_taps),
    )
    gathered, query_conv, both = lax.optimization_barrier((gathered, query_conv, both))
    far_own = gathered.reshape(8, 4, 64, BLOCK)
    far_other = swapped(far_own, "core")
    state = shape(2, SPAN, BLOCK, kind=F32)
    tiles = VMEM((2, 2, 4, HEAD_CHANNELS, BLOCK), BF16)
    tops, totals, sums = call(
        near_kernel,
        "near",
        (state, state, state),
        (query_conv, far_own, conv, near, both),
        scratch=[VMEM((4, 64, ROWS), BF16), tiles, VMEM((2, 11, CHUNK, BLOCK), F32)],
        flops=1 << 30,
    )
    return call(
        far_kernel,
        "far",
        shape(ROWS, HEAD_CHANNELS),
        (query_conv, far_other, tops, totals, sums, out_gain.reshape(1, -1)),
        scratch=[tiles, VMEM((2, 9, CHUNK, BLOCK), F32)] + [VMEM((2, SPAN, BLOCK), F32)] * 3,
        flops=1 << 30,
    )


def solution(mesh):
    fine = Mesh(mesh.devices.reshape(2, 4, 2, 8, 2, 2), CTX + MP)
    in_specs = (P(CTX, MP), P(CTX, MP), P(None, MP), P(None, MP), P(MP))
    return jax.shard_map(
        per_device, mesh=fine, in_specs=in_specs, out_specs=P(CTX, MP), check_vma=False
    )
```

time: 53.6 us -> 47.8 us (0.89)
  blocking collectives: 18.5 us -> 0 us
  waiting for transfers between devices: 2.27 us -> 13.3 us
  starting transfers between devices: 22.4 us -> 23.8 us
    all_to_all x1 -> x0, blocking collectives: 18.5 us -> none  [per_device(): gathered = lax.all_to_all(blocks, CHIPS + GROUP, 0, 0, tiled=True)]
    ppermute x5 -> x4, waiting for transfers between devices: 2.27 us -> 9.94 us  [swapped(): return lax.ppermute(value, axis, [(0, 1), (1, 0)])]
    all_to_all x0 -> x1, starting transfers between devices: none -> 5.23 us  [per_device(): gathered = lax.all_to_all(blocks, CHIPS + GROUP, 0, 0, tiled=True)]
    ppermute x1, waiting for transfers between devices: 0.01 us -> 3.38 us  [per_device(): lax.ppermute(tails, CTX, [(i, i + 1) for i in range(1, 15, 2)] + [(i + 1,...]
    ppermute x1, starting transfers between devices: 4.64 us -> 1.92 us  [per_device(): lax.ppermute(tails, CTX, [(i, i + 1) for i in range(1, 15, 2)] + [(i + 1,...]
    unnamed x13 -> x16, local copies, waits for them, and re-layouts: 0.7 us -> 2.53 us
    slice x2 -> x0, local copies, waits for them, and re-layouts: 1.44 us -> none  [the longest x1 0.74 us: per_device(): kv[:, e - BLOCK:e]]
    ppermute x5 -> x4, starting transfers between devices: 17.8 us -> 16.7 us  [swapped(): return lax.ppermute(value, axis, [(0, 1), (1, 0)])]
  transfers between devices with their start and end apart: 6 -> 6, of which waited for: 2 -> 2; matrix products, arithmetic and copies ran while one was open for 0% -> 0% of each run, Pallas kernels for 2% -> 8%
where the time goes in v2:
time: 47.8 us; the launch traced here: 47.5 us
  starting transfers between devices  23.8 us (50%)
  waiting for transfers between devices  13.3 us (28%)
  Pallas kernels  7.64 us (16%)
  local copies, waits for them, and re-layouts  2.53 us (5%)
    ppermute x4, starting transfers between devices, swapped(): return lax.ppermute(value, axis, [(0, 1), (1, 0)])  16.7 us
    ppermute x4, waiting for transfers between devices, swapped(): return lax.ppermute(value, axis, [(0, 1), (1, 0)])  9.94 us
    pallas_call x7, Pallas kernels, call(): pl.pallas_call(kernel, out_shape=out_shape, in_specs=[spec(s) for s in sp...  7.64 us
    all_to_all x1, starting transfers between devices, per_device(): gathered = lax.all_to_all(blocks, CHIPS + GROUP, 0, 0, tiled=True)  5.23 us
    ppermute x1, waiting for transfers between devices, per_device(): lax.ppermute(tails, CTX, [(i, i + 1) for i in range(1, 15, 2)] + [(i + 1,...  3.38 us
    unnamed x16, local copies, waits for them, and re-layouts  2.53 us
    ppermute x1, starting transfers between devices, per_device(): lax.ppermute(tails, CTX, [(i, i + 1) for i in range(1, 15, 2)] + [(i + 1,...  1.92 us
  transfers between devices with their start and end apart: 6, of which 2 were waited for; matrix products, arithmetic and copies ran while one was open for 0% of the time, Pallas kernels for 8%

profile of v2, /device:TPU:1, one launch (start us, length us, event | category | flops | bytes accessed | tf_op | source)
XLA Modules:
  0.0 47.5 jit_solution(16053172605504574170)
XLA Ops:
  0.0 0.0 copy-start
  0.0 0.9 %copy-done = bf16[1024,128]{1,0:T(8,128)(2,1)S(1)} copy-done((bf16[1024,128]{1,0:T(8,128)(2,1)S(1)}, bf16[1024,128]{1,0:T(8,128)(2,1)}, u32[]{:S(2)}) %copy-start) | copy-done | bytes 262168
  1.0 0.0 copy-start.2
  1.0 0.9 %copy-done.2 = bf16[1024,64]{0,1:T(8,128)(2,1)S(1)} copy-done((bf16[1024,64]{0,1:T(8,128)(2,1)S(1)}, bf16[1024,64]{0,1:T(8,128)(2,1)}, u32[]{:S(2)}) %copy-start.2) | copy-done | bytes 131096
  1.9 0.0 copy-start.3
  1.9 0.0 copy-start.5
  1.9 0.1 tails.1.own
  1.9 0.0 copy-start.4
  1.9 8.9 %collective-permute-start = (bf16[2,80,128]{2,1,0:T(8,128)(2,1)S(1)}, bf16[2,80,128]{2,1,0:T(8,128)(2,1)S(1)}, u32[]{:S(2)}, u32[]{:S(2)}) collective-permute-start(bf16[2,80,128]{2,1,0:T(8,128)(2,1)S(1)} %tails.1.own), channel_id=1, source_target_pairs={{0,32},{32,0},{1,33},{33,1},{2,34},{34,2},{3,35},{35,3},{4,36},{36... | collective-permute-start | bytes 122888 | tf_op jit(solution)/shard_map/ppermute | solution.py:292
  10.9 1.9 %collective-permute-start.1 = (bf16[2,80,128]{2,1,0:T(8,128)(2,1)S(1)}, bf16[2,80,128]{2,1,0:T(8,128)(2,1)S(1)}, u32[]{:S(2)}, u32[]{:S(2)}) collective-permute-start(bf16[2,80,128]{2,1,0:T(8,128)(2,1)S(1)} %tails.1.own), channel_id=1, source_target_pairs={{32,64},{96,128},{160,192},{224,256},{288,320},{352,384},{416,448}... | collective-permute-start | bytes 122888 | tf_op jit(solution)/shard_map/ppermute | solution.py:322
  12.8 0.0 collective-permute-done.swap
  12.8 3.4 %collective-permute-done.1.hop = bf16[2,80,128]{2,1,0:T(8,128)(2,1)S(1)} collective-permute-done((bf16[2,80,128]{2,1,0:T(8,128)(2,1)S(1)}, bf16[2,80,128]{2,1,0:T(8,128)(2,1)S(1)}, u32[]{:S(2)}, u32[]{:S(2)}) %collective-permute-start.1) | collective-permute-done | bytes 40992 | tf_op jit(solution)/shard_map/ppermute | solution.py:322
  16.2 0.0 copy-done.3
  16.2 0.0 copy-done.5
  16.2 0.3 conv.1.mine
  16.5 1.9 %collective-permute-start.2 = (bf16[64,1024]{1,0:T(8,128)(2,1)S(1)}, bf16[64,1024]{1,0:T(8,128)(2,1)S(1)}, u32[]{:S(2)}, u32[]{:S(2)}) collective-permute-start(bf16[64,1024]{1,0:T(8,128)(2,1)S(1)} %conv.1.mine), channel_id=1, source_target_pairs={{0,1},{1,0},{2,3},{3,2},{4,5},{5,4},{6,7},{7,6},{8,9},{9,8},{10,11... | collective-permute-start | bytes 393224 | tf_op jit(solution)/shard_map/ppermute | solution.py:292
  18.4 0.0 copy-done.4
  18.4 1.1 %pack.1 = bf16[32,64,128]{2,1,0:T(8,128)(2,1)} custom-call(bf16[64,1024]{1,0:T(8,128)(2,1)S(1)} %conv.1.mine, bf16[128,128]{1,0:T(8,128)(2,1)S(1)} %copy-done.4), custom_call_target="tpu_custom_call" | custom-call | flops 16777216 | bytes 1048576 | tf_op jit(solution)/shard_map/pack/pallas_call | solution.py:298
  19.6 5.2 %all-to-all-start = ((bf16[32,64,128]{2,1,0:T(8,128)(2,1)}), bf16[32,64,128]{2,1,0:T(8,128)(2,1)S(1)}, u32[]{:S(2)}, u32[]{:S(2)}) async-start(bf16[32,64,128]{2,1,0:T(8,128)(2,1)} %pack.1), calls=%async_computation | async-start | bytes 1048576 | tf_op jit(solution)/shard_map/all_to_all | solution.py:329
  24.8 0.0 copy-start.1
  24.8 0.0 copy-start.6
  24.8 0.0 collective-permute-done.2.near
  24.9 3.3 %collective-permute-start.3 = (bf16[128,1024]{1,0:T(8,128)(2,1)S(1)}, bf16[128,1024]{1,0:T(8,128)(2,1)S(1)}, u32[]{:S(2)}, u32[]{:S(2)}) collective-permute-start(bf16[128,1024]{1,0:T(8,128)(2,1)S(1)} %join.1), channel_id=1, source_target_pairs={{0,2},{2,0},{1,3},{3,1},{4,6},{6,4},{5,7},{7,5},{8,10},{10,8},{9,1... | collective-permute-start | bytes 786440 | tf_op jit(solution)/shard_map/ppermute | solution.py:292
  28.1 0.0 copy-done.1
  28.2 0.0 copy-done.6
  28.2 0.3 queries.1.q
  28.4 9.9 %collective-permute-done.3.both = bf16[128,1024]{1,0:T(8,128)(2,1)S(1)} collective-permute-done((bf16[128,1024]{1,0:T(8,128)(2,1)S(1)}, bf16[128,1024]{1,0:T(8,128)(2,1)S(1)}, u32[]{:S(2)}, u32[]{:S(2)}) %collective-permute-start.3) | collective-permute-done | bytes 262176 | tf_op jit(solution)/shard_map/ppermute | solution.py:292
  38.4 0.0 all-to-all-done
  38.4 2.5 %collective-permute-start.4 = (bf16[8,4,64,128]{3,2,1,0:T(8,128)(2,1)S(1)}, bf16[8,4,64,128]{3,2,1,0:T(8,128)(2,1)S(1)}, u32[]{:S(2)}, u32[]{:S(2)}) collective-permute-start(bf16[8,4,64,128]{3,2,1,0:T(8,128)(2,1)S(1)} %bitcast.5), channel_id=1, source_target_pairs={{0,32},{32,0},{1,33},{33,1},{2,34},{34,2},{3,35},{35,3},{4,36},{36... | collective-permute-start | bytes 1572872 | tf_op jit(solution)/shard_map/ppermute | solution.py:292
  40.9 2.4 %near.1 = (f32[2,512,128]{2,1,0:T(8,128)S(1)}, f32[2,512,128]{2,1,0:T(8,128)S(1)}, f32[2,512,128]{2,1,0:T(8,128)S(1)}) custom-call(bf16[1024,128]{1,0:T(8,128)(2,1)S(1)} %queries.1.q, bf16[8,4,64,128]{3,2,1,0:T(8,128)(2,1)S(1)} %bitcast.6, bf16[64,1024]{1,0:T(8,128)(2,1)S(1)} %conv.1.mine, bf16[64,1024]{1,0:T(8,128)(2,1)S(1)} %collective-permute-done.2.near, ...), custom_call_target="tpu_custom_call" | custom-call | flops 1073741824 | bytes 1048576 | tf_op jit(solution)/shard_map/near/pallas_call | solution.py:298
  43.4 0.0 collective-permute-done.4.far
  43.4 0.0 copy-start.7
  43.4 0.6 %copy-done.7 = f32[128]{0:T(128)S(1)} copy-done((f32[128]{0:T(128)S(1)}, f32[128]{0:T(128)}, u32[]{:S(2)}) %copy-start.7) | copy-done | bytes 536
  44.0 3.4 %far.1 = bf16[1024,128]{1,0:T(8,128)(2,1)} custom-call(bf16[1024,128]{1,0:T(8,128)(2,1)S(1)} %queries.1.q, bf16[8,4,64,128]{3,2,1,0:T(8,128)(2,1)S(1)} %collective-permute-done.4.far, f32[2,512,128]{2,1,0:T(8,128)S(1)} %get-tuple-element.14.old_tops, f32[2,512,128]{2,1,0:T(8,128)S(1)} %get-tuple-element.15.old_totals, ...), custom_call_target="tpu_custom_call" | custom-call | flops 1073741824 | bytes 1048576 | tf_op jit(solution)/shard_map/far/pallas_call | solution.py:298
  (1 shorter events, 0.0 us)
Async XLA Ops:
  0.0 0.9 %copy-start = (bf16[1024,128]{1,0:T(8,128)(2,1)S(1)}, bf16[1024,128]{1,0:T(8,128)(2,1)}, u32[]{:S(2)}) copy-start(bf16[1024,128]{1,0:T(8,128)(2,1)} %q.3) | copy-start | bytes 786436
  1.0 0.9 %copy-start.2 = (bf16[1024,64]{0,1:T(8,128)(2,1)S(1)}, bf16[1024,64]{0,1:T(8,128)(2,1)}, u32[]{:S(2)}) copy-start(bf16[1024,64]{0,1:T(8,128)(2,1)} %param.7) | copy-start | bytes 393220
  1.9 14.3 %copy-start.3 = (bf16[1024,64]{0,1:T(8,128)(2,1)S(1)}, bf16[1024,64]{0,1:T(8,128)(2,1)}, u32[]{:S(2)}) copy-start(bf16[1024,64]{0,1:T(8,128)(2,1)} %param.7) | copy-start | bytes 393220
  1.9 14.3 %copy-start.5 = (f32[4,64]{1,0:T(4,128)S(1)}, f32[4,64]{1,0:T(4,128)}, u32[]{:S(2)}) copy-start(f32[4,64]{1,0:T(4,128)} %taps.2) | copy-start | bytes 3076
  1.9 16.5 %copy-start.4 = (bf16[128,128]{1,0:T(8,128)(2,1)S(1)}, bf16[128,128]{1,0:T(8,128)(2,1)}, u32[]{:S(2)}) copy-start(bf16[128,128]{1,0:T(8,128)(2,1)} %constant.2.clone.table) | copy-start | bytes 98308
  1.9 10.9 %collective-permute-start = (bf16[2,80,128]{2,1,0:T(8,128)(2,1)S(1)}, bf16[2,80,128]{2,1,0:T(8,128)(2,1)S(1)}, u32[]{:S(2)}, u32[]{:S(2)}) collective-permute-start(bf16[2,80,128]{2,1,0:T(8,128)(2,1)S(1)} %tails.1.own), channel_id=1, source_target_pairs={{0,32},{32,0},{1,33},{33,1},{2,34},{34,2},{3,35},{35,3},{4,36},{36... | collective-permute-start | bytes 122888 | tf_op jit(solution)/shard_map/ppermute | solution.py:292
  10.9 5.3 %collective-permute-start.1 = (bf16[2,80,128]{2,1,0:T(8,128)(2,1)S(1)}, bf16[2,80,128]{2,1,0:T(8,128)(2,1)S(1)}, u32[]{:S(2)}, u32[]{:S(2)}) collective-permute-start(bf16[2,80,128]{2,1,0:T(8,128)(2,1)S(1)} %tails.1.own), channel_id=1, source_target_pairs={{32,64},{96,128},{160,192},{224,256},{288,320},{352,384},{416,448}... | collective-permute-start | bytes 122888 | tf_op jit(solution)/shard_map/ppermute | solution.py:322
  16.5 8.3 %collective-permute-start.2 = (bf16[64,1024]{1,0:T(8,128)(2,1)S(1)}, bf16[64,1024]{1,0:T(8,128)(2,1)S(1)}, u32[]{:S(2)}, u32[]{:S(2)}) collective-permute-start(bf16[64,1024]{1,0:T(8,128)(2,1)S(1)} %conv.1.mine), channel_id=1, source_target_pairs={{0,1},{1,0},{2,3},{3,2},{4,5},{5,4},{6,7},{7,6},{8,9},{9,8},{10,11... | collective-permute-start | bytes 393224 | tf_op jit(solution)/shard_map/ppermute | solution.py:292
  19.6 18.8 %all-to-all-start = ((bf16[32,64,128]{2,1,0:T(8,128)(2,1)}), bf16[32,64,128]{2,1,0:T(8,128)(2,1)S(1)}, u32[]{:S(2)}, u32[]{:S(2)}) async-start(bf16[32,64,128]{2,1,0:T(8,128)(2,1)} %pack.1), calls=%async_computation | async-start | bytes 1048576 | tf_op jit(solution)/shard_map/all_to_all | solution.py:329
  24.8 3.3 %copy-start.1 = (bf16[1024,128]{1,0:T(8,128)(2,1)S(1)}, bf16[1024,128]{1,0:T(8,128)(2,1)}, u32[]{:S(2)}) copy-start(bf16[1024,128]{1,0:T(8,128)(2,1)} %q.3) | copy-start | bytes 786436
  24.8 3.3 %copy-start.6 = (f32[4,128]{1,0:T(4,128)S(1)}, f32[4,128]{1,0:T(4,128)}, u32[]{:S(2)}) copy-start(f32[4,128]{1,0:T(4,128)} %taps.3) | copy-start | bytes 6148
  24.9 13.5 %collective-permute-start.3 = (bf16[128,1024]{1,0:T(8,128)(2,1)S(1)}, bf16[128,1024]{1,0:T(8,128)(2,1)S(1)}, u32[]{:S(2)}, u32[]{:S(2)}) collective-permute-start(bf16[128,1024]{1,0:T(8,128)(2,1)S(1)} %join.1), channel_id=1, source_target_pairs={{0,2},{2,0},{1,3},{3,1},{4,6},{6,4},{5,7},{7,5},{8,10},{10,8},{9,1... | collective-permute-start | bytes 786440 | tf_op jit(solution)/shard_map/ppermute | solution.py:292
  38.4 5.0 %collective-permute-start.4 = (bf16[8,4,64,128]{3,2,1,0:T(8,128)(2,1)S(1)}, bf16[8,4,64,128]{3,2,1,0:T(8,128)(2,1)S(1)}, u32[]{:S(2)}, u32[]{:S(2)}) collective-permute-start(bf16[8,4,64,128]{3,2,1,0:T(8,128)(2,1)S(1)} %bitcast.5), channel_id=1, source_target_pairs={{0,32},{32,0},{1,33},{33,1},{2,34},{34,2},{3,35},{35,3},{4,36},{36... | collective-permute-start | bytes 1572872 | tf_op jit(solution)/shard_map/ppermute | solution.py:292
  43.4 0.7 %copy-start.7 = (f32[128]{0:T(128)S(1)}, f32[128]{0:T(128)}, u32[]{:S(2)}) copy-start(f32[128]{0:T(128)} %param.10) | copy-start | bytes 1540

commit v3 on v2

v3 whole, which is shorter than its diff:
```python
import functools
import math

import jax
import jax.numpy as jnp
import numpy as np
from jax import lax
from jax.experimental import pallas as pl
from jax.experimental.pallas import tpu as pltpu
from jax.sharding import Mesh, PartitionSpec as P

HEAD_CHANNELS = 128
TAPS = 4
BLOCK = 128
KEEP = 16
SPAN = 512
ROWS = 2 * SPAN
NEGATIVE = -1e30
EPSILON = 1e-06
EDGE = 16
SENT = 64 + 2 * EDGE
CHUNK = 256

CTX = ("y_lo", "x", "core")
MP = ("z_hi", "z_lo", "y_hi")
GROUP = ("z_lo", "y_hi")
CHIPS = ("y_lo", "x")

VMEM = pltpu.VMEM
SMEM = pltpu.SMEM
F32 = jnp.float32
BF16 = jnp.bfloat16
NT = (((1,), (1,)), ((), ()))
TN = (((0,), (0,)), ((), ()))


def spec(space=VMEM):
    return pl.BlockSpec(memory_space=space)


def dct_table():
    j = np.arange(KEEP, dtype=np.float32)[:, None]
    u = np.arange(BLOCK, dtype=np.float32)[None, :]
    table = np.cos(np.float32(math.pi) * (u + np.float32(0.5)) * j / np.float32(BLOCK))
    table = table * np.float32(math.sqrt(2.0 / BLOCK))
    table = np.where(j == 0, table * np.float32(math.sqrt(0.5)), table)
    return table.astype(jnp.bfloat16)


def dct_tile():
    return np.tile(dct_table().T, (1, BLOCK // KEEP))


def head_tables():
    table = dct_table()
    whole = np.zeros((16, 8, 2, 8, BLOCK), table.dtype)
    half = BLOCK // 2
    for owner in range(16):
        for t in range(TAPS - 1):
            low, high = (0, half) if owner % 2 == 0 else (half, 0)
            whole[owner, t, 0, owner // 2, low : low + KEEP] = table[:, t]
            whole[owner, 3 + t, 1, owner // 2, high : high + KEEP] = table[:, t]
    return whole.reshape(128, 16 * BLOCK)


def conv_kernel(
    kv_in, taps_in, table_in, conv_result, block_result, kv, taps, table, conv_out, block_out, sems
):
    moves = [(kv_in, kv), (taps_in, taps), (table_in, table)]
    moves += [(conv_out, conv_result), (block_out, block_result)]
    moves = [pltpu.make_async_copy(*move, sems.at[k]) for k, move in enumerate(moves)]
    for move in moves[:3]:
        move.start()
    for move in moves[:3]:
        move.wait()
    lanes = lax.broadcasted_iota(jnp.int32, (64, BLOCK), 1)
    turned = jnp.transpose(
        jnp.concatenate(
            [
                jnp.concatenate([taps[...], jnp.zeros((4, 64), F32)], 0),
                jnp.zeros((8, 64), F32),
            ],
            1,
        )
    )[:64]
    heads, tails = [], []
    for half in range(2):
        values = kv[:, half * SPAN : (half + 1) * SPAN].astype(F32)
        padded = jnp.concatenate([values, jnp.zeros((64, BLOCK), F32)], 1)
        total = turned[:, 0:1] * padded
        for w in range(1, TAPS):
            total = total + turned[:, w : w + 1] * pltpu.roll(padded, w, 1)
        conv_out[:, half * SPAN : (half + 1) * SPAN] = total[:, :SPAN].astype(BF16)
        if half:
            moves[3].start()
        heads.append(total[:, :BLOCK])
        tails.append(total[:, SPAN:])

    def join(pair):
        upper = pltpu.roll(pair[1], 3, 1)
        return jnp.where(lanes < 3, pair[0], jnp.where(lanes < 6, upper, 0.0))

    heads, tails = join(heads), join(tails)
    uneven = lax.axis_index("y_hi") == 1
    edges = jnp.concatenate([jnp.where(uneven, tails, heads), jnp.where(uneven, heads, tails)], 0)
    edges = jnp.transpose(edges)[:8]
    high = edges.astype(BF16)
    low = edges - high.astype(F32)
    edges = jnp.concatenate([high.astype(F32), low], 0).astype(BF16)
    packed = jnp.zeros((64, BLOCK), F32)
    for b in range(ROWS // BLOCK):
        part = conv_out[:, b * BLOCK : (b + 1) * BLOCK]
        if b * BLOCK % SPAN == 0:
            part = jnp.where(lanes < TAPS - 1, 0.0, part.astype(F32)).astype(BF16)
        part = jnp.dot(part, table[...], preferred_element_type=F32)
        packed = jnp.where(lanes // KEEP == b, part, packed)
    packed = jnp.where(lax.axis_index("core") == 1, pltpu.roll(packed, BLOCK // 2, 1), packed)
    high = packed.astype(BF16)
    low = jnp.where(lanes % (BLOCK // 2) < KEEP, packed - high.astype(F32), 0.0)
    rest = low[:EDGE]
    for g in range(1, 4):
        rest = rest + pltpu.roll(low[g * EDGE : (g + 1) * EDGE], g * KEEP, 1)
    rest = rest.astype(BF16)
    for k in range(block_out.shape[0]):
        block_out[k, :64] = high
        block_out[k, 64 : 64 + EDGE] = edges
        block_out[k, 64 + EDGE :] = rest
    moves[4].start()
    moves[3].wait()
    moves[4].wait()


def join_kernel(mine, near, out):
    out[:64] = mine[...]
    out[64:] = near[...]


def query_kernel(q, own, swap, hop, taps, out):
    place = lax.axis_index(CTX)
    odd = place % 2 == 1
    own, swap, hop = own[...].astype(F32), swap[...].astype(F32), hop[...].astype(F32)
    lower = jnp.where(odd, swap[0], hop[0])
    lower = jnp.where(place == 0, jnp.zeros_like(lower), lower)
    upper = jnp.where(odd, hop[1], swap[1])
    upper = jnp.where(place == 15, own[0], upper)
    for half, halo in enumerate((lower, upper)):
        for b in range(SPAN // BLOCK):
            start = half * SPAN + b * BLOCK
            values = q[start : start + BLOCK].astype(F32)
            if b:
                halo = q[start - EDGE : start].astype(F32)
            padded = jnp.concatenate([halo, values], 0)
            total = taps[0:1] * values
            for w in range(1, TAPS):
                total = total + taps[w : w + 1] * pltpu.roll(padded, w, 0)[EDGE:]
            out[start : start + BLOCK] = total.astype(BF16)


def pairs_kernel(mine, near, far, pairs):
    member = lax.axis_index(GROUP)
    pairs[member] = mine[...]
    pairs[member ^ 1] = near[...]
    pairs[member ^ 2] = far[:64]
    pairs[member ^ 3] = far[64:]


def attend_kernel(q, pairs, far_own, far_other, table, gain, out, packed, scores, ends):
    place = lax.axis_index(CTX)
    middle = place // 2
    odd = place % 2 == 1
    factor = math.log2(math.e) / math.sqrt(HEAD_CHANNELS)
    lane = lax.broadcasted_iota(jnp.int32, (BLOCK, BLOCK), 1)
    row = lax.broadcasted_iota(jnp.int32, (BLOCK, BLOCK), 0)
    edge_lane = lax.broadcasted_iota(jnp.int32, (8, BLOCK), 1) < BLOCK // 2
    edge_row = lax.broadcasted_iota(jnp.int32, (8, BLOCK), 0)
    tile_lane = lax.broadcasted_iota(jnp.int32, (64, BLOCK), 1)
    own_lane = jnp.where(tile_lane < BLOCK // 2, 1, 0) != jnp.where(odd, 1, 0)
    first_lane = lax.broadcasted_iota(jnp.int32, (EDGE, BLOCK), 1) % (BLOCK // 2) < KEEP

    def turned(value):
        return pltpu.roll(value, BLOCK // 2, 1)

    def edges_of(owner, m):
        mine = far_own[owner // 2, m, 64 : 64 + EDGE]
        other = far_other[owner // 2, m, 64 : 64 + EDGE]
        tile = jnp.where(odd, other, mine) if owner % 2 == 0 else jnp.where(odd, mine, other)
        tile = tile.astype(F32)
        return tile[:8] + tile[8:]

    def whole_tile(ref, i, m):
        rest = ref[i, m, 64 + EDGE :].astype(F32)
        parts = [rest] + [pltpu.roll(rest, BLOCK - g * KEEP, 1) for g in range(1, 4)]
        parts = [jnp.where(first_lane, part, 0.0) for part in parts]
        return ref[i, m, :64].astype(F32) + jnp.concatenate(parts, 0)

    first_rows = []
    for kind in range(2):
        heads, tails = [], []
        for owner in range(16):
            left, right = edges_of(owner, 2 * kind), edges_of(owner, 2 * kind + 1)
            heads.append(jnp.where(edge_lane, left, right))
            tails.append(turned(jnp.where(edge_lane, right, left)))
        for owner in range(16):
            below = tails[owner - 1] if owner else jnp.zeros((8, BLOCK), F32)
            above = tails[owner + 1] if owner < 15 else pltpu.roll(tails[15], 3, 0)
            ends[kind, owner] = heads[owner] + jnp.where(edge_row < 3, below, above)
        both = jnp.transpose(ends[kind].reshape(128, HEAD_CHANNELS)).astype(BF16)
        fix = jnp.dot(both, table[...], preferred_element_type=F32)
        for i in range(8):
            for m in range(2):
                rows = slice(64 * m, 64 * (m + 1))
                mine = whole_tile(far_own, i, 2 * kind + m)
                other = whole_tile(far_other, i, 2 * kind + m)
                low = jnp.where(own_lane, mine, other) + fix[rows, i * BLOCK : (i + 1) * BLOCK]
                high = jnp.where(own_lane, other, mine)
                high = high + fix[rows, (8 + i) * BLOCK : (9 + i) * BLOCK]
                packed[kind, 0, i, rows] = low.astype(BF16)
                packed[kind, 1, i, rows] = high.astype(BF16)
        pick = (
            (edge_row < 3)
            & (lax.broadcasted_iota(jnp.int32, (8, BLOCK), 1) == edge_row)
        ) | (
            (edge_row >= 3)
            & (edge_row < 6)
            & (lax.broadcasted_iota(jnp.int32, (8, BLOCK), 1) == edge_row - 3 + BLOCK // 2)
        )
        first_rows.append(
            lax.dot_general(
                ends[kind, place].astype(BF16),
                jnp.where(pick, 1.0, 0.0).astype(BF16),
                TN,
                preferred_element_type=F32,
            )
        )

    def near_tile(kind, start):
        tile = jnp.concatenate(
            [pairs[2 * kind, :, start : start + BLOCK], pairs[2 * kind + 1, :, start : start + BLOCK]], 0
        )
        if start % SPAN == 0:
            first = first_rows[kind] if start == 0 else turned(first_rows[kind])
            tile = jnp.where(lane < TAPS - 1, first, tile.astype(F32)).astype(BF16)
        return tile

    key_block = (lax.broadcasted_iota(jnp.int32, (1, BLOCK), 1) % (BLOCK // 2)) // KEEP
    left_lanes = lax.broadcasted_iota(jnp.int32, (1, BLOCK), 1) < BLOCK // 2
    per_chunk = CHUNK // BLOCK
    for r in range(SPAN // CHUNK):
        tops = [jnp.full((CHUNK, BLOCK), NEGATIVE, F32) for _ in range(2)]
        for half in range(2):
            tiles = []
            for c in range(per_chunk):
                start = half * SPAN + r * CHUNK + c * BLOCK
                near = jnp.dot(
                    q[start : start + BLOCK], near_tile(0, start), preferred_element_type=F32
                )
                tiles.append(jnp.where(row >= lane, near, NEGATIVE))
            tops[half] = jnp.concatenate(tiles, 0)
            scores[17 + half] = tops[half]
        upper = q[SPAN + r * CHUNK : SPAN + (r + 1) * CHUNK]
        for i in range(4):
            far = jnp.dot(
                upper,
                jnp.concatenate([packed[0, 0, 2 * i], packed[0, 0, 2 * i + 1]], 1),
                preferred_element_type=F32,
            )
            scores[9 + 2 * i] = far[:, :BLOCK]
            scores[10 + 2 * i] = far[:, BLOCK:]
            tops[1] = jnp.maximum(tops[1], jnp.maximum(far[:, :BLOCK], far[:, BLOCK:]))
        for j in range(9):
            high = j > middle
            side = high.astype(jnp.int32)
            partial = (j == middle) | (j == middle + 1)
            start = pl.multiple_of(side * SPAN + r * CHUNK, CHUNK)
            far = jnp.dot(
                q[pl.ds(start, CHUNK)], packed[0, side, j - side], preferred_element_type=F32
            )
            biases = []
            for c in range(per_chunk):
                block = r * per_chunk + c
                left = jnp.where(high, jnp.where(odd, block, 4), jnp.where(odd, 4, block))
                right = jnp.where(high, jnp.where(odd, 0, block), jnp.where(odd, block, 0))
                left, right = jnp.where(partial, left, 4), jnp.where(partial, right, 4)
                seen = key_block < jnp.where(left_lanes, left, right)
                biases.append(
                    jnp.broadcast_to(jnp.where(seen, 0.0, NEGATIVE), (BLOCK, BLOCK))
                )
            far = far + jnp.concatenate(biases, 0)
            scores[j] = far
            tops[0] = jnp.maximum(tops[0], jnp.where(high, NEGATIVE, far))
            tops[1] = jnp.maximum(tops[1], jnp.where(high, far, NEGATIVE))
        tops = [
            jnp.broadcast_to(jnp.max(t, 1, keepdims=True) * factor, (CHUNK, BLOCK)) for t in tops
        ]
        totals, sums = [], []
        for half in range(2):
            weights = jnp.exp2(scores[17 + half] * factor - tops[half])
            totals.append(weights)
            weights = weights.astype(BF16)
            sums.append(
                jnp.concatenate(
                    [
                        lax.dot_general(
                            weights[c * BLOCK : (c + 1) * BLOCK],
                            near_tile(1, half * SPAN + r * CHUNK + c * BLOCK),
                            NT,
                            preferred_element_type=F32,
                        )
                        for c in range(per_chunk)
                    ],
                    0,
                )
            )
        for i in range(4):
            first = jnp.exp2(scores[9 + 2 * i] * factor - tops[1])
            second = jnp.exp2(scores[10 + 2 * i] * factor - tops[1])
            totals[1] = totals[1] + first + second
            sums[1] = sums[1] + lax.dot_general(
                jnp.concatenate([first, second], 1).astype(BF16),
                jnp.concatenate([packed[1, 0, 2 * i], packed[1, 0, 2 * i + 1]], 1),
                NT,
                preferred_element_type=F32,
            )
        for j in range(9):
            high = j > middle
            side = high.astype(jnp.int32)
            weights = jnp.exp2(scores[j] * factor - jnp.where(high, tops[1], tops[0]))
            totals[0] = totals[0] + jnp.where(high, 0.0, weights)
            totals[1] = totals[1] + jnp.where(high, weights, 0.0)
            part = lax.dot_general(
                weights.astype(BF16), packed[1, side, j - side], NT, preferred_element_type=F32
            )
            sums[0] = sums[0] + jnp.where(high, 0.0, part)
            sums[1] = sums[1] + jnp.where(high, part, 0.0)
        for half in range(2):
            attended = sums[half] / jnp.sum(totals[half], 1, keepdims=True)
            mean = jnp.mean(attended * attended, 1, keepdims=True)
            normed = attended * lax.rsqrt(mean + EPSILON)
            start = half * SPAN + r * CHUNK
            out[start : start + CHUNK] = (normed * gain[...]).astype(BF16)


def cost(flops, moved):
    return pl.CostEstimate(flops=flops, bytes_accessed=moved, transcendentals=0)


def swapped(value, axis):
    return lax.ppermute(value, axis, [(0, 1), (1, 0)])


def per_device(queries, keys_values, query_taps, pair_taps, out_gain):
    def call(kernel, name, out_shape, operands, spaces=None, scratch=(), flops=1 << 24):
        many = isinstance(out_shape, tuple)
        return pl.pallas_call(
            kernel,
            out_shape=out_shape,
            in_specs=[spec(s) for s in spaces] if spaces else [spec()] * len(operands),
            out_specs=(spec(),) * len(out_shape) if many else spec(),
            scratch_shapes=scratch,
            compiler_params=pltpu.CompilerParams(vmem_limit_bytes=24 << 20),
            cost_estimate=cost(flops, 1 << 20),
            name=name,
        )(*operands)

    def shape(*dims):
        return jax.ShapeDtypeStruct(dims, BF16)

    conv, blocks = pl.pallas_call(
        conv_kernel,
        out_shape=(shape(64, ROWS), shape(32, SENT, BLOCK)),
        in_specs=[spec(pl.ANY)] * 3,
        out_specs=(spec(pl.ANY), spec(pl.ANY)),
        scratch_shapes=[
            VMEM((64, ROWS), BF16),
            VMEM((TAPS, 64), F32),
            VMEM((BLOCK, BLOCK), BF16),
            VMEM((64, ROWS), BF16),
            VMEM((32, SENT, BLOCK), BF16),
            pltpu.SemaphoreType.DMA((5,)),
        ],
        compiler_params=pltpu.CompilerParams(vmem_limit_bytes=56 << 20),
        cost_estimate=cost(1 << 24, 1 << 20),
        name="conv",
    )(keys_values.T, pair_taps, jnp.asarray(dct_tile()))
    gathered = lax.all_to_all(blocks, CHIPS + GROUP, 0, 0, tiled=True)
    near = swapped(conv, "y_hi")
    far = call(join_kernel, "join", shape(128, ROWS), (conv, near), flops=1 << 37)
    far = swapped(far, "z_lo")
    tails = jnp.stack([queries[e - EDGE : e] for e in (SPAN, ROWS)])
    swap = swapped(tails, "core")
    hop = lax.ppermute(
        tails, CTX, [(i, i + 1) for i in range(1, 15, 2)] + [(i + 1, i) for i in range(1, 15, 2)]
    )
    query_conv = call(
        query_kernel,
        "queries",
        shape(ROWS, HEAD_CHANNELS),
        (queries, tails, swap, hop, query_taps),
    )
    gathered, query_conv, far = lax.optimization_barrier((gathered, query_conv, far))
    far_own = gathered.reshape(8, 4, SENT, BLOCK)
    far_other = swapped(far_own, "core")
    pairs = call(pairs_kernel, "pairs", shape(4, 64, ROWS), (conv, near, far))
    return call(
        attend_kernel,
        "attend",
        shape(ROWS, HEAD_CHANNELS),
        (query_conv, pairs, far_own, far_other, jnp.asarray(head_tables()), out_gain.reshape(1, -1)),
        scratch=[
            VMEM((2, 2, 8, HEAD_CHANNELS, BLOCK), BF16),
            VMEM((19, CHUNK, BLOCK), F32),
            VMEM((2, 16, 8, HEAD_CHANNELS), F32),
        ],
        flops=1 << 30,
    )


def solution(mesh):
    fine = Mesh(mesh.devices.reshape(2, 4, 2, 8, 2, 2), CTX + MP)
    in_specs = (P(CTX, MP), P(CTX, MP), P(None, MP), P(None, MP), P(MP))
    return jax.shard_map(
        per_device, mesh=fine, in_specs=in_specs, out_specs=P(CTX, MP), check_vma=False
    )
```

time: 47.8 us -> 42.1 us (0.88)
  waiting for transfers between devices: 13.3 us -> 4.67 us
  starting transfers between devices: 23.8 us -> 29.6 us
  local copies, waits for them, and re-layouts: 2.53 us -> 0.03 us
    ppermute x4, waiting for transfers between devices: 9.94 us -> 4.67 us  [swapped(): return lax.ppermute(value, axis, [(0, 1), (1, 0)])]
    ppermute x1, starting transfers between devices: 1.92 us -> 5.61 us  [per_device(): lax.ppermute(tails, CTX, [(i, i + 1) for i in range(1, 15, 2)] + [(i + 1,...]
    ppermute x1, waiting for transfers between devices: 3.38 us -> 0.01 us  [per_device(): lax.ppermute(tails, CTX, [(i, i + 1) for i in range(1, 15, 2)] + [(i + 1,...]
    pallas_call x7 -> x4, Pallas kernels: 7.64 us -> 4.77 us  [call(): pl.pallas_call(kernel, out_shape=out_shape, in_specs=[spec(s) for s in sp...]
    unnamed x16 -> x10, local copies, waits for them, and re-layouts: 2.53 us -> 0.03 us
    pallas_call x0 -> x1, Pallas kernels: none -> 2.46 us  [per_device(): pl.pallas_call(conv_kernel, out_shape=(shape(64, ROWS), shape(32, SENT, B...]
    all_to_all x1, starting transfers between devices: 5.23 us -> 6.4 us  [per_device(): gathered = lax.all_to_all(blocks, CHIPS + GROUP, 0, 0, tiled=True)]
    ppermute x4, starting transfers between devices: 16.7 us -> 17.6 us  [swapped(): return lax.ppermute(value, axis, [(0, 1), (1, 0)])]
  transfers between devices with their start and end apart: 6 -> 6, of which waited for: 2 -> 3; matrix products, arithmetic and copies ran while one was open for 0% -> 0% of each run, Pallas kernels for 8% -> 1%
where the time goes in v3:
time: 42.1 us; the launch traced here: 41.7 us
  starting transfers between devices  29.6 us (70%)
  Pallas kernels  7.23 us (17%)
  waiting for transfers between devices  4.67 us (11%)
    ppermute x4, starting transfers between devices, swapped(): return lax.ppermute(value, axis, [(0, 1), (1, 0)])  17.6 us
    all_to_all x1, starting transfers between devices, per_device(): gathered = lax.all_to_all(blocks, CHIPS + GROUP, 0, 0, tiled=True)  6.4 us
    ppermute x1, starting transfers between devices, per_device(): lax.ppermute(tails, CTX, [(i, i + 1) for i in range(1, 15, 2)] + [(i + 1,...  5.61 us
    pallas_call x4, Pallas kernels, call(): pl.pallas_call(kernel, out_shape=out_shape, in_specs=[spec(s) for s in sp...  4.77 us
    ppermute x4, waiting for transfers between devices, swapped(): return lax.ppermute(value, axis, [(0, 1), (1, 0)])  4.67 us
    pallas_call x1, Pallas kernels, per_device(): pl.pallas_call(conv_kernel, out_shape=(shape(64, ROWS), shape(32, SENT, B...  2.46 us
  transfers between devices with their start and end apart: 6, of which 3 were waited for; matrix products, arithmetic and copies ran while one was open for 0% of the time, Pallas kernels for 1%

profile of v3, /device:TPU:1, one launch (start us, length us, event | category | flops | bytes accessed | tf_op | source)
XLA Modules:
  0.0 41.7 jit_solution(11543664090146427224)
XLA Ops:
  0.0 2.5 %conv.1 = (bf16[64,1024]{1,0:T(8,128)(2,1)}, bf16[32,96,128]{2,1,0:T(8,128)(2,1)}) custom-call(bf16[64,1024]{1,0:T(8,128)(2,1)} %bitcast.10, f32[4,64]{1,0:T(4,128)} %taps_in.1, bf16[128,128]{1,0:T(8,128)(2,1)} %constant.4.clone.table_in), custom_call_target="tpu_custom_call" | custom-call | flops 16777216 | bytes 1048576 | tf_op jit(solution)/shard_map/conv/pallas_call | solution.py:368
  2.5 5.7 %collective-permute-start.2 = (bf16[64,1024]{1,0:T(8,128)(2,1)}, bf16[64,1024]{1,0:T(8,128)(2,1)S(1)}, u32[]{:S(2)}, u32[]{:S(2)}) collective-permute-start(bf16[64,1024]{1,0:T(8,128)(2,1)} %get-tuple-element.11.mine), channel_id=1, source_target_pairs={{0,1},{1,0},{2,3},{3,2},{4,5},{5,4},{6,7},{7,6},{8,9},{9,8},{10,11... | collective-permute-start | bytes 393224 | tf_op jit(solution)/shard_map/ppermute | solution.py:348
  8.1 0.0 copy-start.1
  8.1 6.4 %all-to-all-start = ((bf16[32,96,128]{2,1,0:T(8,128)(2,1)}), bf16[32,96,128]{2,1,0:T(8,128)(2,1)S(1)}, u32[]{:S(2)}, u32[]{:S(2)}) async-start(bf16[32,96,128]{2,1,0:T(8,128)(2,1)} %get-tuple-element.10), calls=%async_computation | async-start | bytes 1572864 | tf_op jit(solution)/shard_map/all_to_all | solution.py:385
  14.5 0.0 copy-start
  14.6 0.0 collective-permute-done.2.near
  14.6 0.0 copy-done.1
  14.6 3.3 %collective-permute-start.3 = (bf16[128,1024]{1,0:T(8,128)(2,1)S(1)}, bf16[128,1024]{1,0:T(8,128)(2,1)S(1)}, u32[]{:S(2)}, u32[]{:S(2)}) collective-permute-start(bf16[128,1024]{1,0:T(8,128)(2,1)S(1)} %join.1), channel_id=1, source_target_pairs={{0,2},{2,0},{1,3},{3,1},{4,6},{6,4},{5,7},{7,5},{8,10},{10,8},{9,1... | collective-permute-start | bytes 786440 | tf_op jit(solution)/shard_map/ppermute | solution.py:348
  17.9 0.0 copy-done
  17.9 0.0 copy-start.2
  17.9 5.6 %collective-permute-start.1 = (bf16[2,16,128]{2,1,0:T(8,128)(2,1)S(1)}, bf16[2,16,128]{2,1,0:T(8,128)(2,1)S(1)}, u32[]{:S(2)}, u32[]{:S(2)}) collective-permute-start(bf16[2,16,128]{2,1,0:T(8,128)(2,1)S(1)} %pad_maximum_fusion.own), channel_id=1, source_target_pairs={{32,64},{96,128},{160,192},{224,256},{288,320},{352,384},{416,448}... | collective-permute-start | bytes 24584 | tf_op jit(solution)/shard_map/ppermute | solution.py:391
  23.6 1.9 %collective-permute-start = (bf16[2,16,128]{2,1,0:T(8,128)(2,1)S(1)}, bf16[2,16,128]{2,1,0:T(8,128)(2,1)S(1)}, u32[]{:S(2)}, u32[]{:S(2)}) collective-permute-start(bf16[2,16,128]{2,1,0:T(8,128)(2,1)S(1)} %pad_maximum_fusion.own), channel_id=1, source_target_pairs={{0,32},{32,0},{1,33},{33,1},{2,34},{34,2},{3,35},{35,3},{4,36},{36... | collective-permute-start | bytes 24584 | tf_op jit(solution)/shard_map/ppermute | solution.py:348
  25.5 0.0 collective-permute-done.1.hop
  25.5 1.1 %collective-permute-done.swap = bf16[2,16,128]{2,1,0:T(8,128)(2,1)S(1)} collective-permute-done((bf16[2,16,128]{2,1,0:T(8,128)(2,1)S(1)}, bf16[2,16,128]{2,1,0:T(8,128)(2,1)S(1)}, u32[]{:S(2)}, u32[]{:S(2)}) %collective-permute-start) | collective-permute-done | bytes 8224 | tf_op jit(solution)/shard_map/ppermute | solution.py:348
  26.6 0.0 copy-done.2
  26.6 0.3 queries.1.q
  26.9 1.7 %collective-permute-done.3.far = bf16[128,1024]{1,0:T(8,128)(2,1)S(1)} collective-permute-done((bf16[128,1024]{1,0:T(8,128)(2,1)S(1)}, bf16[128,1024]{1,0:T(8,128)(2,1)S(1)}, u32[]{:S(2)}, u32[]{:S(2)}) %collective-permute-start.3) | collective-permute-done | bytes 262176 | tf_op jit(solution)/shard_map/ppermute | solution.py:348
  28.6 0.0 all-to-all-done
  28.6 0.0 copy-start.4
  28.6 6.8 %collective-permute-start.4 = (bf16[8,4,96,128]{3,2,1,0:T(8,128)(2,1)S(1)}, bf16[8,4,96,128]{3,2,1,0:T(8,128)(2,1)S(1)}, u32[]{:S(2)}, u32[]{:S(2)}) collective-permute-start(bf16[8,4,96,128]{3,2,1,0:T(8,128)(2,1)S(1)} %bitcast.7), channel_id=1, source_target_pairs={{0,32},{32,0},{1,33},{33,1},{2,34},{34,2},{3,35},{35,3},{4,36},{36... | collective-permute-start | bytes 2359304 | tf_op jit(solution)/shard_map/ppermute | solution.py:348
  35.4 0.1 pairs.1
  35.4 0.0 copy-start.3
  35.5 1.8 %collective-permute-done.4.far_other = bf16[8,4,96,128]{3,2,1,0:T(8,128)(2,1)S(1)} collective-permute-done((bf16[8,4,96,128]{3,2,1,0:T(8,128)(2,1)S(1)}, bf16[8,4,96,128]{3,2,1,0:T(8,128)(2,1)S(1)}, u32[]{:S(2)}, u32[]{:S(2)}) %collective-permute-start.4) | collective-permute-done | bytes 786464 | tf_op jit(solution)/shard_map/ppermute | solution.py:348
  37.3 0.0 copy-done.4
  37.3 0.0 copy-done.3
  37.3 4.4 %attend.1 = bf16[1024,128]{1,0:T(8,128)(2,1)} custom-call(bf16[1024,128]{1,0:T(8,128)(2,1)S(1)} %queries.1.q, bf16[4,64,1024]{2,1,0:T(8,128)(2,1)S(1)} %pairs.1, bf16[8,4,96,128]{3,2,1,0:T(8,128)(2,1)S(1)} %bitcast.8, bf16[8,4,96,128]{3,2,1,0:T(8,128)(2,1)S(1)} %collective-permute-done.4.far_other, bf16[128,2048]{1,0:T(8,128)(2,1)S(1)} %copy-done.4, ...), custom_call_target="tpu_custom_call" | custom-call | flops 1073741824 | bytes 1048576 | tf_op jit(solution)/shard_map/attend/pallas_call | solution.py:354
  (3 shorter events, 0.0 us)
Async XLA Ops:
  2.5 12.1 %collective-permute-start.2 = (bf16[64,1024]{1,0:T(8,128)(2,1)}, bf16[64,1024]{1,0:T(8,128)(2,1)S(1)}, u32[]{:S(2)}, u32[]{:S(2)}) collective-permute-start(bf16[64,1024]{1,0:T(8,128)(2,1)} %get-tuple-element.11.mine), channel_id=1, source_target_pairs={{0,1},{1,0},{2,3},{3,2},{4,5},{5,4},{6,7},{7,6},{8,9},{9,8},{10,11... | collective-permute-start | bytes 393224 | tf_op jit(solution)/shard_map/ppermute | solution.py:348
  8.1 6.4 %copy-start.1 = (bf16[64,1024]{1,0:T(8,128)(2,1)S(1)}, bf16[64,1024]{1,0:T(8,128)(2,1)}, u32[]{:S(2)}) copy-start(bf16[64,1024]{1,0:T(8,128)(2,1)} %get-tuple-element.11.mine) | copy-start | bytes 393220
  8.1 20.5 %all-to-all-start = ((bf16[32,96,128]{2,1,0:T(8,128)(2,1)}), bf16[32,96,128]{2,1,0:T(8,128)(2,1)S(1)}, u32[]{:S(2)}, u32[]{:S(2)}) async-start(bf16[32,96,128]{2,1,0:T(8,128)(2,1)} %get-tuple-element.10), calls=%async_computation | async-start | bytes 1572864 | tf_op jit(solution)/shard_map/all_to_all | solution.py:385
  14.5 3.3 %copy-start = (bf16[1024,128]{1,0:T(8,128)(2,1)S(1)}, bf16[1024,128]{1,0:T(8,128)(2,1)}, u32[]{:S(2)}) copy-start(bf16[1024,128]{1,0:T(8,128)(2,1)} %q.1) | copy-start | bytes 786436
  14.6 14.0 %collective-permute-start.3 = (bf16[128,1024]{1,0:T(8,128)(2,1)S(1)}, bf16[128,1024]{1,0:T(8,128)(2,1)S(1)}, u32[]{:S(2)}, u32[]{:S(2)}) collective-permute-start(bf16[128,1024]{1,0:T(8,128)(2,1)S(1)} %join.1), channel_id=1, source_target_pairs={{0,2},{2,0},{1,3},{3,1},{4,6},{6,4},{5,7},{7,5},{8,10},{10,8},{9,1... | collective-permute-start | bytes 786440 | tf_op jit(solution)/shard_map/ppermute | solution.py:348
  17.9 8.7 %copy-start.2 = (f32[4,128]{1,0:T(4,128)S(1)}, f32[4,128]{1,0:T(4,128)}, u32[]{:S(2)}) copy-start(f32[4,128]{1,0:T(4,128)} %taps.1) | copy-start | bytes 6148
  17.9 7.6 %collective-permute-start.1 = (bf16[2,16,128]{2,1,0:T(8,128)(2,1)S(1)}, bf16[2,16,128]{2,1,0:T(8,128)(2,1)S(1)}, u32[]{:S(2)}, u32[]{:S(2)}) collective-permute-start(bf16[2,16,128]{2,1,0:T(8,128)(2,1)S(1)} %pad_maximum_fusion.own), channel_id=1, source_target_pairs={{32,64},{96,128},{160,192},{224,256},{288,320},{352,384},{416,448}... | collective-permute-start | bytes 24584 | tf_op jit(solution)/shard_map/ppermute | solution.py:391
  23.6 3.1 %collective-permute-start = (bf16[2,16,128]{2,1,0:T(8,128)(2,1)S(1)}, bf16[2,16,128]{2,1,0:T(8,128)(2,1)S(1)}, u32[]{:S(2)}, u32[]{:S(2)}) collective-permute-start(bf16[2,16,128]{2,1,0:T(8,128)(2,1)S(1)} %pad_maximum_fusion.own), channel_id=1, source_target_pairs={{0,32},{32,0},{1,33},{33,1},{2,34},{34,2},{3,35},{35,3},{4,36},{36... | collective-permute-start | bytes 24584 | tf_op jit(solution)/shard_map/ppermute | solution.py:348
  28.6 8.7 %copy-start.4 = (bf16[128,2048]{1,0:T(8,128)(2,1)S(1)}, bf16[128,2048]{1,0:T(8,128)(2,1)}, u32[]{:S(2)}) copy-start(bf16[128,2048]{1,0:T(8,128)(2,1)} %constant.5.clone.table) | copy-start | bytes 1572868
  28.6 8.7 %collective-permute-start.4 = (bf16[8,4,96,128]{3,2,1,0:T(8,128)(2,1)S(1)}, bf16[8,4,96,128]{3,2,1,0:T(8,128)(2,1)S(1)}, u32[]{:S(2)}, u32[]{:S(2)}) collective-permute-start(bf16[8,4,96,128]{3,2,1,0:T(8,128)(2,1)S(1)} %bitcast.7), channel_id=1, source_target_pairs={{0,32},{32,0},{1,33},{33,1},{2,34},{34,2},{3,35},{35,3},{4,36},{36... | collective-permute-start | bytes 2359304 | tf_op jit(solution)/shard_map/ppermute | solution.py:348
  35.4 1.8 %copy-start.3 = (f32[128]{0:T(128)S(1)}, f32[128]{0:T(128)}, u32[]{:S(2)}) copy-start(f32[128]{0:T(128)} %param.11) | copy-start | bytes 1540

commit v4 on v3

--- a/solution.py
+++ b/solution.py
@@ -397,10 +397,10 @@
         shape(ROWS, HEAD_CHANNELS),
         (queries, tails, swap, hop, query_taps),
     )
-    gathered, query_conv, far = lax.optimization_barrier((gathered, query_conv, far))
+    gathered, query_conv = lax.optimization_barrier((gathered, query_conv))
     far_own = gathered.reshape(8, 4, SENT, BLOCK)
     far_other = swapped(far_own, "core")
-    pairs = call(pairs_kernel, "pairs", shape(4, 64, ROWS), (conv, near, far))
+    pairs = call(pairs_kernel, "pairs", shape(4, 64, ROWS), (conv, near, far), flops=1 << 37)
     return call(
         attend_kernel,
         "attend",

time: 42.1 us -> 42.1 us (level)
  starting transfers between devices: 29.6 us -> 30.5 us
  waiting for transfers between devices: 4.67 us -> 3.8 us
    ppermute x4, waiting for transfers between devices: 4.67 us -> 2.94 us  [swapped(): return lax.ppermute(value, axis, [(0, 1), (1, 0)])]
    ppermute x4, starting transfers between devices: 17.6 us -> 18.5 us  [swapped(): return lax.ppermute(value, axis, [(0, 1), (1, 0)])]
    all_to_all x1, waiting for transfers between devices: 0.01 us -> 0.85 us  [per_device(): gathered = lax.all_to_all(blocks, CHIPS + GROUP, 0, 0, tiled=True)]
where the time goes in v4:
time: 42.1 us; the launch traced here: 41.7 us
  starting transfers between devices  30.5 us (72%)
  Pallas kernels  7.23 us (17%)
  waiting for transfers between devices  3.8 us (9%)
    ppermute x4, starting transfers between devices, swapped(): return lax.ppermute(value, axis, [(0, 1), (1, 0)])  18.5 us
    all_to_all x1, starting transfers between devices, per_device(): gathered = lax.all_to_all(blocks, CHIPS + GROUP, 0, 0, tiled=True)  6.4 us
    ppermute x1, starting transfers between devices, per_device(): lax.ppermute(tails, CTX, [(i, i + 1) for i in range(1, 15, 2)] + [(i + 1,...  5.61 us
    pallas_call x4, Pallas kernels, call(): pl.pallas_call(kernel, out_shape=out_shape, in_specs=[spec(s) for s in sp...  4.77 us
    ppermute x4, waiting for transfers between devices, swapped(): return lax.ppermute(value, axis, [(0, 1), (1, 0)])  2.94 us
    pallas_call x1, Pallas kernels, per_device(): pl.pallas_call(conv_kernel, out_shape=(shape(64, ROWS), shape(32, SENT, B...  2.46 us
    all_to_all x1, waiting for transfers between devices, per_device(): gathered = lax.all_to_all(blocks, CHIPS + GROUP, 0, 0, tiled=True)  0.85 us
  transfers between devices with their start and end apart: 6, of which 3 were waited for; matrix products, arithmetic and copies ran while one was open for 0% of the time, Pallas kernels for 1%

profile of v4, /device:TPU:1, one launch (start us, length us, event | category | flops | bytes accessed | tf_op | source)
XLA Modules:
  0.0 41.7 jit_solution(13581888205466230995)
XLA Ops:
  0.0 2.5 %conv.1 = (bf16[64,1024]{1,0:T(8,128)(2,1)}, bf16[32,96,128]{2,1,0:T(8,128)(2,1)}) custom-call(bf16[64,1024]{1,0:T(8,128)(2,1)} %bitcast.10, f32[4,64]{1,0:T(4,128)} %taps_in.1, bf16[128,128]{1,0:T(8,128)(2,1)} %constant.4.clone.table_in), custom_call_target="tpu_custom_call" | custom-call | flops 16777216 | bytes 1048576 | tf_op jit(solution)/shard_map/conv/pallas_call | solution.py:368
  2.5 5.7 %collective-permute-start.2 = (bf16[64,1024]{1,0:T(8,128)(2,1)}, bf16[64,1024]{1,0:T(8,128)(2,1)S(1)}, u32[]{:S(2)}, u32[]{:S(2)}) collective-permute-start(bf16[64,1024]{1,0:T(8,128)(2,1)} %get-tuple-element.11.mine), channel_id=1, source_target_pairs={{0,1},{1,0},{2,3},{3,2},{4,5},{5,4},{6,7},{7,6},{8,9},{9,8},{10,11... | collective-permute-start | bytes 393224 | tf_op jit(solution)/shard_map/ppermute | solution.py:348
  8.1 0.0 copy-start.2
  8.1 6.4 %all-to-all-start = ((bf16[32,96,128]{2,1,0:T(8,128)(2,1)}), bf16[32,96,128]{2,1,0:T(8,128)(2,1)S(1)}, u32[]{:S(2)}, u32[]{:S(2)}) async-start(bf16[32,96,128]{2,1,0:T(8,128)(2,1)} %get-tuple-element.9), calls=%async_computation | async-start | bytes 1572864 | tf_op jit(solution)/shard_map/all_to_all | solution.py:385
  14.5 0.0 copy-start
  14.6 0.0 collective-permute-done.2.near
  14.6 0.0 copy-done.2
  14.6 3.3 %collective-permute-start.3 = (bf16[128,1024]{1,0:T(8,128)(2,1)S(1)}, bf16[128,1024]{1,0:T(8,128)(2,1)S(1)}, u32[]{:S(2)}, u32[]{:S(2)}) collective-permute-start(bf16[128,1024]{1,0:T(8,128)(2,1)S(1)} %join.1), channel_id=1, source_target_pairs={{0,2},{2,0},{1,3},{3,1},{4,6},{6,4},{5,7},{7,5},{8,10},{10,8},{9,1... | collective-permute-start | bytes 786440 | tf_op jit(solution)/shard_map/ppermute | solution.py:348
  17.9 0.0 copy-done
  17.9 0.0 copy-start.1
  17.9 5.6 %collective-permute-start.1 = (bf16[2,16,128]{2,1,0:T(8,128)(2,1)S(1)}, bf16[2,16,128]{2,1,0:T(8,128)(2,1)S(1)}, u32[]{:S(2)}, u32[]{:S(2)}) collective-permute-start(bf16[2,16,128]{2,1,0:T(8,128)(2,1)S(1)} %pad_maximum_fusion.own), channel_id=1, source_target_pairs={{32,64},{96,128},{160,192},{224,256},{288,320},{352,384},{416,448}... | collective-permute-start | bytes 24584 | tf_op jit(solution)/shard_map/ppermute | solution.py:391
  23.6 1.9 %collective-permute-start = (bf16[2,16,128]{2,1,0:T(8,128)(2,1)S(1)}, bf16[2,16,128]{2,1,0:T(8,128)(2,1)S(1)}, u32[]{:S(2)}, u32[]{:S(2)}) collective-permute-start(bf16[2,16,128]{2,1,0:T(8,128)(2,1)S(1)} %pad_maximum_fusion.own), channel_id=1, source_target_pairs={{0,32},{32,0},{1,33},{33,1},{2,34},{34,2},{3,35},{35,3},{4,36},{36... | collective-permute-start | bytes 24584 | tf_op jit(solution)/shard_map/ppermute | solution.py:348
  25.5 0.0 collective-permute-done.1.hop
  25.5 1.1 %collective-permute-done.swap = bf16[2,16,128]{2,1,0:T(8,128)(2,1)S(1)} collective-permute-done((bf16[2,16,128]{2,1,0:T(8,128)(2,1)S(1)}, bf16[2,16,128]{2,1,0:T(8,128)(2,1)S(1)}, u32[]{:S(2)}, u32[]{:S(2)}) %collective-permute-start) | collective-permute-done | bytes 8224 | tf_op jit(solution)/shard_map/ppermute | solution.py:348
  26.6 0.0 copy-done.1
  26.6 0.3 queries.1.q
  26.9 0.9 %all-to-all-done = bf16[32,96,128]{2,1,0:T(8,128)(2,1)S(1)} async-done(((bf16[32,96,128]{2,1,0:T(8,128)(2,1)}), bf16[32,96,128]{2,1,0:T(8,128)(2,1)S(1)}, u32[]{:S(2)}, u32[]{:S(2)}) %all-to-all-start) | async-done | bytes 786464 | tf_op jit(solution)/shard_map/all_to_all | solution.py:385
  27.7 0.0 copy-start.4
  27.7 7.6 %collective-permute-start.4 = (bf16[8,4,96,128]{3,2,1,0:T(8,128)(2,1)S(1)}, bf16[8,4,96,128]{3,2,1,0:T(8,128)(2,1)S(1)}, u32[]{:S(2)}, u32[]{:S(2)}) collective-permute-start(bf16[8,4,96,128]{3,2,1,0:T(8,128)(2,1)S(1)} %bitcast.7), channel_id=1, source_target_pairs={{0,32},{32,0},{1,33},{33,1},{2,34},{34,2},{3,35},{35,3},{4,36},{36... | collective-permute-start | bytes 2359304 | tf_op jit(solution)/shard_map/ppermute | solution.py:348
  35.4 0.0 collective-permute-done.3.far
  35.4 0.1 pairs.1
  35.5 0.0 copy-start.3
  35.5 1.8 %collective-permute-done.4.far_other = bf16[8,4,96,128]{3,2,1,0:T(8,128)(2,1)S(1)} collective-permute-done((bf16[8,4,96,128]{3,2,1,0:T(8,128)(2,1)S(1)}, bf16[8,4,96,128]{3,2,1,0:T(8,128)(2,1)S(1)}, u32[]{:S(2)}, u32[]{:S(2)}) %collective-permute-start.4) | collective-permute-done | bytes 786464 | tf_op jit(solution)/shard_map/ppermute | solution.py:348
  37.3 0.0 copy-done.4
  37.3 0.0 copy-done.3
  37.3 4.4 %attend.1 = bf16[1024,128]{1,0:T(8,128)(2,1)} custom-call(bf16[1024,128]{1,0:T(8,128)(2,1)S(1)} %queries.1.q, bf16[4,64,1024]{2,1,0:T(8,128)(2,1)S(1)} %pairs.1, bf16[8,4,96,128]{3,2,1,0:T(8,128)(2,1)S(1)} %bitcast.8, bf16[8,4,96,128]{3,2,1,0:T(8,128)(2,1)S(1)} %collective-permute-done.4.far_other, bf16[128,2048]{1,0:T(8,128)(2,1)S(1)} %copy-done.4, ...), custom_call_target="tpu_custom_call" | custom-call | flops 1073741824 | bytes 1048576 | tf_op jit(solution)/shard_map/attend/pallas_call | solution.py:354
  (3 shorter events, 0.0 us)
Async XLA Ops:
  2.5 12.1 %collective-permute-start.2 = (bf16[64,1024]{1,0:T(8,128)(2,1)}, bf16[64,1024]{1,0:T(8,128)(2,1)S(1)}, u32[]{:S(2)}, u32[]{:S(2)}) collective-permute-start(bf16[64,1024]{1,0:T(8,128)(2,1)} %get-tuple-element.11.mine), channel_id=1, source_target_pairs={{0,1},{1,0},{2,3},{3,2},{4,5},{5,4},{6,7},{7,6},{8,9},{9,8},{10,11... | collective-permute-start | bytes 393224 | tf_op jit(solution)/shard_map/ppermute | solution.py:348
  8.1 6.4 %copy-start.2 = (bf16[64,1024]{1,0:T(8,128)(2,1)S(1)}, bf16[64,1024]{1,0:T(8,128)(2,1)}, u32[]{:S(2)}) copy-start(bf16[64,1024]{1,0:T(8,128)(2,1)} %get-tuple-element.11.mine) | copy-start | bytes 393220
  8.1 19.6 %all-to-all-start = ((bf16[32,96,128]{2,1,0:T(8,128)(2,1)}), bf16[32,96,128]{2,1,0:T(8,128)(2,1)S(1)}, u32[]{:S(2)}, u32[]{:S(2)}) async-start(bf16[32,96,128]{2,1,0:T(8,128)(2,1)} %get-tuple-element.9), calls=%async_computation | async-start | bytes 1572864 | tf_op jit(solution)/shard_map/all_to_all | solution.py:385
  14.5 3.3 %copy-start = (bf16[1024,128]{1,0:T(8,128)(2,1)S(1)}, bf16[1024,128]{1,0:T(8,128)(2,1)}, u32[]{:S(2)}) copy-start(bf16[1024,128]{1,0:T(8,128)(2,1)} %q.1) | copy-start | bytes 786436
  14.6 20.8 %collective-permute-start.3 = (bf16[128,1024]{1,0:T(8,128)(2,1)S(1)}, bf16[128,1024]{1,0:T(8,128)(2,1)S(1)}, u32[]{:S(2)}, u32[]{:S(2)}) collective-permute-start(bf16[128,1024]{1,0:T(8,128)(2,1)S(1)} %join.1), channel_id=1, source_target_pairs={{0,2},{2,0},{1,3},{3,1},{4,6},{6,4},{5,7},{7,5},{8,10},{10,8},{9,1... | collective-permute-start | bytes 786440 | tf_op jit(solution)/shard_map/ppermute | solution.py:348
  17.9 8.7 %copy-start.1 = (f32[4,128]{1,0:T(4,128)S(1)}, f32[4,128]{1,0:T(4,128)}, u32[]{:S(2)}) copy-start(f32[4,128]{1,0:T(4,128)} %taps.1) | copy-start | bytes 6148
  17.9 7.6 %collective-permute-start.1 = (bf16[2,16,128]{2,1,0:T(8,128)(2,1)S(1)}, bf16[2,16,128]{2,1,0:T(8,128)(2,1)S(1)}, u32[]{:S(2)}, u32[]{:S(2)}) collective-permute-start(bf16[2,16,128]{2,1,0:T(8,128)(2,1)S(1)} %pad_maximum_fusion.own), channel_id=1, source_target_pairs={{32,64},{96,128},{160,192},{224,256},{288,320},{352,384},{416,448}... | collective-permute-start | bytes 24584 | tf_op jit(solution)/shard_map/ppermute | solution.py:391
  23.6 3.1 %collective-permute-start = (bf16[2,16,128]{2,1,0:T(8,128)(2,1)S(1)}, bf16[2,16,128]{2,1,0:T(8,128)(2,1)S(1)}, u32[]{:S(2)}, u32[]{:S(2)}) collective-permute-start(bf16[2,16,128]{2,1,0:T(8,128)(2,1)S(1)} %pad_maximum_fusion.own), channel_id=1, source_target_pairs={{0,32},{32,0},{1,33},{33,1},{2,34},{34,2},{3,35},{35,3},{4,36},{36... | collective-permute-start | bytes 24584 | tf_op jit(solution)/shard_map/ppermute | solution.py:348
  27.7 9.5 %copy-start.4 = (bf16[128,2048]{1,0:T(8,128)(2,1)S(1)}, bf16[128,2048]{1,0:T(8,128)(2,1)}, u32[]{:S(2)}) copy-start(bf16[128,2048]{1,0:T(8,128)(2,1)} %constant.5.clone.table) | copy-start | bytes 1572868
  27.7 9.5 %collective-permute-start.4 = (bf16[8,4,96,128]{3,2,1,0:T(8,128)(2,1)S(1)}, bf16[8,4,96,128]{3,2,1,0:T(8,128)(2,1)S(1)}, u32[]{:S(2)}, u32[]{:S(2)}) collective-permute-start(bf16[8,4,96,128]{3,2,1,0:T(8,128)(2,1)S(1)} %bitcast.7), channel_id=1, source_target_pairs={{0,32},{32,0},{1,33},{33,1},{2,34},{34,2},{3,35},{35,3},{4,36},{36... | collective-permute-start | bytes 2359304 | tf_op jit(solution)/shard_map/ppermute | solution.py:348
  35.5 1.8 %copy-start.3 = (f32[128]{0:T(128)S(1)}, f32[128]{0:T(128)}, u32[]{:S(2)}) copy-start(f32[128]{0:T(128)} %param.11) | copy-start | bytes 1540

commit v5 on v4

--- a/solution.py
+++ b/solution.py
@@ -121,13 +121,21 @@
     for g in range(1, 4):
         rest = rest + pltpu.roll(low[g * EDGE : (g + 1) * EDGE], g * KEEP, 1)
     rest = rest.astype(BF16)
-    for k in range(block_out.shape[0]):
-        block_out[k, :64] = high
-        block_out[k, 64 : 64 + EDGE] = edges
-        block_out[k, 64 + EDGE :] = rest
+    block_out[:64] = high
+    block_out[64 : 64 + EDGE] = edges
+    block_out[64 + EDGE :] = rest
     moves[4].start()
     moves[3].wait()
     moves[4].wait()
+
+
+def spread_kernel(mine, other, out):
+    first = lax.axis_index("z_lo") == 0
+    lower = jnp.where(first, mine[...], other[...])
+    upper = jnp.where(first, other[...], mine[...])
+    for k in range(out.shape[0]):
+        out[k, 0] = lower
+        out[k, 1] = upper
 
 
 def join_kernel(mine, near, out):
@@ -164,6 +172,10 @@
     pairs[member ^ 3] = far[64:]
 
 
+def slot(m):
+    return m % 2 * 2 + m // 2
+
+
 def attend_kernel(q, pairs, far_own, far_other, table, gain, out, packed, scores, ends):
     place = lax.axis_index(CTX)
     middle = place // 2
@@ -181,8 +193,8 @@
         return pltpu.roll(value, BLOCK // 2, 1)
 
     def edges_of(owner, m):
-        mine = far_own[owner // 2, m, 64 : 64 + EDGE]
-        other = far_other[owner // 2, m, 64 : 64 + EDGE]
+        mine = far_own[owner // 2, slot(m), 64 : 64 + EDGE]
+        other = far_other[owner // 2, slot(m), 64 : 64 + EDGE]
         tile = jnp.where(odd, other, mine) if owner % 2 == 0 else jnp.where(odd, mine, other)
         tile = tile.astype(F32)
         return tile[:8] + tile[8:]
@@ -209,8 +221,8 @@
         for i in range(8):
             for m in range(2):
                 rows = slice(64 * m, 64 * (m + 1))
-                mine = whole_tile(far_own, i, 2 * kind + m)
-                other = whole_tile(far_other, i, 2 * kind + m)
+                mine = whole_tile(far_own, i, slot(2 * kind + m))
+                other = whole_tile(far_other, i, slot(2 * kind + m))
                 low = jnp.where(own_lane, mine, other) + fix[rows, i * BLOCK : (i + 1) * BLOCK]
                 high = jnp.where(own_lane, other, mine)
                 high = high + fix[rows, (8 + i) * BLOCK : (9 + i) * BLOCK]
@@ -365,9 +377,9 @@
     def shape(*dims):
         return jax.ShapeDtypeStruct(dims, BF16)
 
-    conv, blocks = pl.pallas_call(
+    conv, block = pl.pallas_call(
         conv_kernel,
-        out_shape=(shape(64, ROWS), shape(32, SENT, BLOCK)),
+        out_shape=(shape(64, ROWS), shape(SENT, BLOCK)),
         in_specs=[spec(pl.ANY)] * 3,
         out_specs=(spec(pl.ANY), spec(pl.ANY)),
         scratch_shapes=[
@@ -375,14 +387,17 @@
             VMEM((TAPS, 64), F32),
             VMEM((BLOCK, BLOCK), BF16),
             VMEM((64, ROWS), BF16),
-            VMEM((32, SENT, BLOCK), BF16),
+            VMEM((SENT, BLOCK), BF16),
             pltpu.SemaphoreType.DMA((5,)),
         ],
         compiler_params=pltpu.CompilerParams(vmem_limit_bytes=56 << 20),
         cost_estimate=cost(1 << 24, 1 << 20),
         name="conv",
     )(keys_values.T, pair_taps, jnp.asarray(dct_tile()))
-    gathered = lax.all_to_all(blocks, CHIPS + GROUP, 0, 0, tiled=True)
+    blocks = call(
+        spread_kernel, "spread", shape(16, 2, SENT, BLOCK), (block, swapped(block, "z_lo"))
+    )
+    gathered = lax.all_to_all(blocks, CHIPS + ("y_hi",), 0, 0, tiled=True)
     near = swapped(conv, "y_hi")
     far = call(join_kernel, "join", shape(128, ROWS), (conv, near), flops=1 << 37)
     far = swapped(far, "z_lo")

time: 42.1 us -> 44.4 us (1.055)
  Pallas kernels: 7.23 us -> 7.98 us
  local copies, waits for them, and re-layouts: 0.03 us -> 0.77 us
  waiting for transfers between devices: 3.8 us -> 4.37 us
    ppermute x4 -> x5, waiting for transfers between devices: 2.94 us -> 4.33 us  [swapped(): return lax.ppermute(value, axis, [(0, 1), (1, 0)])]
    all_to_all x1, starting transfers between devices: 6.4 us -> 5.04 us  [per_device(): gathered = lax.all_to_all(blocks, CHIPS + ('y_hi',), 0, 0, tiled=True)]
    pallas_call x4 -> x5, Pallas kernels: 4.77 us -> 5.84 us  [call(): pl.pallas_call(kernel, out_shape=out_shape, in_specs=[spec(s) for s in sp...]
    ppermute x4 -> x5, starting transfers between devices: 18.5 us -> 19.5 us  [swapped(): return lax.ppermute(value, axis, [(0, 1), (1, 0)])]
    all_to_all x1, waiting for transfers between devices: 0.85 us -> 0.01 us  [per_device(): gathered = lax.all_to_all(blocks, CHIPS + ('y_hi',), 0, 0, tiled=True)]
    unnamed x10 -> x12, local copies, waits for them, and re-layouts: 0.03 us -> 0.77 us
    ppermute x1, starting transfers between devices: 5.61 us -> 6.09 us  [per_device(): lax.ppermute(tails, CTX, [(i, i + 1) for i in range(1, 15, 2)] + [(i + 1,...]
  transfers between devices with their start and end apart: 6 -> 7, of which waited for: 3 -> 3; matrix products, arithmetic and copies ran while one was open for 0% -> 0% of each run, Pallas kernels for 1% -> 3%
where the time goes in v5:
time: 44.4 us; the launch traced here: 43.9 us
  starting transfers between devices  30.6 us (69%)
  Pallas kernels  7.98 us (18%)
  waiting for transfers between devices  4.37 us (10%)
  local copies, waits for them, and re-layouts  0.77 us (2%)
    ppermute x5, starting transfers between devices, swapped(): return lax.ppermute(value, axis, [(0, 1), (1, 0)])  19.5 us
    ppermute x1, starting transfers between devices, per_device(): lax.ppermute(tails, CTX, [(i, i + 1) for i in range(1, 15, 2)] + [(i + 1,...  6.09 us
    pallas_call x5, Pallas kernels, call(): pl.pallas_call(kernel, out_shape=out_shape, in_specs=[spec(s) for s in sp...  5.84 us
    all_to_all x1, starting transfers between devices, per_device(): gathered = lax.all_to_all(blocks, CHIPS + ('y_hi',), 0, 0, tiled=True)  5.04 us
    ppermute x5, waiting for transfers between devices, swapped(): return lax.ppermute(value, axis, [(0, 1), (1, 0)])  4.33 us
    pallas_call x1, Pallas kernels, per_device(): pl.pallas_call(conv_kernel, out_shape=(shape(64, ROWS), shape(SENT, BLOCK...  2.14 us
  transfers between devices with their start and end apart: 7, of which 3 were waited for; matrix products, arithmetic and copies ran while one was open for 0% of the time, Pallas kernels for 3%

profile of v5, /device:TPU:1, one launch (start us, length us, event | category | flops | bytes accessed | tf_op | source)
XLA Modules:
  0.0 43.9 jit_solution(13359866422395812889)
XLA Ops:
  0.0 2.1 %conv.1 = (bf16[64,1024]{1,0:T(8,128)(2,1)}, bf16[96,128]{1,0:T(8,128)(2,1)}) custom-call(bf16[64,1024]{1,0:T(8,128)(2,1)} %bitcast.10, f32[4,64]{1,0:T(4,128)} %taps_in.1, bf16[128,128]{1,0:T(8,128)(2,1)} %constant.4.clone.table_in), custom_call_target="tpu_custom_call" | custom-call | flops 16777216 | bytes 1048576 | tf_op jit(solution)/shard_map/conv/pallas_call | solution.py:380
  2.2 5.7 %collective-permute-start.3 = (bf16[64,1024]{1,0:T(8,128)(2,1)}, bf16[64,1024]{1,0:T(8,128)(2,1)S(1)}, u32[]{:S(2)}, u32[]{:S(2)}) collective-permute-start(bf16[64,1024]{1,0:T(8,128)(2,1)} %get-tuple-element.11.mine), channel_id=1, source_target_pairs={{0,1},{1,0},{2,3},{3,2},{4,5},{5,4},{6,7},{7,6},{8,9},{9,8},{10,11... | collective-permute-start | bytes 393224 | tf_op jit(solution)/shard_map/ppermute | solution.py:360
  7.8 3.5 %collective-permute-start = (bf16[96,128]{1,0:T(8,128)(2,1)}, bf16[96,128]{1,0:T(8,128)(2,1)S(1)}, u32[]{:S(2)}, u32[]{:S(2)}) collective-permute-start(bf16[96,128]{1,0:T(8,128)(2,1)} %get-tuple-element.9.mine), channel_id=1, source_target_pairs={{0,2},{2,0},{1,3},{3,1},{4,6},{6,4},{5,7},{7,5},{8,10},{10,8},{9,1... | collective-permute-start | bytes 73736 | tf_op jit(solution)/shard_map/ppermute | solution.py:360
  11.4 1.4 %collective-permute-done.other = bf16[96,128]{1,0:T(8,128)(2,1)S(1)} collective-permute-done((bf16[96,128]{1,0:T(8,128)(2,1)}, bf16[96,128]{1,0:T(8,128)(2,1)S(1)}, u32[]{:S(2)}, u32[]{:S(2)}) %collective-permute-start) | collective-permute-done | bytes 24608 | tf_op jit(solution)/shard_map/ppermute | solution.py:360
  12.8 0.0 copy-start.1
  12.8 0.7 %copy-done.1 = bf16[96,128]{1,0:T(8,128)(2,1)S(1)} copy-done((bf16[96,128]{1,0:T(8,128)(2,1)S(1)}, bf16[96,128]{1,0:T(8,128)(2,1)}, u32[]{:S(2)}) %copy-start.1) | copy-done | bytes 24600
  13.5 1.1 %spread.1 = bf16[16,2,96,128]{3,2,1,0:T(8,128)(2,1)} custom-call(bf16[96,128]{1,0:T(8,128)(2,1)S(1)} %copy-done.1, bf16[96,128]{1,0:T(8,128)(2,1)S(1)} %collective-permute-done.other), custom_call_target="tpu_custom_call" | custom-call | flops 16777216 | bytes 1048576 | tf_op jit(solution)/shard_map/spread/pallas_call | solution.py:366
  14.6 0.0 copy-start.3
  14.6 5.0 %all-to-all-start = ((bf16[16,2,96,128]{3,2,1,0:T(8,128)(2,1)}), bf16[16,2,96,128]{3,2,1,0:T(8,128)(2,1)S(1)}, u32[]{:S(2)}, u32[]{:S(2)}) async-start(bf16[16,2,96,128]{3,2,1,0:T(8,128)(2,1)} %spread.1), calls=%async_computation | async-start | bytes 1572864 | tf_op jit(solution)/shard_map/all_to_all | solution.py:400
  19.6 0.0 copy-start
  19.6 0.0 collective-permute-done.3.near
  19.7 0.0 copy-done.3
  19.7 3.5 %collective-permute-start.4 = (bf16[128,1024]{1,0:T(8,128)(2,1)S(1)}, bf16[128,1024]{1,0:T(8,128)(2,1)S(1)}, u32[]{:S(2)}, u32[]{:S(2)}) collective-permute-start(bf16[128,1024]{1,0:T(8,128)(2,1)S(1)} %join.1), channel_id=1, source_target_pairs={{0,2},{2,0},{1,3},{3,1},{4,6},{6,4},{5,7},{7,5},{8,10},{10,8},{9,1... | collective-permute-start | bytes 786440 | tf_op jit(solution)/shard_map/ppermute | solution.py:360
  23.2 0.0 copy-done
  23.2 0.0 copy-start.2
  23.2 6.1 %collective-permute-start.2 = (bf16[2,16,128]{2,1,0:T(8,128)(2,1)S(1)}, bf16[2,16,128]{2,1,0:T(8,128)(2,1)S(1)}, u32[]{:S(2)}, u32[]{:S(2)}) collective-permute-start(bf16[2,16,128]{2,1,0:T(8,128)(2,1)S(1)} %pad_maximum_fusion.own), channel_id=1, source_target_pairs={{32,64},{96,128},{160,192},{224,256},{288,320},{352,384},{416,448}... | collective-permute-start | bytes 24584 | tf_op jit(solution)/shard_map/ppermute | solution.py:406
  29.3 1.9 %collective-permute-start.1 = (bf16[2,16,128]{2,1,0:T(8,128)(2,1)S(1)}, bf16[2,16,128]{2,1,0:T(8,128)(2,1)S(1)}, u32[]{:S(2)}, u32[]{:S(2)}) collective-permute-start(bf16[2,16,128]{2,1,0:T(8,128)(2,1)S(1)} %pad_maximum_fusion.own), channel_id=1, source_target_pairs={{0,32},{32,0},{1,33},{33,1},{2,34},{34,2},{3,35},{35,3},{4,36},{36... | collective-permute-start | bytes 24584 | tf_op jit(solution)/shard_map/ppermute | solution.py:360
  31.3 0.0 collective-permute-done.2.hop
  31.3 1.1 %collective-permute-done.1.swap = bf16[2,16,128]{2,1,0:T(8,128)(2,1)S(1)} collective-permute-done((bf16[2,16,128]{2,1,0:T(8,128)(2,1)S(1)}, bf16[2,16,128]{2,1,0:T(8,128)(2,1)S(1)}, u32[]{:S(2)}, u32[]{:S(2)}) %collective-permute-start.1) | collective-permute-done | bytes 8224 | tf_op jit(solution)/shard_map/ppermute | solution.py:360
  32.4 0.0 copy-done.2
  32.4 0.3 queries.1.q
  32.7 0.0 all-to-all-done
  32.7 0.0 copy-start.5
  32.7 4.9 %collective-permute-start.5 = (bf16[8,4,96,128]{3,2,1,0:T(8,128)(2,1)S(1)}, bf16[8,4,96,128]{3,2,1,0:T(8,128)(2,1)S(1)}, u32[]{:S(2)}, u32[]{:S(2)}) collective-permute-start(bf16[8,4,96,128]{3,2,1,0:T(8,128)(2,1)S(1)} %bitcast.7), channel_id=1, source_target_pairs={{0,32},{32,0},{1,33},{33,1},{2,34},{34,2},{3,35},{35,3},{4,36},{36... | collective-permute-start | bytes 2359304 | tf_op jit(solution)/shard_map/ppermute | solution.py:360
  37.6 0.0 collective-permute-done.4.far
  37.6 0.1 pairs.1
  37.6 0.0 copy-start.4
  37.7 1.8 %collective-permute-done.5.far_other = bf16[8,4,96,128]{3,2,1,0:T(8,128)(2,1)S(1)} collective-permute-done((bf16[8,4,96,128]{3,2,1,0:T(8,128)(2,1)S(1)}, bf16[8,4,96,128]{3,2,1,0:T(8,128)(2,1)S(1)}, u32[]{:S(2)}, u32[]{:S(2)}) %collective-permute-start.5) | collective-permute-done | bytes 786464 | tf_op jit(solution)/shard_map/ppermute | solution.py:360
  39.5 0.0 copy-done.5
  39.5 0.0 copy-done.4
  39.5 4.4 %attend.1 = bf16[1024,128]{1,0:T(8,128)(2,1)} custom-call(bf16[1024,128]{1,0:T(8,128)(2,1)S(1)} %queries.1.q, bf16[4,64,1024]{2,1,0:T(8,128)(2,1)S(1)} %pairs.1, bf16[8,4,96,128]{3,2,1,0:T(8,128)(2,1)S(1)} %bitcast.8, bf16[8,4,96,128]{3,2,1,0:T(8,128)(2,1)S(1)} %collective-permute-done.5.far_other, bf16[128,2048]{1,0:T(8,128)(2,1)S(1)} %copy-done.5, ...), custom_call_target="tpu_custom_call" | custom-call | flops 1073741824 | bytes 1048576 | tf_op jit(solution)/shard_map/attend/pallas_call | solution.py:366
  (3 shorter events, 0.0 us)
Async XLA Ops:
  2.2 17.5 %collective-permute-start.3 = (bf16[64,1024]{1,0:T(8,128)(2,1)}, bf16[64,1024]{1,0:T(8,128)(2,1)S(1)}, u32[]{:S(2)}, u32[]{:S(2)}) collective-permute-start(bf16[64,1024]{1,0:T(8,128)(2,1)} %get-tuple-element.11.mine), channel_id=1, source_target_pairs={{0,1},{1,0},{2,3},{3,2},{4,5},{5,4},{6,7},{7,6},{8,9},{9,8},{10,11... | collective-permute-start | bytes 393224 | tf_op jit(solution)/shard_map/ppermute | solution.py:360
  7.8 5.0 %collective-permute-start = (bf16[96,128]{1,0:T(8,128)(2,1)}, bf16[96,128]{1,0:T(8,128)(2,1)S(1)}, u32[]{:S(2)}, u32[]{:S(2)}) collective-permute-start(bf16[96,128]{1,0:T(8,128)(2,1)} %get-tuple-element.9.mine), channel_id=1, source_target_pairs={{0,2},{2,0},{1,3},{3,1},{4,6},{6,4},{5,7},{7,5},{8,10},{10,8},{9,1... | collective-permute-start | bytes 73736 | tf_op jit(solution)/shard_map/ppermute | solution.py:360
  12.8 0.7 %copy-start.1 = (bf16[96,128]{1,0:T(8,128)(2,1)S(1)}, bf16[96,128]{1,0:T(8,128)(2,1)}, u32[]{:S(2)}) copy-start(bf16[96,128]{1,0:T(8,128)(2,1)} %get-tuple-element.9.mine) | copy-start | bytes 73732
  14.6 5.1 %copy-start.3 = (bf16[64,1024]{1,0:T(8,128)(2,1)S(1)}, bf16[64,1024]{1,0:T(8,128)(2,1)}, u32[]{:S(2)}) copy-start(bf16[64,1024]{1,0:T(8,128)(2,1)} %get-tuple-element.11.mine) | copy-start | bytes 393220
  14.6 18.1 %all-to-all-start = ((bf16[16,2,96,128]{3,2,1,0:T(8,128)(2,1)}), bf16[16,2,96,128]{3,2,1,0:T(8,128)(2,1)S(1)}, u32[]{:S(2)}, u32[]{:S(2)}) async-start(bf16[16,2,96,128]{3,2,1,0:T(8,128)(2,1)} %spread.1), calls=%async_computation | async-start | bytes 1572864 | tf_op jit(solution)/shard_map/all_to_all | solution.py:400
  19.6 3.6 %copy-start = (bf16[1024,128]{1,0:T(8,128)(2,1)S(1)}, bf16[1024,128]{1,0:T(8,128)(2,1)}, u32[]{:S(2)}) copy-start(bf16[1024,128]{1,0:T(8,128)(2,1)} %q.1) | copy-start | bytes 786436
  19.7 17.9 %collective-permute-start.4 = (bf16[128,1024]{1,0:T(8,128)(2,1)S(1)}, bf16[128,1024]{1,0:T(8,128)(2,1)S(1)}, u32[]{:S(2)}, u32[]{:S(2)}) collective-permute-start(bf16[128,1024]{1,0:T(8,128)(2,1)S(1)} %join.1), channel_id=1, source_target_pairs={{0,2},{2,0},{1,3},{3,1},{4,6},{6,4},{5,7},{7,5},{8,10},{10,8},{9,1... | collective-permute-start | bytes 786440 | tf_op jit(solution)/shard_map/ppermute | solution.py:360
  23.2 9.2 %copy-start.2 = (f32[4,128]{1,0:T(4,128)S(1)}, f32[4,128]{1,0:T(4,128)}, u32[]{:S(2)}) copy-start(f32[4,128]{1,0:T(4,128)} %taps.1) | copy-start | bytes 6148
  23.2 8.1 %collective-permute-start.2 = (bf16[2,16,128]{2,1,0:T(8,128)(2,1)S(1)}, bf16[2,16,128]{2,1,0:T(8,128)(2,1)S(1)}, u32[]{:S(2)}, u32[]{:S(2)}) collective-permute-start(bf16[2,16,128]{2,1,0:T(8,128)(2,1)S(1)} %pad_maximum_fusion.own), channel_id=1, source_target_pairs={{32,64},{96,128},{160,192},{224,256},{288,320},{352,384},{416,448}... | collective-permute-start | bytes 24584 | tf_op jit(solution)/shard_map/ppermute | solution.py:406
  29.3 3.1 %collective-permute-start.1 = (bf16[2,16,128]{2,1,0:T(8,128)(2,1)S(1)}, bf16[2,16,128]{2,1,0:T(8,128)(2,1)S(1)}, u32[]{:S(2)}, u32[]{:S(2)}) collective-permute-start(bf16[2,16,128]{2,1,0:T(8,128)(2,1)S(1)} %pad_maximum_fusion.own), channel_id=1, source_target_pairs={{0,32},{32,0},{1,33},{33,1},{2,34},{34,2},{3,35},{35,3},{4,36},{36... | collective-permute-start | bytes 24584 | tf_op jit(solution)/shard_map/ppermute | solution.py:360
  32.7 6.8 %copy-start.5 = (bf16[128,2048]{1,0:T(8,128)(2,1)S(1)}, bf16[128,2048]{1,0:T(8,128)(2,1)}, u32[]{:S(2)}) copy-start(bf16[128,2048]{1,0:T(8,128)(2,1)} %constant.5.clone.table) | copy-start | bytes 1572868
  32.7 6.8 %collective-permute-start.5 = (bf16[8,4,96,128]{3,2,1,0:T(8,128)(2,1)S(1)}, bf16[8,4,96,128]{3,2,1,0:T(8,128)(2,1)S(1)}, u32[]{:S(2)}, u32[]{:S(2)}) collective-permute-start(bf16[8,4,96,128]{3,2,1,0:T(8,128)(2,1)S(1)} %bitcast.7), channel_id=1, source_target_pairs={{0,32},{32,0},{1,33},{33,1},{2,34},{34,2},{3,35},{35,3},{4,36},{36... | collective-permute-start | bytes 2359304 | tf_op jit(solution)/shard_map/ppermute | solution.py:360
  37.6 1.8 %copy-start.4 = (f32[128]{0:T(128)S(1)}, f32[128]{0:T(128)}, u32[]{:S(2)}) copy-start(f32[128]{0:T(128)} %param.11) | copy-start | bytes 1540

commit v6 on v5

--- a/solution.py
+++ b/solution.py
@@ -129,13 +129,16 @@
     moves[4].wait()
 
 
-def spread_kernel(mine, other, out):
-    first = lax.axis_index("z_lo") == 0
-    lower = jnp.where(first, mine[...], other[...])
-    upper = jnp.where(first, other[...], mine[...])
+def spread_kernel(mine, other, out, sems):
+    place = lax.axis_index("z_lo")
+    copies = []
     for k in range(out.shape[0]):
-        out[k, 0] = lower
-        out[k, 1] = upper
+        copies.append(pltpu.make_async_copy(mine, out.at[k, place], sems.at[k, 0]))
+        copies.append(pltpu.make_async_copy(other, out.at[k, 1 - place], sems.at[k, 1]))
+    for copy in copies:
+        copy.start()
+    for copy in copies:
+        copy.wait()
 
 
 def join_kernel(mine, near, out):
@@ -394,9 +397,16 @@
         cost_estimate=cost(1 << 24, 1 << 20),
         name="conv",
     )(keys_values.T, pair_taps, jnp.asarray(dct_tile()))
-    blocks = call(
-        spread_kernel, "spread", shape(16, 2, SENT, BLOCK), (block, swapped(block, "z_lo"))
-    )
+    blocks = pl.pallas_call(
+        spread_kernel,
+        out_shape=shape(16, 2, SENT, BLOCK),
+        in_specs=[spec(pl.ANY)] * 2,
+        out_specs=spec(pl.ANY),
+        scratch_shapes=[pltpu.SemaphoreType.DMA((16, 2))],
+        compiler_params=pltpu.CompilerParams(vmem_limit_bytes=56 << 20),
+        cost_estimate=cost(1 << 37, 1 << 20),
+        name="spread",
+    )(block, swapped(block, "z_lo"))
     gathered = lax.all_to_all(blocks, CHIPS + ("y_hi",), 0, 0, tiled=True)
     near = swapped(conv, "y_hi")
     far = call(join_kernel, "join", shape(128, ROWS), (conv, near), flops=1 << 37)

time: 44.4 us -> 66 us (1.49)
  Pallas kernels: 7.98 us -> 32.1 us
  waiting for transfers between devices: 4.37 us -> 2.95 us
  starting transfers between devices: 30.6 us -> 29.7 us
    pallas_call x0 -> x1, Pallas kernels: none -> 25.2 us  [per_device(): pl.pallas_call(spread_kernel, out_shape=shape(16, 2, SENT, BLOCK), in_spe...]
    ppermute x5, starting transfers between devices: 19.5 us -> 17.8 us  [swapped(): return lax.ppermute(value, axis, [(0, 1), (1, 0)])]
    ppermute x5, waiting for transfers between devices: 4.33 us -> 2.95 us  [swapped(): return lax.ppermute(value, axis, [(0, 1), (1, 0)])]
    pallas_call x5 -> x4, Pallas kernels: 5.84 us -> 4.76 us  [call(): pl.pallas_call(kernel, out_shape=out_shape, in_specs=[spec(s) for s in sp...]
    ppermute x1, starting transfers between devices: 6.09 us -> 7.09 us  [per_device(): lax.ppermute(tails, CTX, [(i, i + 1) for i in range(1, 15, 2)] + [(i + 1,...]
  transfers between devices with their start and end apart: 7 -> 7, of which waited for: 3 -> 2; matrix products, arithmetic and copies ran while one was open for 0% -> 0% of each run, Pallas kernels for 3% -> 39%
where the time goes in v6:
time: 66 us; the launch traced here: 65.6 us
  Pallas kernels  32.1 us (49%)
  starting transfers between devices  29.7 us (45%)
  waiting for transfers between devices  2.95 us (4%)
    pallas_call x1, Pallas kernels, per_device(): pl.pallas_call(spread_kernel, out_shape=shape(16, 2, SENT, BLOCK), in_spe...  25.2 us
    ppermute x5, starting transfers between devices, swapped(): return lax.ppermute(value, axis, [(0, 1), (1, 0)])  17.8 us
    ppermute x1, starting transfers between devices, per_device(): lax.ppermute(tails, CTX, [(i, i + 1) for i in range(1, 15, 2)] + [(i + 1,...  7.09 us
    all_to_all x1, starting transfers between devices, per_device(): gathered = lax.all_to_all(blocks, CHIPS + ('y_hi',), 0, 0, tiled=True)  4.76 us
    pallas_call x4, Pallas kernels, call(): pl.pallas_call(kernel, out_shape=out_shape, in_specs=[spec(s) for s in sp...  4.76 us
    ppermute x5, waiting for transfers between devices, swapped(): return lax.ppermute(value, axis, [(0, 1), (1, 0)])  2.95 us
    pallas_call x1, Pallas kernels, per_device(): pl.pallas_call(conv_kernel, out_shape=(shape(64, ROWS), shape(SENT, BLOCK...  2.15 us
  transfers between devices with their start and end apart: 7, of which 2 were waited for; matrix products, arithmetic and copies ran while one was open for 0% of the time, Pallas kernels for 39%

profile of v6, /device:TPU:1, one launch (start us, length us, event | category | flops | bytes accessed | tf_op | source)
XLA Modules:
  0.0 65.6 jit_solution(13923642979863191800)
XLA Ops:
  0.0 2.1 %conv.1 = (bf16[64,1024]{1,0:T(8,128)(2,1)}, bf16[96,128]{1,0:T(8,128)(2,1)}) custom-call(bf16[64,1024]{1,0:T(8,128)(2,1)} %bitcast.10, f32[4,64]{1,0:T(4,128)} %taps_in.1, bf16[128,128]{1,0:T(8,128)(2,1)} %constant.4.clone.table_in), custom_call_target="tpu_custom_call" | custom-call | flops 16777216 | bytes 1048576 | tf_op jit(solution)/shard_map/conv/pallas_call | solution.py:383
  2.2 4.4 %collective-permute-start = (bf16[96,128]{1,0:T(8,128)(2,1)}, bf16[96,128]{1,0:T(8,128)(2,1)S(1)}, u32[]{:S(2)}, u32[]{:S(2)}) collective-permute-start(bf16[96,128]{1,0:T(8,128)(2,1)} %get-tuple-element.9.mine), channel_id=1, source_target_pairs={{0,2},{2,0},{1,3},{3,1},{4,6},{6,4},{5,7},{7,5},{8,10},{10,8},{9,1... | collective-permute-start | bytes 73736 | tf_op jit(solution)/shard_map/ppermute | solution.py:363
  6.5 4.8 %collective-permute-start.3 = (bf16[64,1024]{1,0:T(8,128)(2,1)}, bf16[64,1024]{1,0:T(8,128)(2,1)S(1)}, u32[]{:S(2)}, u32[]{:S(2)}) collective-permute-start(bf16[64,1024]{1,0:T(8,128)(2,1)} %get-tuple-element.11.mine), channel_id=1, source_target_pairs={{0,1},{1,0},{2,3},{3,2},{4,5},{5,4},{6,7},{7,6},{8,9},{9,8},{10,11... | collective-permute-start | bytes 393224 | tf_op jit(solution)/shard_map/ppermute | solution.py:363
  11.4 0.0 collective-permute-done.other
  11.4 0.0 copy-start.5
  11.4 0.6 copy-done.5
  12.0 25.2 %spread.1 = bf16[16,2,96,128]{3,2,1,0:T(8,128)(2,1)} custom-call(bf16[96,128]{1,0:T(8,128)(2,1)} %get-tuple-element.9.mine, bf16[96,128]{1,0:T(8,128)(2,1)} %copy-done.5), custom_call_target="tpu_custom_call" | custom-call | flops 137438953472 | bytes 1048576 | tf_op jit(solution)/shard_map/spread/pallas_call | solution.py:400
  37.2 0.0 copy-start.2
  37.2 4.8 %all-to-all-start = ((bf16[16,2,96,128]{3,2,1,0:T(8,128)(2,1)}), bf16[16,2,96,128]{3,2,1,0:T(8,128)(2,1)S(1)}, u32[]{:S(2)}, u32[]{:S(2)}) async-start(bf16[16,2,96,128]{3,2,1,0:T(8,128)(2,1)} %spread.1), calls=%async_computation | async-start | bytes 1572864 | tf_op jit(solution)/shard_map/all_to_all | solution.py:410
  42.0 0.0 copy-start
  42.0 0.0 collective-permute-done.3.near
  42.0 0.0 copy-done.2
  42.0 2.2 %collective-permute-start.4 = (bf16[128,1024]{1,0:T(8,128)(2,1)S(1)}, bf16[128,1024]{1,0:T(8,128)(2,1)S(1)}, u32[]{:S(2)}, u32[]{:S(2)}) collective-permute-start(bf16[128,1024]{1,0:T(8,128)(2,1)S(1)} %join.1), channel_id=1, source_target_pairs={{0,2},{2,0},{1,3},{3,1},{4,6},{6,4},{5,7},{7,5},{8,10},{10,8},{9,1... | collective-permute-start | bytes 786440 | tf_op jit(solution)/shard_map/ppermute | solution.py:363
  44.3 0.0 copy-done
  44.3 0.0 copy-start.1
  44.3 7.1 %collective-permute-start.2 = (bf16[2,16,128]{2,1,0:T(8,128)(2,1)S(1)}, bf16[2,16,128]{2,1,0:T(8,128)(2,1)S(1)}, u32[]{:S(2)}, u32[]{:S(2)}) collective-permute-start(bf16[2,16,128]{2,1,0:T(8,128)(2,1)S(1)} %pad_maximum_fusion.own), channel_id=1, source_target_pairs={{32,64},{96,128},{160,192},{224,256},{288,320},{352,384},{416,448}... | collective-permute-start | bytes 24584 | tf_op jit(solution)/shard_map/ppermute | solution.py:416
  51.4 1.9 %collective-permute-start.1 = (bf16[2,16,128]{2,1,0:T(8,128)(2,1)S(1)}, bf16[2,16,128]{2,1,0:T(8,128)(2,1)S(1)}, u32[]{:S(2)}, u32[]{:S(2)}) collective-permute-start(bf16[2,16,128]{2,1,0:T(8,128)(2,1)S(1)} %pad_maximum_fusion.own), channel_id=1, source_target_pairs={{0,32},{32,0},{1,33},{33,1},{2,34},{34,2},{3,35},{35,3},{4,36},{36... | collective-permute-start | bytes 24584 | tf_op jit(solution)/shard_map/ppermute | solution.py:363
  53.3 0.0 collective-permute-done.2.hop
  53.3 1.1 %collective-permute-done.1.swap = bf16[2,16,128]{2,1,0:T(8,128)(2,1)S(1)} collective-permute-done((bf16[2,16,128]{2,1,0:T(8,128)(2,1)S(1)}, bf16[2,16,128]{2,1,0:T(8,128)(2,1)S(1)}, u32[]{:S(2)}, u32[]{:S(2)}) %collective-permute-start.1) | collective-permute-done | bytes 8224 | tf_op jit(solution)/shard_map/ppermute | solution.py:363
  54.5 0.0 copy-done.1
  54.5 0.3 queries.1.q
  54.7 0.0 all-to-all-done
  54.7 0.0 copy-start.4
  54.8 4.5 %collective-permute-start.5 = (bf16[8,4,96,128]{3,2,1,0:T(8,128)(2,1)S(1)}, bf16[8,4,96,128]{3,2,1,0:T(8,128)(2,1)S(1)}, u32[]{:S(2)}, u32[]{:S(2)}) collective-permute-start(bf16[8,4,96,128]{3,2,1,0:T(8,128)(2,1)S(1)} %bitcast.7), channel_id=1, source_target_pairs={{0,32},{32,0},{1,33},{33,1},{2,34},{34,2},{3,35},{35,3},{4,36},{36... | collective-permute-start | bytes 2359304 | tf_op jit(solution)/shard_map/ppermute | solution.py:363
  59.3 0.0 collective-permute-done.4.far
  59.3 0.1 pairs.1
  59.3 0.0 copy-start.3
  59.4 1.8 %collective-permute-done.5.far_other = bf16[8,4,96,128]{3,2,1,0:T(8,128)(2,1)S(1)} collective-permute-done((bf16[8,4,96,128]{3,2,1,0:T(8,128)(2,1)S(1)}, bf16[8,4,96,128]{3,2,1,0:T(8,128)(2,1)S(1)}, u32[]{:S(2)}, u32[]{:S(2)}) %collective-permute-start.5) | collective-permute-done | bytes 786464 | tf_op jit(solution)/shard_map/ppermute | solution.py:363
  61.2 0.0 copy-done.4
  61.2 0.0 copy-done.3
  61.2 4.4 %attend.1 = bf16[1024,128]{1,0:T(8,128)(2,1)} custom-call(bf16[1024,128]{1,0:T(8,128)(2,1)S(1)} %queries.1.q, bf16[4,64,1024]{2,1,0:T(8,128)(2,1)S(1)} %pairs.1, bf16[8,4,96,128]{3,2,1,0:T(8,128)(2,1)S(1)} %bitcast.8, bf16[8,4,96,128]{3,2,1,0:T(8,128)(2,1)S(1)} %collective-permute-done.5.far_other, bf16[128,2048]{1,0:T(8,128)(2,1)S(1)} %copy-done.4, ...), custom_call_target="tpu_custom_call" | custom-call | flops 1073741824 | bytes 1048576 | tf_op jit(solution)/shard_map/attend/pallas_call | solution.py:369
  (3 shorter events, 0.0 us)
Async XLA Ops:
  2.2 9.2 %collective-permute-start = (bf16[96,128]{1,0:T(8,128)(2,1)}, bf16[96,128]{1,0:T(8,128)(2,1)S(1)}, u32[]{:S(2)}, u32[]{:S(2)}) collective-permute-start(bf16[96,128]{1,0:T(8,128)(2,1)} %get-tuple-element.9.mine), channel_id=1, source_target_pairs={{0,2},{2,0},{1,3},{3,1},{4,6},{6,4},{5,7},{7,5},{8,10},{10,8},{9,1... | collective-permute-start | bytes 73736 | tf_op jit(solution)/shard_map/ppermute | solution.py:363
  6.5 35.5 %collective-permute-start.3 = (bf16[64,1024]{1,0:T(8,128)(2,1)}, bf16[64,1024]{1,0:T(8,128)(2,1)S(1)}, u32[]{:S(2)}, u32[]{:S(2)}) collective-permute-start(bf16[64,1024]{1,0:T(8,128)(2,1)} %get-tuple-element.11.mine), channel_id=1, source_target_pairs={{0,1},{1,0},{2,3},{3,2},{4,5},{5,4},{6,7},{7,6},{8,9},{9,8},{10,11... | collective-permute-start | bytes 393224 | tf_op jit(solution)/shard_map/ppermute | solution.py:363
  11.4 0.6 copy-start.5
  37.2 4.8 %copy-start.2 = (bf16[64,1024]{1,0:T(8,128)(2,1)S(1)}, bf16[64,1024]{1,0:T(8,128)(2,1)}, u32[]{:S(2)}) copy-start(bf16[64,1024]{1,0:T(8,128)(2,1)} %get-tuple-element.11.mine) | copy-start | bytes 393220
  37.2 17.5 %all-to-all-start = ((bf16[16,2,96,128]{3,2,1,0:T(8,128)(2,1)}), bf16[16,2,96,128]{3,2,1,0:T(8,128)(2,1)S(1)}, u32[]{:S(2)}, u32[]{:S(2)}) async-start(bf16[16,2,96,128]{3,2,1,0:T(8,128)(2,1)} %spread.1), calls=%async_computation | async-start | bytes 1572864 | tf_op jit(solution)/shard_map/all_to_all | solution.py:410
  42.0 2.3 %copy-start = (bf16[1024,128]{1,0:T(8,128)(2,1)S(1)}, bf16[1024,128]{1,0:T(8,128)(2,1)}, u32[]{:S(2)}) copy-start(bf16[1024,128]{1,0:T(8,128)(2,1)} %q.1) | copy-start | bytes 786436
  42.0 17.2 %collective-permute-start.4 = (bf16[128,1024]{1,0:T(8,128)(2,1)S(1)}, bf16[128,1024]{1,0:T(8,128)(2,1)S(1)}, u32[]{:S(2)}, u32[]{:S(2)}) collective-permute-start(bf16[128,1024]{1,0:T(8,128)(2,1)S(1)} %join.1), channel_id=1, source_target_pairs={{0,2},{2,0},{1,3},{3,1},{4,6},{6,4},{5,7},{7,5},{8,10},{10,8},{9,1... | collective-permute-start | bytes 786440 | tf_op jit(solution)/shard_map/ppermute | solution.py:363
  44.3 10.2 %copy-start.1 = (f32[4,128]{1,0:T(4,128)S(1)}, f32[4,128]{1,0:T(4,128)}, u32[]{:S(2)}) copy-start(f32[4,128]{1,0:T(4,128)} %taps.1) | copy-start | bytes 6148
  44.3 9.0 %collective-permute-start.2 = (bf16[2,16,128]{2,1,0:T(8,128)(2,1)S(1)}, bf16[2,16,128]{2,1,0:T(8,128)(2,1)S(1)}, u32[]{:S(2)}, u32[]{:S(2)}) collective-permute-start(bf16[2,16,128]{2,1,0:T(8,128)(2,1)S(1)} %pad_maximum_fusion.own), channel_id=1, source_target_pairs={{32,64},{96,128},{160,192},{224,256},{288,320},{352,384},{416,448}... | collective-permute-start | bytes 24584 | tf_op jit(solution)/shard_map/ppermute | solution.py:416
  51.4 3.1 %collective-permute-start.1 = (bf16[2,16,128]{2,1,0:T(8,128)(2,1)S(1)}, bf16[2,16,128]{2,1,0:T(8,128)(2,1)S(1)}, u32[]{:S(2)}, u32[]{:S(2)}) collective-permute-start(bf16[2,16,128]{2,1,0:T(8,128)(2,1)S(1)} %pad_maximum_fusion.own), channel_id=1, source_target_pairs={{0,32},{32,0},{1,33},{33,1},{2,34},{34,2},{3,35},{35,3},{4,36},{36... | collective-permute-start | bytes 24584 | tf_op jit(solution)/shard_map/ppermute | solution.py:363
  54.7 6.4 %copy-start.4 = (bf16[128,2048]{1,0:T(8,128)(2,1)S(1)}, bf16[128,2048]{1,0:T(8,128)(2,1)}, u32[]{:S(2)}) copy-start(bf16[128,2048]{1,0:T(8,128)(2,1)} %constant.5.clone.table) | copy-start | bytes 1572868
  54.8 6.4 %collective-permute-start.5 = (bf16[8,4,96,128]{3,2,1,0:T(8,128)(2,1)S(1)}, bf16[8,4,96,128]{3,2,1,0:T(8,128)(2,1)S(1)}, u32[]{:S(2)}, u32[]{:S(2)}) collective-permute-start(bf16[8,4,96,128]{3,2,1,0:T(8,128)(2,1)S(1)} %bitcast.7), channel_id=1, source_target_pairs={{0,32},{32,0},{1,33},{33,1},{2,34},{34,2},{3,35},{35,3},{4,36},{36... | collective-permute-start | bytes 2359304 | tf_op jit(solution)/shard_map/ppermute | solution.py:363
  59.3 1.8 %copy-start.3 = (f32[128]{0:T(128)S(1)}, f32[128]{0:T(128)}, u32[]{:S(2)}) copy-start(f32[128]{0:T(128)} %param.11) | copy-start | bytes 1540

commit v7 on v4

--- a/solution.py
+++ b/solution.py
@@ -130,7 +130,12 @@
     moves[4].wait()
 
 
-def join_kernel(mine, near, out):
+def tails_kernel(q, near, out):
+    for half in range(2):
+        out[half] = q[(half + 1) * SPAN - EDGE : (half + 1) * SPAN]
+
+
+def join_kernel(mine, near, query_conv, out):
     out[:64] = mine[...]
     out[64:] = near[...]
 
@@ -384,9 +389,14 @@
     )(keys_values.T, pair_taps, jnp.asarray(dct_tile()))
     gathered = lax.all_to_all(blocks, CHIPS + GROUP, 0, 0, tiled=True)
     near = swapped(conv, "y_hi")
-    far = call(join_kernel, "join", shape(128, ROWS), (conv, near), flops=1 << 37)
-    far = swapped(far, "z_lo")
-    tails = jnp.stack([queries[e - EDGE : e] for e in (SPAN, ROWS)])
+    tails = call(
+        tails_kernel,
+        "tails",
+        shape(2, EDGE, BLOCK),
+        (queries, near),
+        (VMEM, pl.ANY),
+        flops=1 << 37,
+    )
     swap = swapped(tails, "core")
     hop = lax.ppermute(
         tails, CTX, [(i, i + 1) for i in range(1, 15, 2)] + [(i + 1, i) for i in range(1, 15, 2)]
@@ -397,6 +407,10 @@
         shape(ROWS, HEAD_CHANNELS),
         (queries, tails, swap, hop, query_taps),
     )
+    joined = call(
+        join_kernel, "join", shape(128, ROWS), (conv, near, query_conv), (VMEM, VMEM, pl.ANY)
+    )
+    far = swapped(joined, "z_lo")
     gathered, query_conv = lax.optimization_barrier((gathered, query_conv))
     far_own = gathered.reshape(8, 4, SENT, BLOCK)
     far_other = swapped(far_own, "core")

time: 42.1 us -> 40.3 us (0.957)
  the two profiles are of different devices: /device:TPU:1 before, /device:TPU:9 now
where the time goes in v7:
time: 40.3 us; the launch traced here: 39.9 us
  starting transfers between devices  25.3 us (63%)
  Pallas kernels  7.19 us (18%)
  waiting for transfers between devices  6.59 us (16%)
  local copies, waits for them, and re-layouts  0.66 us (2%)
    ppermute x4, starting transfers between devices, swapped(): return lax.ppermute(value, axis, [(0, 1), (1, 0)])  12.6 us
    all_to_all x1, starting transfers between devices, per_device(): gathered = lax.all_to_all(blocks, CHIPS + GROUP, 0, 0, tiled=True)  7.24 us
    ppermute x1, starting transfers between devices, per_device(): lax.ppermute(tails, CTX, [(i, i + 1) for i in range(1, 15, 2)] + [(i + 1,...  5.47 us
    pallas_call x5, Pallas kernels, call(): pl.pallas_call(kernel, out_shape=out_shape, in_specs=[spec(s) for s in sp...  4.75 us
    ppermute x4, waiting for transfers between devices, swapped(): return lax.ppermute(value, axis, [(0, 1), (1, 0)])  3.8 us
    ppermute x1, waiting for transfers between devices, per_device(): lax.ppermute(tails, CTX, [(i, i + 1) for i in range(1, 15, 2)] + [(i + 1,...  2.79 us
    pallas_call x1, Pallas kernels, per_device(): pl.pallas_call(conv_kernel, out_shape=(shape(64, ROWS), shape(32, SENT, B...  2.44 us
  transfers between devices with their start and end apart: 6, of which 2 were waited for; matrix products, arithmetic and copies ran while one was open for 0% of the time, Pallas kernels for 1%

profile of v7, /device:TPU:9, one launch (start us, length us, event | category | flops | bytes accessed | tf_op | source)
XLA Modules:
  0.0 39.9 jit_solution(2525666695375799121)
XLA Ops:
  0.0 2.4 %conv.1 = (bf16[64,1024]{1,0:T(8,128)(2,1)}, bf16[32,96,128]{2,1,0:T(8,128)(2,1)}) custom-call(bf16[64,1024]{1,0:T(8,128)(2,1)} %bitcast.6, f32[4,64]{1,0:T(4,128)} %taps_in.1, bf16[128,128]{1,0:T(8,128)(2,1)} %constant.4.clone.table_in), custom_call_target="tpu_custom_call" | custom-call | flops 16777216 | bytes 1048576 | tf_op jit(solution)/shard_map/conv/pallas_call | solution.py:373
  2.5 3.9 %collective-permute-start = (bf16[64,1024]{1,0:T(8,128)(2,1)}, bf16[64,1024]{1,0:T(8,128)(2,1)S(1)}, u32[]{:S(2)}, u32[]{:S(2)}) collective-permute-start(bf16[64,1024]{1,0:T(8,128)(2,1)} %get-tuple-element.10.mine), channel_id=1, source_target_pairs={{0,1},{1,0},{2,3},{3,2},{4,5},{5,4},{6,7},{7,6},{8,9},{9,8},{10,11... | collective-permute-start | bytes 393224 | tf_op jit(solution)/shard_map/ppermute | solution.py:353
  6.4 0.0 copy-start
  6.4 7.2 %all-to-all-start = ((bf16[32,96,128]{2,1,0:T(8,128)(2,1)}), bf16[32,96,128]{2,1,0:T(8,128)(2,1)S(1)}, u32[]{:S(2)}, u32[]{:S(2)}) async-start(bf16[32,96,128]{2,1,0:T(8,128)(2,1)} %get-tuple-element.9), calls=%async_computation | async-start | bytes 1572864 | tf_op jit(solution)/shard_map/all_to_all | solution.py:390
  13.6 0.0 copy-start.2
  13.7 0.0 collective-permute-done.near
  13.7 0.0 copy-done
  13.7 0.0 copy-start.1
  13.7 5.5 %collective-permute-start.2 = (bf16[2,16,128]{2,1,0:T(8,128)(2,1)S(1)}, bf16[2,16,128]{2,1,0:T(8,128)(2,1)S(1)}, u32[]{:S(2)}, u32[]{:S(2)}) collective-permute-start(bf16[2,16,128]{2,1,0:T(8,128)(2,1)S(1)} %tails.1.own), channel_id=1, source_target_pairs={{32,64},{96,128},{160,192},{224,256},{288,320},{352,384},{416,448}... | collective-permute-start | bytes 24584 | tf_op jit(solution)/shard_map/ppermute | solution.py:401
  19.2 1.9 %collective-permute-start.1 = (bf16[2,16,128]{2,1,0:T(8,128)(2,1)S(1)}, bf16[2,16,128]{2,1,0:T(8,128)(2,1)S(1)}, u32[]{:S(2)}, u32[]{:S(2)}) collective-permute-start(bf16[2,16,128]{2,1,0:T(8,128)(2,1)S(1)} %tails.1.own), channel_id=1, source_target_pairs={{0,32},{32,0},{1,33},{33,1},{2,34},{34,2},{3,35},{35,3},{4,36},{36... | collective-permute-start | bytes 24584 | tf_op jit(solution)/shard_map/ppermute | solution.py:353
  21.1 2.8 %collective-permute-done.2.hop = bf16[2,16,128]{2,1,0:T(8,128)(2,1)S(1)} collective-permute-done((bf16[2,16,128]{2,1,0:T(8,128)(2,1)S(1)}, bf16[2,16,128]{2,1,0:T(8,128)(2,1)S(1)}, u32[]{:S(2)}, u32[]{:S(2)}) %collective-permute-start.2) | collective-permute-done | bytes 8224 | tf_op jit(solution)/shard_map/ppermute | solution.py:401
  23.9 0.0 collective-permute-done.1.swap
  23.9 0.0 copy-done.2
  23.9 0.3 queries.1.query_conv.q
  24.2 0.0 copy-done.1
  24.2 3.9 %collective-permute-start.3 = (bf16[128,1024]{1,0:T(8,128)(2,1)S(1)}, bf16[128,1024]{1,0:T(8,128)(2,1)S(1)}, u32[]{:S(2)}, u32[]{:S(2)}) collective-permute-start(bf16[128,1024]{1,0:T(8,128)(2,1)S(1)} %join.1), channel_id=1, source_target_pairs={{0,2},{2,0},{1,3},{3,1},{4,6},{6,4},{5,7},{7,5},{8,10},{10,8},{9,1... | collective-permute-start | bytes 786440 | tf_op jit(solution)/shard_map/ppermute | solution.py:353
  28.1 0.0 all-to-all-done
  28.1 0.0 copy-start.4
  28.1 2.9 %collective-permute-start.4 = (bf16[8,4,96,128]{3,2,1,0:T(8,128)(2,1)S(1)}, bf16[8,4,96,128]{3,2,1,0:T(8,128)(2,1)S(1)}, u32[]{:S(2)}, u32[]{:S(2)}) collective-permute-start(bf16[8,4,96,128]{3,2,1,0:T(8,128)(2,1)S(1)} %bitcast.3), channel_id=1, source_target_pairs={{0,32},{32,0},{1,33},{33,1},{2,34},{34,2},{3,35},{35,3},{4,36},{36... | collective-permute-start | bytes 2359304 | tf_op jit(solution)/shard_map/ppermute | solution.py:353
  31.0 3.8 %collective-permute-done.3.far = bf16[128,1024]{1,0:T(8,128)(2,1)S(1)} collective-permute-done((bf16[128,1024]{1,0:T(8,128)(2,1)S(1)}, bf16[128,1024]{1,0:T(8,128)(2,1)S(1)}, u32[]{:S(2)}, u32[]{:S(2)}) %collective-permute-start.3) | collective-permute-done | bytes 262176 | tf_op jit(solution)/shard_map/ppermute | solution.py:353
  34.8 0.0 copy-start.3
  34.9 0.0 collective-permute-done.4.far_other
  34.9 0.0 copy-done.4
  34.9 0.6 %copy-done.3 = f32[128]{0:T(128)S(1)} copy-done((f32[128]{0:T(128)S(1)}, f32[128]{0:T(128)}, u32[]{:S(2)}) %copy-start.3) | copy-done | bytes 536
  35.5 4.4 %attend.1 = bf16[1024,128]{1,0:T(8,128)(2,1)} custom-call(bf16[1024,128]{1,0:T(8,128)(2,1)S(1)} %queries.1.query_conv.q, bf16[4,64,1024]{2,1,0:T(8,128)(2,1)S(1)} %pairs.1, bf16[8,4,96,128]{3,2,1,0:T(8,128)(2,1)S(1)} %bitcast.4, bf16[8,4,96,128]{3,2,1,0:T(8,128)(2,1)S(1)} %collective-permute-done.4.far_other, bf16[128,2048]{1,0:T(8,128)(2,1)S(1)} %copy-done.4, ...), custom_call_target="tpu_custom_call" | custom-call | flops 1073741824 | bytes 1048576 | tf_op jit(solution)/shard_map/attend/pallas_call | solution.py:359
  (3 shorter events, 0.1 us)
Async XLA Ops:
  2.5 11.2 %collective-permute-start = (bf16[64,1024]{1,0:T(8,128)(2,1)}, bf16[64,1024]{1,0:T(8,128)(2,1)S(1)}, u32[]{:S(2)}, u32[]{:S(2)}) collective-permute-start(bf16[64,1024]{1,0:T(8,128)(2,1)} %get-tuple-element.10.mine), channel_id=1, source_target_pairs={{0,1},{1,0},{2,3},{3,2},{4,5},{5,4},{6,7},{7,6},{8,9},{9,8},{10,11... | collective-permute-start | bytes 393224 | tf_op jit(solution)/shard_map/ppermute | solution.py:353
  6.4 7.3 %copy-start = (bf16[1024,128]{1,0:T(8,128)(2,1)S(1)}, bf16[1024,128]{1,0:T(8,128)(2,1)}, u32[]{:S(2)}) copy-start(bf16[1024,128]{1,0:T(8,128)(2,1)} %q.3) | copy-start | bytes 786436
  6.4 21.7 %all-to-all-start = ((bf16[32,96,128]{2,1,0:T(8,128)(2,1)}), bf16[32,96,128]{2,1,0:T(8,128)(2,1)S(1)}, u32[]{:S(2)}, u32[]{:S(2)}) async-start(bf16[32,96,128]{2,1,0:T(8,128)(2,1)} %get-tuple-element.9), calls=%async_computation | async-start | bytes 1572864 | tf_op jit(solution)/shard_map/all_to_all | solution.py:390
  13.6 10.3 %copy-start.2 = (f32[4,128]{1,0:T(4,128)S(1)}, f32[4,128]{1,0:T(4,128)}, u32[]{:S(2)}) copy-start(f32[4,128]{1,0:T(4,128)} %taps.1) | copy-start | bytes 6148
  13.7 10.5 %copy-start.1 = (bf16[64,1024]{1,0:T(8,128)(2,1)S(1)}, bf16[64,1024]{1,0:T(8,128)(2,1)}, u32[]{:S(2)}) copy-start(bf16[64,1024]{1,0:T(8,128)(2,1)} %get-tuple-element.10.mine) | copy-start | bytes 393220
  13.7 10.2 %collective-permute-start.2 = (bf16[2,16,128]{2,1,0:T(8,128)(2,1)S(1)}, bf16[2,16,128]{2,1,0:T(8,128)(2,1)S(1)}, u32[]{:S(2)}, u32[]{:S(2)}) collective-permute-start(bf16[2,16,128]{2,1,0:T(8,128)(2,1)S(1)} %tails.1.own), channel_id=1, source_target_pairs={{32,64},{96,128},{160,192},{224,256},{288,320},{352,384},{416,448}... | collective-permute-start | bytes 24584 | tf_op jit(solution)/shard_map/ppermute | solution.py:401
  19.2 4.7 %collective-permute-start.1 = (bf16[2,16,128]{2,1,0:T(8,128)(2,1)S(1)}, bf16[2,16,128]{2,1,0:T(8,128)(2,1)S(1)}, u32[]{:S(2)}, u32[]{:S(2)}) collective-permute-start(bf16[2,16,128]{2,1,0:T(8,128)(2,1)S(1)} %tails.1.own), channel_id=1, source_target_pairs={{0,32},{32,0},{1,33},{33,1},{2,34},{34,2},{3,35},{35,3},{4,36},{36... | collective-permute-start | bytes 24584 | tf_op jit(solution)/shard_map/ppermute | solution.py:353
  24.2 10.6 %collective-permute-start.3 = (bf16[128,1024]{1,0:T(8,128)(2,1)S(1)}, bf16[128,1024]{1,0:T(8,128)(2,1)S(1)}, u32[]{:S(2)}, u32[]{:S(2)}) collective-permute-start(bf16[128,1024]{1,0:T(8,128)(2,1)S(1)} %join.1), channel_id=1, source_target_pairs={{0,2},{2,0},{1,3},{3,1},{4,6},{6,4},{5,7},{7,5},{8,10},{10,8},{9,1... | collective-permute-start | bytes 786440 | tf_op jit(solution)/shard_map/ppermute | solution.py:353
  28.1 6.8 %copy-start.4 = (bf16[128,2048]{1,0:T(8,128)(2,1)S(1)}, bf16[128,2048]{1,0:T(8,128)(2,1)}, u32[]{:S(2)}) copy-start(bf16[128,2048]{1,0:T(8,128)(2,1)} %constant.5.clone.table) | copy-start | bytes 1572868
  28.1 6.7 %collective-permute-start.4 = (bf16[8,4,96,128]{3,2,1,0:T(8,128)(2,1)S(1)}, bf16[8,4,96,128]{3,2,1,0:T(8,128)(2,1)S(1)}, u32[]{:S(2)}, u32[]{:S(2)}) collective-permute-start(bf16[8,4,96,128]{3,2,1,0:T(8,128)(2,1)S(1)} %bitcast.3), channel_id=1, source_target_pairs={{0,32},{32,0},{1,33},{33,1},{2,34},{34,2},{3,35},{35,3},{4,36},{36... | collective-permute-start | bytes 2359304 | tf_op jit(solution)/shard_map/ppermute | solution.py:353
  34.8 0.7 %copy-start.3 = (f32[128]{0:T(128)S(1)}, f32[128]{0:T(128)}, u32[]{:S(2)}) copy-start(f32[128]{0:T(128)} %param.11) | copy-start | bytes 1540

commit v8 on v7

--- a/solution.py
+++ b/solution.py
@@ -140,7 +140,8 @@
     out[64:] = near[...]
 
 
-def query_kernel(q, own, swap, hop, taps, out):
+def query_kernel(q, own, swap, hop, taps, gain, out, gain_out):
+    gain_out[...] = gain[...]
     place = lax.axis_index(CTX)
     odd = place % 2 == 1
     own, swap, hop = own[...].astype(F32), swap[...].astype(F32), hop[...].astype(F32)
@@ -401,11 +402,11 @@
     hop = lax.ppermute(
         tails, CTX, [(i, i + 1) for i in range(1, 15, 2)] + [(i + 1, i) for i in range(1, 15, 2)]
     )
-    query_conv = call(
+    query_conv, gain = call(
         query_kernel,
         "queries",
-        shape(ROWS, HEAD_CHANNELS),
-        (queries, tails, swap, hop, query_taps),
+        (shape(ROWS, HEAD_CHANNELS), jax.ShapeDtypeStruct((1, HEAD_CHANNELS), F32)),
+        (queries, tails, swap, hop, query_taps, out_gain.reshape(1, -1)),
     )
     joined = call(
         join_kernel, "join", shape(128, ROWS), (conv, near, query_conv), (VMEM, VMEM, pl.ANY)
@@ -419,7 +420,7 @@
         attend_kernel,
         "attend",
         shape(ROWS, HEAD_CHANNELS),
-        (query_conv, pairs, far_own, far_other, jnp.asarray(head_tables()), out_gain.reshape(1, -1)),
+        (query_conv, pairs, far_own, far_other, jnp.asarray(head_tables()), gain),
         scratch=[
             VMEM((2, 2, 8, HEAD_CHANNELS, BLOCK), BF16),
             VMEM((19, CHUNK, BLOCK), F32),

time: 40.3 us -> 40.3 us (level)
  waiting for transfers between devices: 6.59 us -> 7.3 us
  starting transfers between devices: 25.3 us -> 24.6 us
    ppermute x4, waiting for transfers between devices: 3.8 us -> 4.37 us  [swapped(): return lax.ppermute(value, axis, [(0, 1), (1, 0)])]
    ppermute x4, starting transfers between devices: 12.6 us -> 12 us  [swapped(): return lax.ppermute(value, axis, [(0, 1), (1, 0)])]
where the time goes in v8:
time: 40.3 us; the launch traced here: 40 us
  starting transfers between devices  24.6 us (61%)
  waiting for transfers between devices  7.3 us (18%)
  Pallas kernels  7.24 us (18%)
  local copies, waits for them, and re-layouts  0.66 us (2%)
    ppermute x4, starting transfers between devices, swapped(): return lax.ppermute(value, axis, [(0, 1), (1, 0)])  12 us
    all_to_all x1, starting transfers between devices, per_device(): gathered = lax.all_to_all(blocks, CHIPS + GROUP, 0, 0, tiled=True)  7.24 us
    ppermute x1, starting transfers between devices, per_device(): lax.ppermute(tails, CTX, [(i, i + 1) for i in range(1, 15, 2)] + [(i + 1,...  5.34 us
    pallas_call x5, Pallas kernels, call(): pl.pallas_call(kernel, out_shape=out_shape, in_specs=[spec(s) for s in sp...  4.78 us
    ppermute x4, waiting for transfers between devices, swapped(): return lax.ppermute(value, axis, [(0, 1), (1, 0)])  4.37 us
    ppermute x1, waiting for transfers between devices, per_device(): lax.ppermute(tails, CTX, [(i, i + 1) for i in range(1, 15, 2)] + [(i + 1,...  2.92 us
    pallas_call x1, Pallas kernels, per_device(): pl.pallas_call(conv_kernel, out_shape=(shape(64, ROWS), shape(32, SENT, B...  2.46 us
  transfers between devices with their start and end apart: 6, of which 2 were waited for; matrix products, arithmetic and copies ran while one was open for 0% of the time, Pallas kernels for 1%

profile of v8, /device:TPU:9, one launch (start us, length us, event | category | flops | bytes accessed | tf_op | source)
XLA Modules:
  0.0 40.0 jit_solution(4752912633076431117)
XLA Ops:
  0.0 2.5 %conv.1 = (bf16[64,1024]{1,0:T(8,128)(2,1)}, bf16[32,96,128]{2,1,0:T(8,128)(2,1)}) custom-call(bf16[64,1024]{1,0:T(8,128)(2,1)} %bitcast.6, f32[4,64]{1,0:T(4,128)} %taps_in.1, bf16[128,128]{1,0:T(8,128)(2,1)} %constant.4.clone.table_in), custom_call_target="tpu_custom_call" | custom-call | flops 16777216 | bytes 1048576 | tf_op jit(solution)/shard_map/conv/pallas_call | solution.py:374
  2.5 3.9 %collective-permute-start = (bf16[64,1024]{1,0:T(8,128)(2,1)}, bf16[64,1024]{1,0:T(8,128)(2,1)S(1)}, u32[]{:S(2)}, u32[]{:S(2)}) collective-permute-start(bf16[64,1024]{1,0:T(8,128)(2,1)} %get-tuple-element.12.mine), channel_id=1, source_target_pairs={{0,1},{1,0},{2,3},{3,2},{4,5},{5,4},{6,7},{7,6},{8,9},{9,8},{10,11... | collective-permute-start | bytes 393224 | tf_op jit(solution)/shard_map/ppermute | solution.py:354
  6.4 0.0 copy-start
  6.4 7.2 %all-to-all-start = ((bf16[32,96,128]{2,1,0:T(8,128)(2,1)}), bf16[32,96,128]{2,1,0:T(8,128)(2,1)S(1)}, u32[]{:S(2)}, u32[]{:S(2)}) async-start(bf16[32,96,128]{2,1,0:T(8,128)(2,1)} %get-tuple-element.11), calls=%async_computation | async-start | bytes 1572864 | tf_op jit(solution)/shard_map/all_to_all | solution.py:391
  13.7 0.0 collective-permute-done.near
  13.7 0.0 copy-done
  13.7 0.0 copy-start.2
  13.7 0.0 copy-start.3
  13.7 5.3 %collective-permute-start.2 = (bf16[2,16,128]{2,1,0:T(8,128)(2,1)S(1)}, bf16[2,16,128]{2,1,0:T(8,128)(2,1)S(1)}, u32[]{:S(2)}, u32[]{:S(2)}) collective-permute-start(bf16[2,16,128]{2,1,0:T(8,128)(2,1)S(1)} %tails.1.own), channel_id=1, source_target_pairs={{32,64},{96,128},{160,192},{224,256},{288,320},{352,384},{416,448}... | collective-permute-start | bytes 24584 | tf_op jit(solution)/shard_map/ppermute | solution.py:402
  19.1 1.9 %collective-permute-start.1 = (bf16[2,16,128]{2,1,0:T(8,128)(2,1)S(1)}, bf16[2,16,128]{2,1,0:T(8,128)(2,1)S(1)}, u32[]{:S(2)}, u32[]{:S(2)}) collective-permute-start(bf16[2,16,128]{2,1,0:T(8,128)(2,1)S(1)} %tails.1.own), channel_id=1, source_target_pairs={{0,32},{32,0},{1,33},{33,1},{2,34},{34,2},{3,35},{35,3},{4,36},{36... | collective-permute-start | bytes 24584 | tf_op jit(solution)/shard_map/ppermute | solution.py:354
  21.0 2.9 %collective-permute-done.2.hop = bf16[2,16,128]{2,1,0:T(8,128)(2,1)S(1)} collective-permute-done((bf16[2,16,128]{2,1,0:T(8,128)(2,1)S(1)}, bf16[2,16,128]{2,1,0:T(8,128)(2,1)S(1)}, u32[]{:S(2)}, u32[]{:S(2)}) %collective-permute-start.2) | collective-permute-done | bytes 8224 | tf_op jit(solution)/shard_map/ppermute | solution.py:402
  23.9 0.0 collective-permute-done.1.swap
  23.9 0.0 copy-done.2
  23.9 0.0 copy-done.3
  23.9 0.0 copy-start.1
  23.9 0.3 queries.1
  24.2 0.6 %copy-done.1 = bf16[64,1024]{1,0:T(8,128)(2,1)S(1)} copy-done((bf16[64,1024]{1,0:T(8,128)(2,1)S(1)}, bf16[64,1024]{1,0:T(8,128)(2,1)}, u32[]{:S(2)}) %copy-start.1) | copy-done | bytes 131096
  24.9 3.9 %collective-permute-start.3 = (bf16[128,1024]{1,0:T(8,128)(2,1)S(1)}, bf16[128,1024]{1,0:T(8,128)(2,1)S(1)}, u32[]{:S(2)}, u32[]{:S(2)}) collective-permute-start(bf16[128,1024]{1,0:T(8,128)(2,1)S(1)} %join.1), channel_id=1, source_target_pairs={{0,2},{2,0},{1,3},{3,1},{4,6},{6,4},{5,7},{7,5},{8,10},{10,8},{9,1... | collective-permute-start | bytes 786440 | tf_op jit(solution)/shard_map/ppermute | solution.py:354
  28.7 0.0 all-to-all-done
  28.8 0.0 copy-start.4
  28.8 2.3 %collective-permute-start.4 = (bf16[8,4,96,128]{3,2,1,0:T(8,128)(2,1)S(1)}, bf16[8,4,96,128]{3,2,1,0:T(8,128)(2,1)S(1)}, u32[]{:S(2)}, u32[]{:S(2)}) collective-permute-start(bf16[8,4,96,128]{3,2,1,0:T(8,128)(2,1)S(1)} %bitcast.3), channel_id=1, source_target_pairs={{0,32},{32,0},{1,33},{33,1},{2,34},{34,2},{3,35},{35,3},{4,36},{36... | collective-permute-start | bytes 2359304 | tf_op jit(solution)/shard_map/ppermute | solution.py:354
  31.1 4.4 %collective-permute-done.3.far = bf16[128,1024]{1,0:T(8,128)(2,1)S(1)} collective-permute-done((bf16[128,1024]{1,0:T(8,128)(2,1)S(1)}, bf16[128,1024]{1,0:T(8,128)(2,1)S(1)}, u32[]{:S(2)}, u32[]{:S(2)}) %collective-permute-start.3) | collective-permute-done | bytes 262176 | tf_op jit(solution)/shard_map/ppermute | solution.py:354
  35.5 0.0 collective-permute-done.4.far_other
  35.5 0.0 copy-done.4
  35.5 4.5 %attend.1 = bf16[1024,128]{1,0:T(8,128)(2,1)} custom-call(bf16[1024,128]{1,0:T(8,128)(2,1)S(1)} %get-tuple-element.14.query_conv.q, bf16[4,64,1024]{2,1,0:T(8,128)(2,1)S(1)} %pairs.1, bf16[8,4,96,128]{3,2,1,0:T(8,128)(2,1)S(1)} %bitcast.4, bf16[8,4,96,128]{3,2,1,0:T(8,128)(2,1)S(1)} %collective-permute-done.4.far_other, bf16[128,2048]{1,0:T(8,128)(2,1)S(1)} %copy-done.4, ...), custom_call_target="tpu_custom_call" | custom-call | flops 1073741824 | bytes 1048576 | tf_op jit(solution)/shard_map/attend/pallas_call | solution.py:360
  (3 shorter events, 0.1 us)
Async XLA Ops:
  2.5 11.2 %collective-permute-start = (bf16[64,1024]{1,0:T(8,128)(2,1)}, bf16[64,1024]{1,0:T(8,128)(2,1)S(1)}, u32[]{:S(2)}, u32[]{:S(2)}) collective-permute-start(bf16[64,1024]{1,0:T(8,128)(2,1)} %get-tuple-element.12.mine), channel_id=1, source_target_pairs={{0,1},{1,0},{2,3},{3,2},{4,5},{5,4},{6,7},{7,6},{8,9},{9,8},{10,11... | collective-permute-start | bytes 393224 | tf_op jit(solution)/shard_map/ppermute | solution.py:354
  6.4 7.3 %copy-start = (bf16[1024,128]{1,0:T(8,128)(2,1)S(1)}, bf16[1024,128]{1,0:T(8,128)(2,1)}, u32[]{:S(2)}) copy-start(bf16[1024,128]{1,0:T(8,128)(2,1)} %q.3) | copy-start | bytes 786436
  6.4 22.3 %all-to-all-start = ((bf16[32,96,128]{2,1,0:T(8,128)(2,1)}), bf16[32,96,128]{2,1,0:T(8,128)(2,1)S(1)}, u32[]{:S(2)}, u32[]{:S(2)}) async-start(bf16[32,96,128]{2,1,0:T(8,128)(2,1)} %get-tuple-element.11), calls=%async_computation | async-start | bytes 1572864 | tf_op jit(solution)/shard_map/all_to_all | solution.py:391
  13.7 10.2 %copy-start.2 = (f32[4,128]{1,0:T(4,128)S(1)}, f32[4,128]{1,0:T(4,128)}, u32[]{:S(2)}) copy-start(f32[4,128]{1,0:T(4,128)} %taps.1) | copy-start | bytes 6148
  13.7 10.2 %copy-start.3 = (f32[128]{0:T(128)S(1)}, f32[128]{0:T(128)}, u32[]{:S(2)}) copy-start(f32[128]{0:T(128)} %param.11) | copy-start | bytes 1540
  13.7 10.2 %collective-permute-start.2 = (bf16[2,16,128]{2,1,0:T(8,128)(2,1)S(1)}, bf16[2,16,128]{2,1,0:T(8,128)(2,1)S(1)}, u32[]{:S(2)}, u32[]{:S(2)}) collective-permute-start(bf16[2,16,128]{2,1,0:T(8,128)(2,1)S(1)} %tails.1.own), channel_id=1, source_target_pairs={{32,64},{96,128},{160,192},{224,256},{288,320},{352,384},{416,448}... | collective-permute-start | bytes 24584 | tf_op jit(solution)/shard_map/ppermute | solution.py:402
  19.1 4.9 %collective-permute-start.1 = (bf16[2,16,128]{2,1,0:T(8,128)(2,1)S(1)}, bf16[2,16,128]{2,1,0:T(8,128)(2,1)S(1)}, u32[]{:S(2)}, u32[]{:S(2)}) collective-permute-start(bf16[2,16,128]{2,1,0:T(8,128)(2,1)S(1)} %tails.1.own), channel_id=1, source_target_pairs={{0,32},{32,0},{1,33},{33,1},{2,34},{34,2},{3,35},{35,3},{4,36},{36... | collective-permute-start | bytes 24584 | tf_op jit(solution)/shard_map/ppermute | solution.py:354
  23.9 0.9 %copy-start.1 = (bf16[64,1024]{1,0:T(8,128)(2,1)S(1)}, bf16[64,1024]{1,0:T(8,128)(2,1)}, u32[]{:S(2)}) copy-start(bf16[64,1024]{1,0:T(8,128)(2,1)} %get-tuple-element.12.mine) | copy-start | bytes 393220
  24.9 10.6 %collective-permute-start.3 = (bf16[128,1024]{1,0:T(8,128)(2,1)S(1)}, bf16[128,1024]{1,0:T(8,128)(2,1)S(1)}, u32[]{:S(2)}, u32[]{:S(2)}) collective-permute-start(bf16[128,1024]{1,0:T(8,128)(2,1)S(1)} %join.1), channel_id=1, source_target_pairs={{0,2},{2,0},{1,3},{3,1},{4,6},{6,4},{5,7},{7,5},{8,10},{10,8},{9,1... | collective-permute-start | bytes 786440 | tf_op jit(solution)/shard_map/ppermute | solution.py:354
  28.8 6.7 %copy-start.4 = (bf16[128,2048]{1,0:T(8,128)(2,1)S(1)}, bf16[128,2048]{1,0:T(8,128)(2,1)}, u32[]{:S(2)}) copy-start(bf16[128,2048]{1,0:T(8,128)(2,1)} %constant.5.clone.table) | copy-start | bytes 1572868
  28.8 6.7 %collective-permute-start.4 = (bf16[8,4,96,128]{3,2,1,0:T(8,128)(2,1)S(1)}, bf16[8,4,96,128]{3,2,1,0:T(8,128)(2,1)S(1)}, u32[]{:S(2)}, u32[]{:S(2)}) collective-permute-start(bf16[8,4,96,128]{3,2,1,0:T(8,128)(2,1)S(1)} %bitcast.3), channel_id=1, source_target_pairs={{0,32},{32,0},{1,33},{33,1},{2,34},{34,2},{3,35},{35,3},{4,36},{36... | collective-permute-start | bytes 2359304 | tf_op jit(solution)/shard_map/ppermute | solution.py:354

commit v9 on v8

--- a/solution.py
+++ b/solution.py
@@ -130,7 +130,7 @@
     moves[4].wait()
 
 
-def tails_kernel(q, near, out):
+def tails_kernel(q, near, conv, out):
     for half in range(2):
         out[half] = q[(half + 1) * SPAN - EDGE : (half + 1) * SPAN]
 
@@ -394,8 +394,8 @@
         tails_kernel,
         "tails",
         shape(2, EDGE, BLOCK),
-        (queries, near),
-        (VMEM, pl.ANY),
+        (queries, near, conv),
+        (VMEM, pl.ANY, VMEM),
         flops=1 << 37,
     )
     swap = swapped(tails, "core")

time: 40.3 us -> 39.7 us (0.985)
  the two profiles are of different devices: /device:TPU:9 before, /device:TPU:1 now
where the time goes in v9:
time: 39.7 us; the launch traced here: 39.1 us
  starting transfers between devices  27 us (68%)
  Pallas kernels  7.22 us (18%)
  waiting for transfers between devices  4.76 us (12%)
    ppermute x4, starting transfers between devices, swapped(): return lax.ppermute(value, axis, [(0, 1), (1, 0)])  15.2 us
    all_to_all x1, starting transfers between devices, per_device(): gathered = lax.all_to_all(blocks, CHIPS + GROUP, 0, 0, tiled=True)  6.4 us
    ppermute x1, starting transfers between devices, per_device(): lax.ppermute(tails, CTX, [(i, i + 1) for i in range(1, 15, 2)] + [(i + 1,...  5.38 us
    pallas_call x5, Pallas kernels, call(): pl.pallas_call(kernel, out_shape=out_shape, in_specs=[spec(s) for s in sp...  4.76 us
    ppermute x1, waiting for transfers between devices, per_device(): lax.ppermute(tails, CTX, [(i, i + 1) for i in range(1, 15, 2)] + [(i + 1,...  2.91 us
    pallas_call x1, Pallas kernels, per_device(): pl.pallas_call(conv_kernel, out_shape=(shape(64, ROWS), shape(32, SENT, B...  2.46 us
    ppermute x4, waiting for transfers between devices, swapped(): return lax.ppermute(value, axis, [(0, 1), (1, 0)])  1.84 us
  transfers between devices with their start and end apart: 6, of which 3 were waited for; matrix products, arithmetic and copies ran while one was open for 0% of the time, Pallas kernels for 1%

profile of v9, /device:TPU:1, one launch (start us, length us, event | category | flops | bytes accessed | tf_op | source)
XLA Modules:
  0.0 39.1 jit_solution(14393568992649505468)
XLA Ops:
  0.0 2.5 %conv.1 = (bf16[64,1024]{1,0:T(8,128)(2,1)}, bf16[32,96,128]{2,1,0:T(8,128)(2,1)}) custom-call(bf16[64,1024]{1,0:T(8,128)(2,1)} %bitcast.6, f32[4,64]{1,0:T(4,128)} %taps_in.1, bf16[128,128]{1,0:T(8,128)(2,1)} %constant.4.clone.table_in), custom_call_target="tpu_custom_call" | custom-call | flops 16777216 | bytes 1048576 | tf_op jit(solution)/shard_map/conv/pallas_call | solution.py:374
  2.5 5.7 %collective-permute-start = (bf16[64,1024]{1,0:T(8,128)(2,1)}, bf16[64,1024]{1,0:T(8,128)(2,1)S(1)}, u32[]{:S(2)}, u32[]{:S(2)}) collective-permute-start(bf16[64,1024]{1,0:T(8,128)(2,1)} %get-tuple-element.12.conv.mine), channel_id=1, source_target_pairs={{0,1},{1,0},{2,3},{3,2},{4,5},{5,4},{6,7},{7,6},{8,9},{9,8},{10,11... | collective-permute-start | bytes 393224 | tf_op jit(solution)/shard_map/ppermute | solution.py:354
  8.1 0.0 copy-start
  8.1 0.0 copy-start.1
  8.2 6.4 %all-to-all-start = ((bf16[32,96,128]{2,1,0:T(8,128)(2,1)}), bf16[32,96,128]{2,1,0:T(8,128)(2,1)S(1)}, u32[]{:S(2)}, u32[]{:S(2)}) async-start(bf16[32,96,128]{2,1,0:T(8,128)(2,1)} %get-tuple-element.11), calls=%async_computation | async-start | bytes 1572864 | tf_op jit(solution)/shard_map/all_to_all | solution.py:391
  14.6 0.0 collective-permute-done.near
  14.6 0.0 copy-done
  14.6 0.0 copy-done.1
  14.6 0.0 copy-start.2
  14.6 0.0 copy-start.3
  14.6 5.4 %collective-permute-start.2 = (bf16[2,16,128]{2,1,0:T(8,128)(2,1)S(1)}, bf16[2,16,128]{2,1,0:T(8,128)(2,1)S(1)}, u32[]{:S(2)}, u32[]{:S(2)}) collective-permute-start(bf16[2,16,128]{2,1,0:T(8,128)(2,1)S(1)} %tails.1.own), channel_id=1, source_target_pairs={{32,64},{96,128},{160,192},{224,256},{288,320},{352,384},{416,448}... | collective-permute-start | bytes 24584 | tf_op jit(solution)/shard_map/ppermute | solution.py:402
  20.0 1.9 %collective-permute-start.1 = (bf16[2,16,128]{2,1,0:T(8,128)(2,1)S(1)}, bf16[2,16,128]{2,1,0:T(8,128)(2,1)S(1)}, u32[]{:S(2)}, u32[]{:S(2)}) collective-permute-start(bf16[2,16,128]{2,1,0:T(8,128)(2,1)S(1)} %tails.1.own), channel_id=1, source_target_pairs={{0,32},{32,0},{1,33},{33,1},{2,34},{34,2},{3,35},{35,3},{4,36},{36... | collective-permute-start | bytes 24584 | tf_op jit(solution)/shard_map/ppermute | solution.py:354
  21.9 2.9 %collective-permute-done.2.hop = bf16[2,16,128]{2,1,0:T(8,128)(2,1)S(1)} collective-permute-done((bf16[2,16,128]{2,1,0:T(8,128)(2,1)S(1)}, bf16[2,16,128]{2,1,0:T(8,128)(2,1)S(1)}, u32[]{:S(2)}, u32[]{:S(2)}) %collective-permute-start.2) | collective-permute-done | bytes 8224 | tf_op jit(solution)/shard_map/ppermute | solution.py:402
  24.9 0.0 collective-permute-done.1.swap
  24.9 0.0 copy-done.2
  24.9 0.0 copy-done.3
  24.9 0.3 queries.1
  25.2 3.9 %collective-permute-start.3 = (bf16[128,1024]{1,0:T(8,128)(2,1)S(1)}, bf16[128,1024]{1,0:T(8,128)(2,1)S(1)}, u32[]{:S(2)}, u32[]{:S(2)}) collective-permute-start(bf16[128,1024]{1,0:T(8,128)(2,1)S(1)} %join.1), channel_id=1, source_target_pairs={{0,2},{2,0},{1,3},{3,1},{4,6},{6,4},{5,7},{7,5},{8,10},{10,8},{9,1... | collective-permute-start | bytes 786440 | tf_op jit(solution)/shard_map/ppermute | solution.py:354
  29.0 0.0 all-to-all-done
  29.1 0.0 copy-start.4
  29.1 3.7 %collective-permute-start.4 = (bf16[8,4,96,128]{3,2,1,0:T(8,128)(2,1)S(1)}, bf16[8,4,96,128]{3,2,1,0:T(8,128)(2,1)S(1)}, u32[]{:S(2)}, u32[]{:S(2)}) collective-permute-start(bf16[8,4,96,128]{3,2,1,0:T(8,128)(2,1)S(1)} %bitcast.3), channel_id=1, source_target_pairs={{0,32},{32,0},{1,33},{33,1},{2,34},{34,2},{3,35},{35,3},{4,36},{36... | collective-permute-start | bytes 2359304 | tf_op jit(solution)/shard_map/ppermute | solution.py:354
  32.8 1.1 %collective-permute-done.3.far = bf16[128,1024]{1,0:T(8,128)(2,1)S(1)} collective-permute-done((bf16[128,1024]{1,0:T(8,128)(2,1)S(1)}, bf16[128,1024]{1,0:T(8,128)(2,1)S(1)}, u32[]{:S(2)}, u32[]{:S(2)}) %collective-permute-start.3) | collective-permute-done | bytes 262176 | tf_op jit(solution)/shard_map/ppermute | solution.py:354
  34.0 0.7 %collective-permute-done.4.far_other = bf16[8,4,96,128]{3,2,1,0:T(8,128)(2,1)S(1)} collective-permute-done((bf16[8,4,96,128]{3,2,1,0:T(8,128)(2,1)S(1)}, bf16[8,4,96,128]{3,2,1,0:T(8,128)(2,1)S(1)}, u32[]{:S(2)}, u32[]{:S(2)}) %collective-permute-start.4) | collective-permute-done | bytes 786464 | tf_op jit(solution)/shard_map/ppermute | solution.py:354
  34.7 0.0 copy-done.4
  34.7 4.4 %attend.1 = bf16[1024,128]{1,0:T(8,128)(2,1)} custom-call(bf16[1024,128]{1,0:T(8,128)(2,1)S(1)} %get-tuple-element.14.query_conv.q, bf16[4,64,1024]{2,1,0:T(8,128)(2,1)S(1)} %pairs.1, bf16[8,4,96,128]{3,2,1,0:T(8,128)(2,1)S(1)} %bitcast.4, bf16[8,4,96,128]{3,2,1,0:T(8,128)(2,1)S(1)} %collective-permute-done.4.far_other, bf16[128,2048]{1,0:T(8,128)(2,1)S(1)} %copy-done.4, ...), custom_call_target="tpu_custom_call" | custom-call | flops 1073741824 | bytes 1048576 | tf_op jit(solution)/shard_map/attend/pallas_call | solution.py:360
  (3 shorter events, 0.1 us)
Async XLA Ops:
  2.5 12.1 %collective-permute-start = (bf16[64,1024]{1,0:T(8,128)(2,1)}, bf16[64,1024]{1,0:T(8,128)(2,1)S(1)}, u32[]{:S(2)}, u32[]{:S(2)}) collective-permute-start(bf16[64,1024]{1,0:T(8,128)(2,1)} %get-tuple-element.12.conv.mine), channel_id=1, source_target_pairs={{0,1},{1,0},{2,3},{3,2},{4,5},{5,4},{6,7},{7,6},{8,9},{9,8},{10,11... | collective-permute-start | bytes 393224 | tf_op jit(solution)/shard_map/ppermute | solution.py:354
  8.1 6.4 %copy-start = (bf16[1024,128]{1,0:T(8,128)(2,1)S(1)}, bf16[1024,128]{1,0:T(8,128)(2,1)}, u32[]{:S(2)}) copy-start(bf16[1024,128]{1,0:T(8,128)(2,1)} %q.3) | copy-start | bytes 786436
  8.1 6.4 %copy-start.1 = (bf16[64,1024]{1,0:T(8,128)(2,1)S(1)}, bf16[64,1024]{1,0:T(8,128)(2,1)}, u32[]{:S(2)}) copy-start(bf16[64,1024]{1,0:T(8,128)(2,1)} %get-tuple-element.12.conv.mine) | copy-start | bytes 393220
  8.2 20.9 %all-to-all-start = ((bf16[32,96,128]{2,1,0:T(8,128)(2,1)}), bf16[32,96,128]{2,1,0:T(8,128)(2,1)S(1)}, u32[]{:S(2)}, u32[]{:S(2)}) async-start(bf16[32,96,128]{2,1,0:T(8,128)(2,1)} %get-tuple-element.11), calls=%async_computation | async-start | bytes 1572864 | tf_op jit(solution)/shard_map/all_to_all | solution.py:391
  14.6 10.3 %copy-start.2 = (f32[4,128]{1,0:T(4,128)S(1)}, f32[4,128]{1,0:T(4,128)}, u32[]{:S(2)}) copy-start(f32[4,128]{1,0:T(4,128)} %taps.1) | copy-start | bytes 6148
  14.6 10.2 %copy-start.3 = (f32[128]{0:T(128)S(1)}, f32[128]{0:T(128)}, u32[]{:S(2)}) copy-start(f32[128]{0:T(128)} %param.11) | copy-start | bytes 1540
  14.6 10.2 %collective-permute-start.2 = (bf16[2,16,128]{2,1,0:T(8,128)(2,1)S(1)}, bf16[2,16,128]{2,1,0:T(8,128)(2,1)S(1)}, u32[]{:S(2)}, u32[]{:S(2)}) collective-permute-start(bf16[2,16,128]{2,1,0:T(8,128)(2,1)S(1)} %tails.1.own), channel_id=1, source_target_pairs={{32,64},{96,128},{160,192},{224,256},{288,320},{352,384},{416,448}... | collective-permute-start | bytes 24584 | tf_op jit(solution)/shard_map/ppermute | solution.py:402
  20.0 4.8 %collective-permute-start.1 = (bf16[2,16,128]{2,1,0:T(8,128)(2,1)S(1)}, bf16[2,16,128]{2,1,0:T(8,128)(2,1)S(1)}, u32[]{:S(2)}, u32[]{:S(2)}) collective-permute-start(bf16[2,16,128]{2,1,0:T(8,128)(2,1)S(1)} %tails.1.own), channel_id=1, source_target_pairs={{0,32},{32,0},{1,33},{33,1},{2,34},{34,2},{3,35},{35,3},{4,36},{36... | collective-permute-start | bytes 24584 | tf_op jit(solution)/shard_map/ppermute | solution.py:354
  25.2 8.8 %collective-permute-start.3 = (bf16[128,1024]{1,0:T(8,128)(2,1)S(1)}, bf16[128,1024]{1,0:T(8,128)(2,1)S(1)}, u32[]{:S(2)}, u32[]{:S(2)}) collective-permute-start(bf16[128,1024]{1,0:T(8,128)(2,1)S(1)} %join.1), channel_id=1, source_target_pairs={{0,2},{2,0},{1,3},{3,1},{4,6},{6,4},{5,7},{7,5},{8,10},{10,8},{9,1... | collective-permute-start | bytes 786440 | tf_op jit(solution)/shard_map/ppermute | solution.py:354
  29.1 5.6 %copy-start.4 = (bf16[128,2048]{1,0:T(8,128)(2,1)S(1)}, bf16[128,2048]{1,0:T(8,128)(2,1)}, u32[]{:S(2)}) copy-start(bf16[128,2048]{1,0:T(8,128)(2,1)} %constant.5.clone.table) | copy-start | bytes 1572868
  29.1 5.6 %collective-permute-start.4 = (bf16[8,4,96,128]{3,2,1,0:T(8,128)(2,1)S(1)}, bf16[8,4,96,128]{3,2,1,0:T(8,128)(2,1)S(1)}, u32[]{:S(2)}, u32[]{:S(2)}) collective-permute-start(bf16[8,4,96,128]{3,2,1,0:T(8,128)(2,1)S(1)} %bitcast.3), channel_id=1, source_target_pairs={{0,32},{32,0},{1,33},{33,1},{2,34},{34,2},{3,35},{35,3},{4,36},{36... | collective-permute-start | bytes 2359304 | tf_op jit(solution)/shard_map/ppermute | solution.py:354

commit v10 on v9

--- a/solution.py
+++ b/solution.py
@@ -162,7 +162,7 @@
             out[start : start + BLOCK] = total.astype(BF16)
 
 
-def pairs_kernel(mine, near, far, pairs):
+def pairs_kernel(mine, near, far, edges, pairs):
     member = lax.axis_index(GROUP)
     pairs[member] = mine[...]
     pairs[member ^ 1] = near[...]
@@ -170,7 +170,29 @@
     pairs[member ^ 3] = far[64:]
 
 
-def attend_kernel(q, pairs, far_own, far_other, table, gain, out, packed, scores, ends):
+def block_edges(ref, i, m):
+    tile = ref[i, m, 64 : 64 + EDGE].astype(F32)
+    return tile[:8] + tile[8:]
+
+
+def block_rows(ref, i, m):
+    first_lane = lax.broadcasted_iota(jnp.int32, (EDGE, BLOCK), 1) % (BLOCK // 2) < KEEP
+    rest = ref[i, m, 64 + EDGE :].astype(F32)
+    parts = [rest] + [pltpu.roll(rest, BLOCK - g * KEEP, 1) for g in range(1, 4)]
+    parts = [jnp.where(first_lane, part, 0.0) for part in parts]
+    return ref[i, m, :64].astype(F32) + jnp.concatenate(parts, 0)
+
+
+def own_kernel(far, table, tiles, edges):
+    for i in range(8):
+        for m in range(4):
+            tiles[i, m] = block_rows(far, i, m)
+            edges[i, m] = block_edges(far, i, m)
+
+
+def attend_kernel(
+    q, pairs, own_tiles, own_edges, far_other, table, gain, out, packed, scores, ends
+):
     place = lax.axis_index(CTX)
     middle = place // 2
     odd = place % 2 == 1
@@ -181,23 +203,13 @@
     edge_row = lax.broadcasted_iota(jnp.int32, (8, BLOCK), 0)
     tile_lane = lax.broadcasted_iota(jnp.int32, (64, BLOCK), 1)
     own_lane = jnp.where(tile_lane < BLOCK // 2, 1, 0) != jnp.where(odd, 1, 0)
-    first_lane = lax.broadcasted_iota(jnp.int32, (EDGE, BLOCK), 1) % (BLOCK // 2) < KEEP
 
     def turned(value):
         return pltpu.roll(value, BLOCK // 2, 1)
 
     def edges_of(owner, m):
-        mine = far_own[owner // 2, m, 64 : 64 + EDGE]
-        other = far_other[owner // 2, m, 64 : 64 + EDGE]
-        tile = jnp.where(odd, other, mine) if owner % 2 == 0 else jnp.where(odd, mine, other)
-        tile = tile.astype(F32)
-        return tile[:8] + tile[8:]
-
-    def whole_tile(ref, i, m):
-        rest = ref[i, m, 64 + EDGE :].astype(F32)
-        parts = [rest] + [pltpu.roll(rest, BLOCK - g * KEEP, 1) for g in range(1, 4)]
-        parts = [jnp.where(first_lane, part, 0.0) for part in parts]
-        return ref[i, m, :64].astype(F32) + jnp.concatenate(parts, 0)
+        mine, other = own_edges[owner // 2, m], block_edges(far_other, owner // 2, m)
+        return jnp.where(odd, other, mine) if owner % 2 == 0 else jnp.where(odd, mine, other)
 
     first_rows = []
     for kind in range(2):
@@ -215,8 +227,8 @@
         for i in range(8):
             for m in range(2):
                 rows = slice(64 * m, 64 * (m + 1))
-                mine = whole_tile(far_own, i, 2 * kind + m)
-                other = whole_tile(far_other, i, 2 * kind + m)
+                mine = own_tiles[i, 2 * kind + m]
+                other = block_rows(far_other, i, 2 * kind + m)
                 low = jnp.where(own_lane, mine, other) + fix[rows, i * BLOCK : (i + 1) * BLOCK]
                 high = jnp.where(own_lane, other, mine)
                 high = high + fix[rows, (8 + i) * BLOCK : (9 + i) * BLOCK]
@@ -415,12 +427,29 @@
     gathered, query_conv = lax.optimization_barrier((gathered, query_conv))
     far_own = gathered.reshape(8, 4, SENT, BLOCK)
     far_other = swapped(far_own, "core")
-    pairs = call(pairs_kernel, "pairs", shape(4, 64, ROWS), (conv, near, far), flops=1 << 37)
+    table = jnp.asarray(head_tables())
+    tiles, edges = call(
+        own_kernel,
+        "own",
+        (
+            jax.ShapeDtypeStruct((8, 4, 64, BLOCK), F32),
+            jax.ShapeDtypeStruct((8, 4, 8, BLOCK), F32),
+        ),
+        (far_own, table),
+    )
+    pairs = call(
+        pairs_kernel,
+        "pairs",
+        shape(4, 64, ROWS),
+        (conv, near, far, edges),
+        (VMEM, VMEM, VMEM, pl.ANY),
+        flops=1 << 37,
+    )
     return call(
         attend_kernel,
         "attend",
         shape(ROWS, HEAD_CHANNELS),
-        (query_conv, pairs, far_own, far_other, jnp.asarray(head_tables()), gain),
+        (query_conv, pairs, tiles, edges, far_other, table, gain),
         scratch=[
             VMEM((2, 2, 8, HEAD_CHANNELS, BLOCK), BF16),
             VMEM((19, CHUNK, BLOCK), F32),

time: 39.7 us -> 39.6 us (level)
    pallas_call x5 -> x6, Pallas kernels: 4.76 us -> 4.83 us  [call(): pl.pallas_call(kernel, out_shape=out_shape, in_specs=[spec(s) for s in sp...]
where the time goes in v10:
time: 39.6 us; the launch traced here: 38.9 us
  starting transfers between devices  26.8 us (68%)
  Pallas kernels  7.3 us (18%)
  waiting for transfers between devices  4.55 us (11%)
    ppermute x4, starting transfers between devices, swapped(): return lax.ppermute(value, axis, [(0, 1), (1, 0)])  15 us
    all_to_all x1, starting transfers between devices, per_device(): gathered = lax.all_to_all(blocks, CHIPS + GROUP, 0, 0, tiled=True)  6.4 us
    ppermute x1, starting transfers between devices, per_device(): lax.ppermute(tails, CTX, [(i, i + 1) for i in range(1, 15, 2)] + [(i + 1,...  5.38 us
    pallas_call x6, Pallas kernels, call(): pl.pallas_call(kernel, out_shape=out_shape, in_specs=[spec(s) for s in sp...  4.83 us
    ppermute x1, waiting for transfers between devices, per_device(): lax.ppermute(tails, CTX, [(i, i + 1) for i in range(1, 15, 2)] + [(i + 1,...  2.91 us
    pallas_call x1, Pallas kernels, per_device(): pl.pallas_call(conv_kernel, out_shape=(shape(64, ROWS), shape(32, SENT, B...  2.47 us
    ppermute x4, waiting for transfers between devices, swapped(): return lax.ppermute(value, axis, [(0, 1), (1, 0)])  1.64 us
  transfers between devices with their start and end apart: 6, of which 3 were waited for; matrix products, arithmetic and copies ran while one was open for 0% of the time, Pallas kernels for 1%

profile of v10, /device:TPU:1, one launch (start us, length us, event | category | flops | bytes accessed | tf_op | source)
XLA Modules:
  0.0 38.9 jit_solution(6788140219259820212)
XLA Ops:
  0.0 2.5 %conv.1 = (bf16[64,1024]{1,0:T(8,128)(2,1)}, bf16[32,96,128]{2,1,0:T(8,128)(2,1)}) custom-call(bf16[64,1024]{1,0:T(8,128)(2,1)} %bitcast.6, f32[4,64]{1,0:T(4,128)} %taps_in.1, bf16[128,128]{1,0:T(8,128)(2,1)} %constant.4.clone.table_in), custom_call_target="tpu_custom_call" | custom-call | flops 16777216 | bytes 1048576 | tf_op jit(solution)/shard_map/conv/pallas_call | solution.py:386
  2.5 5.7 %collective-permute-start = (bf16[64,1024]{1,0:T(8,128)(2,1)}, bf16[64,1024]{1,0:T(8,128)(2,1)S(1)}, u32[]{:S(2)}, u32[]{:S(2)}) collective-permute-start(bf16[64,1024]{1,0:T(8,128)(2,1)} %get-tuple-element.14.conv.mine), channel_id=1, source_target_pairs={{0,1},{1,0},{2,3},{3,2},{4,5},{5,4},{6,7},{7,6},{8,9},{9,8},{10,11... | collective-permute-start | bytes 393224 | tf_op jit(solution)/shard_map/ppermute | solution.py:366
  8.1 0.0 copy-start.1
  8.2 0.0 copy-start.2
  8.2 6.4 %all-to-all-start = ((bf16[32,96,128]{2,1,0:T(8,128)(2,1)}), bf16[32,96,128]{2,1,0:T(8,128)(2,1)S(1)}, u32[]{:S(2)}, u32[]{:S(2)}) async-start(bf16[32,96,128]{2,1,0:T(8,128)(2,1)} %get-tuple-element.13), calls=%async_computation | async-start | bytes 1572864 | tf_op jit(solution)/shard_map/all_to_all | solution.py:403
  14.6 0.0 collective-permute-done.near
  14.6 0.0 copy-done.1
  14.6 0.0 copy-done.2
  14.6 0.0 copy-start.3
  14.6 0.0 copy-start.4
  14.6 5.4 %collective-permute-start.2 = (bf16[2,16,128]{2,1,0:T(8,128)(2,1)S(1)}, bf16[2,16,128]{2,1,0:T(8,128)(2,1)S(1)}, u32[]{:S(2)}, u32[]{:S(2)}) collective-permute-start(bf16[2,16,128]{2,1,0:T(8,128)(2,1)S(1)} %tails.1.own), channel_id=1, source_target_pairs={{32,64},{96,128},{160,192},{224,256},{288,320},{352,384},{416,448}... | collective-permute-start | bytes 24584 | tf_op jit(solution)/shard_map/ppermute | solution.py:414
  20.0 1.9 %collective-permute-start.1 = (bf16[2,16,128]{2,1,0:T(8,128)(2,1)S(1)}, bf16[2,16,128]{2,1,0:T(8,128)(2,1)S(1)}, u32[]{:S(2)}, u32[]{:S(2)}) collective-permute-start(bf16[2,16,128]{2,1,0:T(8,128)(2,1)S(1)} %tails.1.own), channel_id=1, source_target_pairs={{0,32},{32,0},{1,33},{33,1},{2,34},{34,2},{3,35},{35,3},{4,36},{36... | collective-permute-start | bytes 24584 | tf_op jit(solution)/shard_map/ppermute | solution.py:366
  22.0 2.9 %collective-permute-done.2.hop = bf16[2,16,128]{2,1,0:T(8,128)(2,1)S(1)} collective-permute-done((bf16[2,16,128]{2,1,0:T(8,128)(2,1)S(1)}, bf16[2,16,128]{2,1,0:T(8,128)(2,1)S(1)}, u32[]{:S(2)}, u32[]{:S(2)}) %collective-permute-start.2) | collective-permute-done | bytes 8224 | tf_op jit(solution)/shard_map/ppermute | solution.py:414
  24.9 0.0 collective-permute-done.1.swap
  24.9 0.0 copy-done.3
  24.9 0.0 copy-done.4
  24.9 0.0 copy-start
  24.9 0.3 queries.1
  25.2 3.9 %collective-permute-start.3 = (bf16[128,1024]{1,0:T(8,128)(2,1)S(1)}, bf16[128,1024]{1,0:T(8,128)(2,1)S(1)}, u32[]{:S(2)}, u32[]{:S(2)}) collective-permute-start(bf16[128,1024]{1,0:T(8,128)(2,1)S(1)} %join.1), channel_id=1, source_target_pairs={{0,2},{2,0},{1,3},{3,1},{4,6},{6,4},{5,7},{7,5},{8,10},{10,8},{9,1... | collective-permute-start | bytes 786440 | tf_op jit(solution)/shard_map/ppermute | solution.py:366
  29.1 0.0 all-to-all-done
  29.1 3.6 %collective-permute-start.4 = (bf16[8,4,96,128]{3,2,1,0:T(8,128)(2,1)S(1)}, bf16[8,4,96,128]{3,2,1,0:T(8,128)(2,1)S(1)}, u32[]{:S(2)}, u32[]{:S(2)}) collective-permute-start(bf16[8,4,96,128]{3,2,1,0:T(8,128)(2,1)S(1)} %bitcast.3), channel_id=1, source_target_pairs={{0,32},{32,0},{1,33},{33,1},{2,34},{34,2},{3,35},{35,3},{4,36},{36... | collective-permute-start | bytes 2359304 | tf_op jit(solution)/shard_map/ppermute | solution.py:366
  32.7 0.0 copy-done
  32.7 0.2 own.1
  32.9 1.1 %collective-permute-done.3.far = bf16[128,1024]{1,0:T(8,128)(2,1)S(1)} collective-permute-done((bf16[128,1024]{1,0:T(8,128)(2,1)S(1)}, bf16[128,1024]{1,0:T(8,128)(2,1)S(1)}, u32[]{:S(2)}, u32[]{:S(2)}) %collective-permute-start.3) | collective-permute-done | bytes 262176 | tf_op jit(solution)/shard_map/ppermute | solution.py:366
  34.0 0.6 %collective-permute-done.4.far_other = bf16[8,4,96,128]{3,2,1,0:T(8,128)(2,1)S(1)} collective-permute-done((bf16[8,4,96,128]{3,2,1,0:T(8,128)(2,1)S(1)}, bf16[8,4,96,128]{3,2,1,0:T(8,128)(2,1)S(1)}, u32[]{:S(2)}, u32[]{:S(2)}) %collective-permute-start.4) | collective-permute-done | bytes 786464 | tf_op jit(solution)/shard_map/ppermute | solution.py:366
  34.6 4.3 %attend.1 = bf16[1024,128]{1,0:T(8,128)(2,1)} custom-call(bf16[1024,128]{1,0:T(8,128)(2,1)S(1)} %get-tuple-element.16.query_conv.q, bf16[4,64,1024]{2,1,0:T(8,128)(2,1)S(1)} %pairs.1, f32[8,4,64,128]{3,2,1,0:T(8,128)S(1)} %get-tuple-element.19.own_tiles, f32[8,4,8,128]{3,2,1,0:T(8,128)S(1)} %get-tuple-element.18.edges.own_edges, ...), custom_call_target="tpu_custom_call" | custom-call | flops 1073741824 | bytes 1048576 | tf_op jit(solution)/shard_map/attend/pallas_call | solution.py:372
  (3 shorter events, 0.1 us)
Async XLA Ops:
  2.5 12.1 %collective-permute-start = (bf16[64,1024]{1,0:T(8,128)(2,1)}, bf16[64,1024]{1,0:T(8,128)(2,1)S(1)}, u32[]{:S(2)}, u32[]{:S(2)}) collective-permute-start(bf16[64,1024]{1,0:T(8,128)(2,1)} %get-tuple-element.14.conv.mine), channel_id=1, source_target_pairs={{0,1},{1,0},{2,3},{3,2},{4,5},{5,4},{6,7},{7,6},{8,9},{9,8},{10,11... | collective-permute-start | bytes 393224 | tf_op jit(solution)/shard_map/ppermute | solution.py:366
  8.1 6.4 %copy-start.1 = (bf16[1024,128]{1,0:T(8,128)(2,1)S(1)}, bf16[1024,128]{1,0:T(8,128)(2,1)}, u32[]{:S(2)}) copy-start(bf16[1024,128]{1,0:T(8,128)(2,1)} %q.3) | copy-start | bytes 786436
  8.2 6.4 %copy-start.2 = (bf16[64,1024]{1,0:T(8,128)(2,1)S(1)}, bf16[64,1024]{1,0:T(8,128)(2,1)}, u32[]{:S(2)}) copy-start(bf16[64,1024]{1,0:T(8,128)(2,1)} %get-tuple-element.14.conv.mine) | copy-start | bytes 393220
  8.2 20.9 %all-to-all-start = ((bf16[32,96,128]{2,1,0:T(8,128)(2,1)}), bf16[32,96,128]{2,1,0:T(8,128)(2,1)S(1)}, u32[]{:S(2)}, u32[]{:S(2)}) async-start(bf16[32,96,128]{2,1,0:T(8,128)(2,1)} %get-tuple-element.13), calls=%async_computation | async-start | bytes 1572864 | tf_op jit(solution)/shard_map/all_to_all | solution.py:403
  14.6 10.3 %copy-start.3 = (f32[4,128]{1,0:T(4,128)S(1)}, f32[4,128]{1,0:T(4,128)}, u32[]{:S(2)}) copy-start(f32[4,128]{1,0:T(4,128)} %taps.1) | copy-start | bytes 6148
  14.6 10.2 %copy-start.4 = (f32[128]{0:T(128)S(1)}, f32[128]{0:T(128)}, u32[]{:S(2)}) copy-start(f32[128]{0:T(128)} %param.11) | copy-start | bytes 1540
  14.6 10.2 %collective-permute-start.2 = (bf16[2,16,128]{2,1,0:T(8,128)(2,1)S(1)}, bf16[2,16,128]{2,1,0:T(8,128)(2,1)S(1)}, u32[]{:S(2)}, u32[]{:S(2)}) collective-permute-start(bf16[2,16,128]{2,1,0:T(8,128)(2,1)S(1)} %tails.1.own), channel_id=1, source_target_pairs={{32,64},{96,128},{160,192},{224,256},{288,320},{352,384},{416,448}... | collective-permute-start | bytes 24584 | tf_op jit(solution)/shard_map/ppermute | solution.py:414
  20.0 4.8 %collective-permute-start.1 = (bf16[2,16,128]{2,1,0:T(8,128)(2,1)S(1)}, bf16[2,16,128]{2,1,0:T(8,128)(2,1)S(1)}, u32[]{:S(2)}, u32[]{:S(2)}) collective-permute-start(bf16[2,16,128]{2,1,0:T(8,128)(2,1)S(1)} %tails.1.own), channel_id=1, source_target_pairs={{0,32},{32,0},{1,33},{33,1},{2,34},{34,2},{3,35},{35,3},{4,36},{36... | collective-permute-start | bytes 24584 | tf_op jit(solution)/shard_map/ppermute | solution.py:366
  24.9 7.8 %copy-start = (bf16[128,2048]{1,0:T(8,128)(2,1)S(1)}, bf16[128,2048]{1,0:T(8,128)(2,1)}, u32[]{:S(2)}) copy-start(bf16[128,2048]{1,0:T(8,128)(2,1)} %constant.5.clone.table) | copy-start | bytes 1572868
  25.2 8.8 %collective-permute-start.3 = (bf16[128,1024]{1,0:T(8,128)(2,1)S(1)}, bf16[128,1024]{1,0:T(8,128)(2,1)S(1)}, u32[]{:S(2)}, u32[]{:S(2)}) collective-permute-start(bf16[128,1024]{1,0:T(8,128)(2,1)S(1)} %join.1), channel_id=1, source_target_pairs={{0,2},{2,0},{1,3},{3,1},{4,6},{6,4},{5,7},{7,5},{8,10},{10,8},{9,1... | collective-permute-start | bytes 786440 | tf_op jit(solution)/shard_map/ppermute | solution.py:366
  29.1 5.5 %collective-permute-start.4 = (bf16[8,4,96,128]{3,2,1,0:T(8,128)(2,1)S(1)}, bf16[8,4,96,128]{3,2,1,0:T(8,128)(2,1)S(1)}, u32[]{:S(2)}, u32[]{:S(2)}) collective-permute-start(bf16[8,4,96,128]{3,2,1,0:T(8,128)(2,1)S(1)} %bitcast.3), channel_id=1, source_target_pairs={{0,32},{32,0},{1,33},{33,1},{2,34},{34,2},{3,35},{35,3},{4,36},{36... | collective-permute-start | bytes 2359304 | tf_op jit(solution)/shard_map/ppermute | solution.py:366

commit v11 on v10

--- a/solution.py
+++ b/solution.py
@@ -135,7 +135,7 @@
         out[half] = q[(half + 1) * SPAN - EDGE : (half + 1) * SPAN]
 
 
-def join_kernel(mine, near, query_conv, out):
+def join_kernel(mine, near, hop, out):
     out[:64] = mine[...]
     out[64:] = near[...]
 
@@ -421,7 +421,7 @@
         (queries, tails, swap, hop, query_taps, out_gain.reshape(1, -1)),
     )
     joined = call(
-        join_kernel, "join", shape(128, ROWS), (conv, near, query_conv), (VMEM, VMEM, pl.ANY)
+        join_kernel, "join", shape(128, ROWS), (conv, near, hop), (VMEM, VMEM, pl.ANY)
     )
     far = swapped(joined, "z_lo")
     gathered, query_conv = lax.optimization_barrier((gathered, query_conv))

time: 39.6 us -> 41 us (1.035)
  waiting for transfers between devices: 4.55 us -> 7.69 us
  starting transfers between devices: 26.8 us -> 25.4 us
    ppermute x1, waiting for transfers between devices: 2.91 us -> 4.72 us  [per_device(): lax.ppermute(tails, CTX, [(i, i + 1) for i in range(1, 15, 2)] + [(i + 1,...]
    ppermute x4, starting transfers between devices: 15 us -> 13.5 us  [swapped(): return lax.ppermute(value, axis, [(0, 1), (1, 0)])]
    ppermute x4, waiting for transfers between devices: 1.64 us -> 2.97 us  [swapped(): return lax.ppermute(value, axis, [(0, 1), (1, 0)])]
where the time goes in v11:
time: 41 us; the launch traced here: 40.6 us
  starting transfers between devices  25.4 us (62%)
  waiting for transfers between devices  7.69 us (19%)
  Pallas kernels  7.3 us (18%)
    ppermute x4, starting transfers between devices, swapped(): return lax.ppermute(value, axis, [(0, 1), (1, 0)])  13.5 us
    all_to_all x1, starting transfers between devices, per_device(): gathered = lax.all_to_all(blocks, CHIPS + GROUP, 0, 0, tiled=True)  6.4 us
    ppermute x1, starting transfers between devices, per_device(): lax.ppermute(tails, CTX, [(i, i + 1) for i in range(1, 15, 2)] + [(i + 1,...  5.51 us
    pallas_call x6, Pallas kernels, call(): pl.pallas_call(kernel, out_shape=out_shape, in_specs=[spec(s) for s in sp...  4.83 us
    ppermute x1, waiting for transfers between devices, per_device(): lax.ppermute(tails, CTX, [(i, i + 1) for i in range(1, 15, 2)] + [(i + 1,...  4.72 us
    ppermute x4, waiting for transfers between devices, swapped(): return lax.ppermute(value, axis, [(0, 1), (1, 0)])  2.97 us
    pallas_call x1, Pallas kernels, per_device(): pl.pallas_call(conv_kernel, out_shape=(shape(64, ROWS), shape(32, SENT, B...  2.47 us
  transfers between devices with their start and end apart: 6, of which 3 were waited for; matrix products, arithmetic and copies ran while one was open for 0% of the time, Pallas kernels for 1%

profile of v11, /device:TPU:1, one launch (start us, length us, event | category | flops | bytes accessed | tf_op | source)
XLA Modules:
  0.0 40.6 jit_solution(6369410089122827949)
XLA Ops:
  0.0 2.5 %conv.1 = (bf16[64,1024]{1,0:T(8,128)(2,1)}, bf16[32,96,128]{2,1,0:T(8,128)(2,1)}) custom-call(bf16[64,1024]{1,0:T(8,128)(2,1)} %bitcast.6, f32[4,64]{1,0:T(4,128)} %taps_in.1, bf16[128,128]{1,0:T(8,128)(2,1)} %constant.4.clone.table_in), custom_call_target="tpu_custom_call" | custom-call | flops 16777216 | bytes 1048576 | tf_op jit(solution)/shard_map/conv/pallas_call | solution.py:386
  2.5 5.7 %collective-permute-start = (bf16[64,1024]{1,0:T(8,128)(2,1)}, bf16[64,1024]{1,0:T(8,128)(2,1)S(1)}, u32[]{:S(2)}, u32[]{:S(2)}) collective-permute-start(bf16[64,1024]{1,0:T(8,128)(2,1)} %get-tuple-element.14.conv.mine), channel_id=1, source_target_pairs={{0,1},{1,0},{2,3},{3,2},{4,5},{5,4},{6,7},{7,6},{8,9},{9,8},{10,11... | collective-permute-start | bytes 393224 | tf_op jit(solution)/shard_map/ppermute | solution.py:366
  8.1 0.0 copy-start.1
  8.2 0.0 copy-start.2
  8.2 6.4 %all-to-all-start = ((bf16[32,96,128]{2,1,0:T(8,128)(2,1)}), bf16[32,96,128]{2,1,0:T(8,128)(2,1)S(1)}, u32[]{:S(2)}, u32[]{:S(2)}) async-start(bf16[32,96,128]{2,1,0:T(8,128)(2,1)} %get-tuple-element.13), calls=%async_computation | async-start | bytes 1572864 | tf_op jit(solution)/shard_map/all_to_all | solution.py:403
  14.6 0.0 collective-permute-done.near
  14.6 0.0 copy-done.1
  14.6 0.0 copy-done.2
  14.6 0.0 copy-start
  14.6 5.5 %collective-permute-start.2 = (bf16[2,16,128]{2,1,0:T(8,128)(2,1)S(1)}, bf16[2,16,128]{2,1,0:T(8,128)(2,1)S(1)}, u32[]{:S(2)}, u32[]{:S(2)}) collective-permute-start(bf16[2,16,128]{2,1,0:T(8,128)(2,1)S(1)} %tails.1.own), channel_id=1, source_target_pairs={{32,64},{96,128},{160,192},{224,256},{288,320},{352,384},{416,448}... | collective-permute-start | bytes 24584 | tf_op jit(solution)/shard_map/ppermute | solution.py:414
  20.1 4.7 %collective-permute-done.2.hop = bf16[2,16,128]{2,1,0:T(8,128)(2,1)S(1)} collective-permute-done((bf16[2,16,128]{2,1,0:T(8,128)(2,1)S(1)}, bf16[2,16,128]{2,1,0:T(8,128)(2,1)S(1)}, u32[]{:S(2)}, u32[]{:S(2)}) %collective-permute-start.2) | collective-permute-done | bytes 8224 | tf_op jit(solution)/shard_map/ppermute | solution.py:414
  24.9 0.0 copy-start.3
  24.9 0.0 copy-start.4
  24.9 3.9 %collective-permute-start.3 = (bf16[128,1024]{1,0:T(8,128)(2,1)S(1)}, bf16[128,1024]{1,0:T(8,128)(2,1)S(1)}, u32[]{:S(2)}, u32[]{:S(2)}) collective-permute-start(bf16[128,1024]{1,0:T(8,128)(2,1)S(1)} %join.1), channel_id=1, source_target_pairs={{0,2},{2,0},{1,3},{3,1},{4,6},{6,4},{5,7},{7,5},{8,10},{10,8},{9,1... | collective-permute-start | bytes 786440 | tf_op jit(solution)/shard_map/ppermute | solution.py:366
  28.8 1.9 %collective-permute-start.1 = (bf16[2,16,128]{2,1,0:T(8,128)(2,1)S(1)}, bf16[2,16,128]{2,1,0:T(8,128)(2,1)S(1)}, u32[]{:S(2)}, u32[]{:S(2)}) collective-permute-start(bf16[2,16,128]{2,1,0:T(8,128)(2,1)S(1)} %tails.1.own), channel_id=1, source_target_pairs={{0,32},{32,0},{1,33},{33,1},{2,34},{34,2},{3,35},{35,3},{4,36},{36... | collective-permute-start | bytes 24584 | tf_op jit(solution)/shard_map/ppermute | solution.py:366
  30.7 1.1 %collective-permute-done.1.swap = bf16[2,16,128]{2,1,0:T(8,128)(2,1)S(1)} collective-permute-done((bf16[2,16,128]{2,1,0:T(8,128)(2,1)S(1)}, bf16[2,16,128]{2,1,0:T(8,128)(2,1)S(1)}, u32[]{:S(2)}, u32[]{:S(2)}) %collective-permute-start.1) | collective-permute-done | bytes 8224 | tf_op jit(solution)/shard_map/ppermute | solution.py:366
  31.9 0.0 copy-done.3
  31.9 0.0 copy-done.4
  31.9 0.3 queries.1
  32.1 0.0 all-to-all-done
  32.1 2.1 %collective-permute-start.4 = (bf16[8,4,96,128]{3,2,1,0:T(8,128)(2,1)S(1)}, bf16[8,4,96,128]{3,2,1,0:T(8,128)(2,1)S(1)}, u32[]{:S(2)}, u32[]{:S(2)}) collective-permute-start(bf16[8,4,96,128]{3,2,1,0:T(8,128)(2,1)S(1)} %bitcast.3), channel_id=1, source_target_pairs={{0,32},{32,0},{1,33},{33,1},{2,34},{34,2},{3,35},{35,3},{4,36},{36... | collective-permute-start | bytes 2359304 | tf_op jit(solution)/shard_map/ppermute | solution.py:366
  34.2 0.0 copy-done
  34.2 0.2 own.1
  34.4 0.0 collective-permute-done.3.far
  34.4 0.1 pairs.1
  34.5 1.8 %collective-permute-done.4.far_other = bf16[8,4,96,128]{3,2,1,0:T(8,128)(2,1)S(1)} collective-permute-done((bf16[8,4,96,128]{3,2,1,0:T(8,128)(2,1)S(1)}, bf16[8,4,96,128]{3,2,1,0:T(8,128)(2,1)S(1)}, u32[]{:S(2)}, u32[]{:S(2)}) %collective-permute-start.4) | collective-permute-done | bytes 786464 | tf_op jit(solution)/shard_map/ppermute | solution.py:366
  36.3 4.3 %attend.1 = bf16[1024,128]{1,0:T(8,128)(2,1)} custom-call(bf16[1024,128]{1,0:T(8,128)(2,1)S(1)} %get-tuple-element.16.q, bf16[4,64,1024]{2,1,0:T(8,128)(2,1)S(1)} %pairs.1, f32[8,4,64,128]{3,2,1,0:T(8,128)S(1)} %get-tuple-element.19.own_tiles, f32[8,4,8,128]{3,2,1,0:T(8,128)S(1)} %get-tuple-element.18.edges.own_edges, ...), custom_call_target="tpu_custom_call" | custom-call | flops 1073741824 | bytes 1048576 | tf_op jit(solution)/shard_map/attend/pallas_call | solution.py:372
  (2 shorter events, 0.0 us)
Async XLA Ops:
  2.5 12.1 %collective-permute-start = (bf16[64,1024]{1,0:T(8,128)(2,1)}, bf16[64,1024]{1,0:T(8,128)(2,1)S(1)}, u32[]{:S(2)}, u32[]{:S(2)}) collective-permute-start(bf16[64,1024]{1,0:T(8,128)(2,1)} %get-tuple-element.14.conv.mine), channel_id=1, source_target_pairs={{0,1},{1,0},{2,3},{3,2},{4,5},{5,4},{6,7},{7,6},{8,9},{9,8},{10,11... | collective-permute-start | bytes 393224 | tf_op jit(solution)/shard_map/ppermute | solution.py:366
  8.1 6.4 %copy-start.1 = (bf16[1024,128]{1,0:T(8,128)(2,1)S(1)}, bf16[1024,128]{1,0:T(8,128)(2,1)}, u32[]{:S(2)}) copy-start(bf16[1024,128]{1,0:T(8,128)(2,1)} %q.3) | copy-start | bytes 786436
  8.2 6.4 %copy-start.2 = (bf16[64,1024]{1,0:T(8,128)(2,1)S(1)}, bf16[64,1024]{1,0:T(8,128)(2,1)}, u32[]{:S(2)}) copy-start(bf16[64,1024]{1,0:T(8,128)(2,1)} %get-tuple-element.14.conv.mine) | copy-start | bytes 393220
  8.2 24.0 %all-to-all-start = ((bf16[32,96,128]{2,1,0:T(8,128)(2,1)}), bf16[32,96,128]{2,1,0:T(8,128)(2,1)S(1)}, u32[]{:S(2)}, u32[]{:S(2)}) async-start(bf16[32,96,128]{2,1,0:T(8,128)(2,1)} %get-tuple-element.13), calls=%async_computation | async-start | bytes 1572864 | tf_op jit(solution)/shard_map/all_to_all | solution.py:403
  14.6 19.6 %copy-start = (bf16[128,2048]{1,0:T(8,128)(2,1)S(1)}, bf16[128,2048]{1,0:T(8,128)(2,1)}, u32[]{:S(2)}) copy-start(bf16[128,2048]{1,0:T(8,128)(2,1)} %constant.5.clone.table) | copy-start | bytes 1572868
  14.6 10.2 %collective-permute-start.2 = (bf16[2,16,128]{2,1,0:T(8,128)(2,1)S(1)}, bf16[2,16,128]{2,1,0:T(8,128)(2,1)S(1)}, u32[]{:S(2)}, u32[]{:S(2)}) collective-permute-start(bf16[2,16,128]{2,1,0:T(8,128)(2,1)S(1)} %tails.1.own), channel_id=1, source_target_pairs={{32,64},{96,128},{160,192},{224,256},{288,320},{352,384},{416,448}... | collective-permute-start | bytes 24584 | tf_op jit(solution)/shard_map/ppermute | solution.py:414
  24.9 7.0 %copy-start.3 = (f32[4,128]{1,0:T(4,128)S(1)}, f32[4,128]{1,0:T(4,128)}, u32[]{:S(2)}) copy-start(f32[4,128]{1,0:T(4,128)} %taps.1) | copy-start | bytes 6148
  24.9 7.0 %copy-start.4 = (f32[128]{0:T(128)S(1)}, f32[128]{0:T(128)}, u32[]{:S(2)}) copy-start(f32[128]{0:T(128)} %param.11) | copy-start | bytes 1540
  24.9 9.5 %collective-permute-start.3 = (bf16[128,1024]{1,0:T(8,128)(2,1)S(1)}, bf16[128,1024]{1,0:T(8,128)(2,1)S(1)}, u32[]{:S(2)}, u32[]{:S(2)}) collective-permute-start(bf16[128,1024]{1,0:T(8,128)(2,1)S(1)} %join.1), channel_id=1, source_target_pairs={{0,2},{2,0},{1,3},{3,1},{4,6},{6,4},{5,7},{7,5},{8,10},{10,8},{9,1... | collective-permute-start | bytes 786440 | tf_op jit(solution)/shard_map/ppermute | solution.py:366
  28.8 3.1 %collective-permute-start.1 = (bf16[2,16,128]{2,1,0:T(8,128)(2,1)S(1)}, bf16[2,16,128]{2,1,0:T(8,128)(2,1)S(1)}, u32[]{:S(2)}, u32[]{:S(2)}) collective-permute-start(bf16[2,16,128]{2,1,0:T(8,128)(2,1)S(1)} %tails.1.own), channel_id=1, source_target_pairs={{0,32},{32,0},{1,33},{33,1},{2,34},{34,2},{3,35},{35,3},{4,36},{36... | collective-permute-start | bytes 24584 | tf_op jit(solution)/shard_map/ppermute | solution.py:366
  32.1 4.2 %collective-permute-start.4 = (bf16[8,4,96,128]{3,2,1,0:T(8,128)(2,1)S(1)}, bf16[8,4,96,128]{3,2,1,0:T(8,128)(2,1)S(1)}, u32[]{:S(2)}, u32[]{:S(2)}) collective-permute-start(bf16[8,4,96,128]{3,2,1,0:T(8,128)(2,1)S(1)} %bitcast.3), channel_id=1, source_target_pairs={{0,32},{32,0},{1,33},{33,1},{2,34},{34,2},{3,35},{35,3},{4,36},{36... | collective-permute-start | bytes 2359304 | tf_op jit(solution)/shard_map/ppermute | solution.py:366
